TPU v7x, 32 devices: a whole 2x2x4 slice. The times are simulated.
32 devices in a mesh: rows: 16 (over z, y, x), branch: 2 (over core).
Axes of the slice: x: 2, y: 2, z: 4, core: 2. Of those that a mesh axis runs over, the one named last changes fastest.
Arguments:
- node_feats: bfloat16 [65536, 256], P('rows')
- edge_feats: bfloat16 [131072, 256], P('rows')
- cotangent: bfloat16 [65536, 256], P(('rows', 'branch')), may hold values from -6 to 6
- graph_ids: int32 [65536], P('rows'), may hold values from 0 to 16383, as said below
- node_mask: int32 [65536], P('rows'), may hold values from 0 to 1, as said below
- edge_src: int32 [131072], P('rows'), may hold values from 0 to 126, as said below
- edge_dst: int32 [131072], P('rows'), may hold values from 0 to 126, as said below
- edge_mask: int32 [131072], P('rows'), may hold values from 0 to 1, as said below
- weights: float32 [13, 65536], P(None, ('rows', 'branch'))
- weight_moment1: float32 [13, 65536], P(None, ('rows', 'branch')), may hold values from -0.0017089844 to 0.0017089844
- weight_moment2: float32 [13, 65536], P(None, ('rows', 'branch')), may hold values from 1.168836e-09 to 4.675344e-09
- vectors: float32 [14, 256], replicated
- vector_moment1: float32 [14, 256], replicated, may hold values from -0.0048828125 to 0.0048828125
- vector_moment2: float32 [14, 256], replicated, may hold values from 1.0519524e-08 to 4.2078096e-08
Outputs:
- layer_out: bfloat16 [65536, 256], P(('rows', 'branch'))
- node_grad: float32 [65536, 256], P(('rows', 'branch'))
- edge_grad: float32 [131072, 256], P(('rows', 'branch'))
- new_weights: float32 [13, 65536], P(None, ('rows', 'branch'))
- new_moment1: float32 [13, 65536], P(None, ('rows', 'branch'))
- new_moment2: float32 [13, 65536], P(None, ('rows', 'branch'))
- new_vectors: float32 [14, 256], replicated
- new_vector_moment1: float32 [14, 256], replicated
- new_vector_moment2: float32 [14, 256], replicated
- grad_norm: float32 [], replicated
Inputs may be any that keep to these rules, and one draw needn't show every extreme that they name: `graph_ids`: graph ids of block b lie in 32 * b to 32 * b + 25 for used nodes; unused nodes of block b carry 32 * b + 31; a block's used nodes come first, molecules are consecutive runs of 1 to 50 nodes. `node_mask`: each block's used slots come first; from 40 to 127 used slots a block, the last block holding 128 - 1. `edge_src`: edges join used nodes of one molecule; unused edge slots hold 0. `edge_dst`: the target lies in the source's molecule. `edge_mask`: at most twice the block's used nodes, and at most 256, edge slots of a block are used, all among the first slots.
All inputs are finite; a program needn't handle non-finite values.
Results may differ from a plain program's by a relative error of at most 0.011.
Values may be sent and summed in bfloat16 or wider, within the bound.
No kernel may reach another device: no remote copies, remote signals or barrier semaphores. Data moves between devices by JAX's collectives and lax.ppermute only.
A program may use at most 192 MiB of HBM per device.

v0:
```python
import functools
import math

import jax
import jax.numpy as jnp
from jax import lax
from jax.experimental import pallas as pl
from jax.experimental.pallas import tpu as pltpu
from jax.sharding import PartitionSpec as P

HEADS = 8
BLOCK = 128
EB = 256
MATS = 13
STEP = 7
GROUP = 4

eps_norm = 1e-05
clip_limit = 1.0
beta_one = 0.9
beta_two = 0.999
rate_mats = 0.1
rate_vecs = 0.8
decay_mats = 0.01
adam_eps = 1e-08
hidden_floor = -1e30
axis_names = ("rows", "branch")
f32 = jnp.float32
bf16 = jnp.bfloat16


def mm(left, right):
    return jnp.dot(left, right, preferred_element_type=f32)


def mm_back(left, right):
    return lax.dot_general(left, right, (((1,), (1,)), ((), ())), preferred_element_type=f32)


def mm_rows(left, right):
    return lax.dot_general(left, right, (((0,), (0,)), ((), ())), preferred_element_type=f32)


def low(values):
    return values.astype(bf16)


def sig(values):
    return 0.5 * jnp.tanh(0.5 * values) + 0.5


def col_sum(values):
    return jnp.sum(values, axis=0, keepdims=True)


def live_of(info_ref, first_block, group, width):
    slot = lax.broadcasted_iota(jnp.int32, (BLOCK, width), 0)
    return jnp.concatenate(
        [
            jnp.where(slot < info_ref[1 + first_block + place], 1.0, 0.0)
            for place in range(group)
        ],
        axis=0,
    )


def add_rows(out_ref, rows):
    @pl.when(pl.program_id(0) == 0)
    def _():
        out_ref[...] = jnp.zeros_like(out_ref)

    for place, row in enumerate(rows):
        out_ref[place : place + 1, :] += row


def norm_terms(sums, first, count_row):
    mean = sums[first : first + 1] / count_row
    rstd = lax.rsqrt(sums[first + 1 : first + 2] / count_row - mean * mean + eps_norm)
    return (mean, rstd)


def prep_kernel(info_ref, src_ref, dst_ref, mask_ref, id_ref, hot_ref, turned_ref, bias_ref):
    for place in range(GROUP):
        row = pl.ds(place, 1)
        node = lax.broadcasted_iota(jnp.int32, (BLOCK, EB), 0)
        live = mask_ref[0, row, :] != 0
        dst_rows = jnp.where((node == dst_ref[0, row, :]) & live, 1.0, 0.0)
        src_rows = jnp.where((node == src_ref[0, row, :]) & live, 1.0, 0.0)
        turned = jnp.concatenate([dst_rows, src_rows], axis=0)
        turned_ref[place * EB : (place + 1) * EB, :] = low(turned)
        hot_ref[place * EB : (place + 1) * EB, :] = low(turned.T)
        ids = jnp.broadcast_to(id_ref[0, row, :].astype(f32), (BLOCK, BLOCK))
        bias_ref[place * BLOCK : (place + 1) * BLOCK, :] = jnp.where(
            ids == ids.T, 0.0, hidden_floor
        )


def local_kernel(
    info_ref, x_ref, e_ref, hot_ref, turned_ref, w_ref, vec_ref,
    out_ref, gated_ref, recip_ref, ratio_ref, open_ref, bsrc_ref, sums_ref,
):
    group = x_ref.shape[0] // BLOCK
    x = x_ref[...]
    a_part = mm(x, w_ref[0]) + vec_ref[0:1, :]
    b_part = low(mm(x, w_ref[1]))
    d_part = low(mm(x, w_ref[3]))
    e_part = low(mm(x, w_ref[4]))
    c_part = mm(e_ref[...], w_ref[2]) + vec_ref[1:2, :]
    nums = []
    dens = []
    for place in range(group):
        nodes = slice(place * BLOCK, (place + 1) * BLOCK)
        edges = slice(place * EB, (place + 1) * EB)
        hot = hot_ref[edges, :]
        gate = c_part[edges] + mm(hot, jnp.concatenate([d_part[nodes], e_part[nodes]], axis=0))
        opened = sig(gate)
        b_source = mm(hot[:, BLOCK:], b_part[nodes])
        open_ref[edges, :] = opened
        bsrc_ref[edges, :] = low(b_source)
        dst_turned = turned_ref[place * EB : place * EB + BLOCK, :]
        nums.append(mm(dst_turned, low(opened * b_source)))
        dens.append(mm(dst_turned, low(opened)))
    recip = 1.0 / (jnp.concatenate(dens, axis=0) + 1.0)
    ratio = jnp.concatenate(nums, axis=0) * recip
    gated = a_part + ratio
    out = x.astype(f32) + gated * sig(gated)
    gated_ref[...] = gated
    recip_ref[...] = recip
    ratio_ref[...] = ratio
    out_ref[...] = out
    live = live_of(info_ref, pl.program_id(0) * group, group, out.shape[1])
    kept = live * out
    add_rows(sums_ref, [col_sum(kept), col_sum(kept * out)])


def head_stack(values):
    head = lax.broadcasted_iota(jnp.int32, values.shape, 1) // (values.shape[1] // HEADS)
    wide = values.astype(f32)
    return jnp.concatenate(
        [low(jnp.where(head == place, wide, 0.0)) for place in range(HEADS)], axis=0
    )


def attend_kernel(
    info_ref, x_ref, bias_ref, w_ref, vec_ref,
    out_ref, q_ref, k_ref, v_ref, att_ref, prob_ref, sums_ref,
):
    group = x_ref.shape[0] // BLOCK
    x = x_ref[...]
    queries = low(mm(x, w_ref[5]) + vec_ref[2:3, :])
    keyed = low(mm(x, w_ref[6]))
    valued = low(mm(x, w_ref[7]) + vec_ref[3:4, :])
    q_ref[...] = queries
    k_ref[...] = keyed
    v_ref[...] = valued
    score_scale = (x.shape[1] // HEADS) ** (-0.5)
    for place in range(group):
        nodes = slice(place * BLOCK, (place + 1) * BLOCK)
        raw = mm_back(keyed[nodes], head_stack(queries[nodes]))
        bias = bias_ref[nodes, :]
        probs = []
        turned = []
        for head in range(HEADS):
            part = raw[:, head * BLOCK : (head + 1) * BLOCK] + bias
            part = jnp.exp((part - jnp.max(part, axis=0, keepdims=True)) * score_scale)
            part = part * (1.0 / jnp.sum(part, axis=0, keepdims=True))
            probs.append(low(part))
            turned.append(low(part.T))
        prob_ref[nodes, :] = jnp.concatenate(probs, axis=1)
        att_ref[nodes, :] = low(
            mm(jnp.concatenate(turned, axis=1), head_stack(valued[nodes]))
        )
    out = x.astype(f32) + mm(att_ref[...], w_ref[8]) + vec_ref[4:5, :]
    out_ref[...] = out
    live = live_of(info_ref, pl.program_id(0) * group, group, out.shape[1])
    kept = live * out
    add_rows(sums_ref, [col_sum(kept), col_sum(kept * out)])


def mix_kernel(
    info_ref, local_ref, global_ref, cot_ref, sums_ref, w_ref, vec_ref,
    low_ref, hidden_ref, mixed_ref, stat_ref,
):
    group = local_ref.shape[0] // BLOCK
    width = local_ref.shape[1]
    sums = sums_ref[...]
    count_row = sums[4:5]
    local_mean, local_rstd = norm_terms(sums, 0, count_row)
    global_mean, global_rstd = norm_terms(sums, 2, count_row)
    local_norm = (local_ref[...] - local_mean) * (vec_ref[5:6, :] * local_rstd) + vec_ref[6:7, :]
    global_norm = (global_ref[...] - global_mean) * (vec_ref[7:8, :] * global_rstd) + vec_ref[
        8:9, :
    ]
    summed = low(local_norm).astype(f32) + low(global_norm).astype(f32)
    summed_low = low(summed)
    low_ref[...] = summed_low
    mixed = summed + vec_ref[11:12, :]
    for half in range(2):
        hidden = mm(summed_low, w_ref[9 + half]) + vec_ref[9 + half : 10 + half, :]
        hidden_ref[:, half * width : (half + 1) * width] = hidden
        mixed = mixed + mm(low(hidden * sig(hidden)), w_ref[11 + half])
    mixed_ref[...] = mixed
    live = live_of(info_ref, pl.program_id(0) * group, group, width)
    kept = live * mixed
    d_norm = live * cot_ref[...].astype(f32)
    add_rows(
        stat_ref, [col_sum(kept), col_sum(kept * mixed), col_sum(d_norm), col_sum(d_norm * mixed)]
    )


def mix_back_kernel(
    info_ref, mixed_ref, hidden_ref, cot_ref, local_ref, global_ref, sums_ref, tops_ref, w_ref,
    vec_ref,
    layer_ref, dmix_ref, dhid_ref, hlow_ref, dsum_ref, stat_ref,
):
    group = mixed_ref.shape[0] // BLOCK
    width = mixed_ref.shape[1]
    sums = sums_ref[...]
    tops = tops_ref[...]
    count_row = sums[4:5]
    mean, rstd = norm_terms(tops, 0, count_row)
    live = live_of(info_ref, pl.program_id(0) * group, group, width)
    hat = (mixed_ref[...] - mean) * rstd
    layer_ref[...] = low(live * (vec_ref[12:13, :] * hat + vec_ref[13:14, :]))
    d_norm = live * cot_ref[...].astype(f32)
    dz_sum = tops[2:3]
    dz_hat = (tops[3:4] - mean * dz_sum) * rstd
    d_mixed = (vec_ref[12:13, :] * rstd) * (
        d_norm - live * (dz_sum / count_row + hat * (dz_hat / count_row))
    )
    d_mixed_low = low(d_mixed)
    dmix_ref[...] = d_mixed_low
    d_summed = d_mixed
    rows = []
    for half in range(2):
        cols = slice(half * width, (half + 1) * width)
        hidden = hidden_ref[:, cols]
        sig_value = sig(hidden)
        hlow_ref[:, cols] = low(hidden * sig_value)
        d_hidden = low(
            mm_back(d_mixed_low, w_ref[11 + half])
            * (sig_value * (1.0 + hidden * (1.0 - sig_value)))
        )
        dhid_ref[:, cols] = d_hidden
        rows.append(col_sum(d_hidden.astype(f32)))
        d_summed = d_summed + mm_back(d_hidden, w_ref[9 + half])
    d_low = low(d_summed)
    dsum_ref[...] = d_low
    d_sum = d_low.astype(f32)
    local_mean, local_rstd = norm_terms(sums, 0, count_row)
    global_mean, global_rstd = norm_terms(sums, 2, count_row)
    add_rows(
        stat_ref,
        [
            col_sum(d_sum),
            col_sum(d_sum * ((local_ref[...] - local_mean) * local_rstd)),
            col_sum(d_sum * ((global_ref[...] - global_mean) * global_rstd)),
            rows[0],
            rows[1],
            col_sum(d_mixed),
        ],
    )


def accumulate(acc_ref, terms):
    @pl.when(pl.program_id(0) == 0)
    def _():
        acc_ref[...] = jnp.zeros_like(acc_ref)

    for place, term in enumerate(terms):
        acc_ref[place] += term


def emit(acc_ref, out_ref):
    @pl.when(pl.program_id(0) == pl.num_programs(0) - 1)
    def _():
        out_ref[...] = low(acc_ref[...])


def mix_grad_kernel(slow_ref, dhid_ref, hlow_ref, dmix_ref, out_ref, acc_ref):
    width = slow_ref.shape[1]
    terms = []
    for half in range(2):
        terms.append(mm_rows(slow_ref[...], dhid_ref[:, half * width : (half + 1) * width]))
    for half in range(2):
        terms.append(mm_rows(hlow_ref[:, half * width : (half + 1) * width], dmix_ref[...]))
    accumulate(acc_ref, terms)
    emit(acc_ref, out_ref)


def norm_back(info_ref, dsum_ref, value_ref, sums, backs, first, gain_row, hat_row):
    group = value_ref.shape[0] // BLOCK
    count_row = sums[4:5]
    mean, rstd = norm_terms(sums, first, count_row)
    live = live_of(info_ref, pl.program_id(0) * group, group, value_ref.shape[1])
    hat = (value_ref[...] - mean) * rstd
    return (gain_row * rstd) * (
        dsum_ref[...].astype(f32)
        - live * (backs[0:1] / count_row + hat * (backs[hat_row : hat_row + 1] / count_row))
    )


def local_back_kernel(
    info_ref, dsum_ref, local_ref, gated_ref, recip_ref, ratio_ref, open_ref, bsrc_ref, hot_ref,
    turned_ref, x_ref, e_ref, sums_ref, backs_ref, vec_ref,
    dnode_ref, dedge_ref, stat_ref, out_ref, acc_ref,
):
    group = local_ref.shape[0] // BLOCK
    width = local_ref.shape[1]
    d_local = norm_back(
        info_ref, dsum_ref, local_ref, sums_ref[...], backs_ref[...], 0, vec_ref[5:6, :], 1
    )
    gated = gated_ref[...]
    sig_value = sig(gated)
    d_gated = d_local * (sig_value * (1.0 + gated * (1.0 - sig_value)))
    dnode_ref[:, :width] = low(d_gated)
    scaled = d_gated * recip_ref[...]
    d_num = low(scaled)
    d_den = low(-scaled * ratio_ref[...])
    pre_row = jnp.zeros((1, width), f32)
    for place in range(group):
        nodes = slice(place * BLOCK, (place + 1) * BLOCK)
        edges = slice(place * EB, (place + 1) * EB)
        hot_dst = hot_ref[edges, :BLOCK]
        d_message = mm(hot_dst, d_num[nodes])
        opened = open_ref[edges, :]
        d_open = d_message * bsrc_ref[edges, :].astype(f32) + mm(hot_dst, d_den[nodes])
        d_source = low(d_message * opened)
        d_pre = d_open * (opened * (1.0 - opened))
        d_pre_low = low(d_pre)
        pre_row = pre_row + col_sum(d_pre)
        dedge_ref[edges, :] = d_pre_low
        turned = turned_ref[edges, :]
        d_b = low(mm(turned[BLOCK:], d_source))
        d_both = low(mm(turned, d_pre_low))
        dnode_ref[nodes, width : 2 * width] = d_b
        dnode_ref[nodes, 2 * width : 3 * width] = d_both[:BLOCK]
        dnode_ref[nodes, 3 * width :] = d_both[BLOCK:]
    x = x_ref[...]
    add_rows(stat_ref, [col_sum(d_gated), pre_row])
    accumulate(
        acc_ref,
        [
            mm_rows(x, dnode_ref[:, :width]),
            mm_rows(x, dnode_ref[:, width : 2 * width]),
            mm_rows(e_ref[...], dedge_ref[...]),
            mm_rows(x, dnode_ref[:, 2 * width : 3 * width]),
            mm_rows(x, dnode_ref[:, 3 * width :]),
        ],
    )
    emit(acc_ref, out_ref)


def attend_back_kernel(
    info_ref, dsum_ref, global_ref, att_ref, q_ref, k_ref, v_ref, prob_ref, x_ref, sums_ref,
    backs_ref, w_ref, vec_ref,
    dqkv_ref, stat_ref, out_ref, acc_ref,
):
    group = global_ref.shape[0] // BLOCK
    width = global_ref.shape[1]
    score_scale = (width // HEADS) ** (-0.5)
    d_global = norm_back(
        info_ref, dsum_ref, global_ref, sums_ref[...], backs_ref[...], 2, vec_ref[7:8, :], 2
    )
    d_low = low(d_global)
    d_att = low(mm_back(d_low, w_ref[8]))
    for place in range(group):
        nodes = slice(place * BLOCK, (place + 1) * BLOCK)
        att_stack = head_stack(d_att[nodes])
        d_prob = mm_back(v_ref[nodes, :], att_stack)
        turned = []
        straight = []
        for head in range(HEADS):
            cols = slice(head * BLOCK, (head + 1) * BLOCK)
            prob = prob_ref[nodes, cols].astype(f32)
            part = d_prob[:, cols]
            inner = jnp.sum(prob * part, axis=0, keepdims=True)
            d_score = prob * (part - inner) * score_scale
            straight.append(low(d_score))
            turned.append(low(d_score.T))
        dqkv_ref[nodes, :width] = low(
            mm(jnp.concatenate(turned, axis=1), head_stack(k_ref[nodes, :]))
        )
        dqkv_ref[nodes, width : 2 * width] = low(
            mm(jnp.concatenate(straight, axis=1), head_stack(q_ref[nodes, :]))
        )
        dqkv_ref[nodes, 2 * width :] = low(mm(prob_ref[nodes, :], att_stack))
    x = x_ref[...]
    add_rows(
        stat_ref,
        [
            col_sum(dqkv_ref[:, :width].astype(f32)),
            col_sum(dqkv_ref[:, 2 * width :].astype(f32)),
            col_sum(d_global),
        ],
    )
    accumulate(
        acc_ref,
        [mm_rows(x, dqkv_ref[:, part * width : (part + 1) * width]) for part in range(3)]
        + [mm_rows(att_ref[...], d_low)],
    )
    emit(acc_ref, out_ref)


def input_grad_kernel(
    info_ref, dsum_ref, local_ref, global_ref, dnode_ref, dqkv_ref, dedge_ref, sums_ref,
    backs_ref, w_ref, vec_ref,
    node_ref, edge_ref,
):
    width = local_ref.shape[1]
    sums = sums_ref[...]
    backs = backs_ref[...]
    total = norm_back(info_ref, dsum_ref, local_ref, sums, backs, 0, vec_ref[5:6, :], 1)
    total = total + norm_back(info_ref, dsum_ref, global_ref, sums, backs, 2, vec_ref[7:8, :], 2)
    for place, mat in enumerate((0, 1, 3, 4)):
        total = total + mm_back(dnode_ref[:, place * width : (place + 1) * width], w_ref[mat])
    for place in range(3):
        total = total + mm_back(dqkv_ref[:, place * width : (place + 1) * width], w_ref[5 + place])
    node_ref[...] = total
    edge_ref[...] = mm_back(dedge_ref[...], w_ref[2])


def rows_spec(rows, width, offset=0):
    if offset:
        return pl.BlockSpec((rows, width), lambda step, info: (step + info[0], 0))
    return pl.BlockSpec((rows, width), lambda step, info: (step, 0))


def whole_spec(shape):
    zeros = (0,) * len(shape)
    return pl.BlockSpec(shape, lambda step, info: zeros)


def call(kernel, steps, info, inputs, outputs, scratch=(), cost=None):
    in_specs = []
    arrays = []
    for array, spec in inputs:
        arrays.append(array)
        in_specs.append(whole_spec(array.shape) if spec is None else spec)
    out_specs = []
    out_shapes = []
    for shape, dtype, spec in outputs:
        out_specs.append(whole_spec(shape) if spec is None else spec)
        out_shapes.append(jax.ShapeDtypeStruct(shape, dtype))
    return pl.pallas_call(
        kernel,
        grid_spec=pltpu.PrefetchScalarGridSpec(
            num_scalar_prefetch=1,
            grid=(steps,),
            in_specs=in_specs,
            out_specs=out_specs,
            scratch_shapes=list(scratch),
        ),
        out_shape=out_shapes,
        compiler_params=pltpu.CompilerParams(
            dimension_semantics=("arbitrary",), vmem_limit_bytes=48 * 1024 * 1024
        ),
        cost_estimate=cost,
    )(info, *arrays)


def swap_with(values, step, total):
    return lax.ppermute(values, axis_names, [(place, place ^ step) for place in range(total)])


def steps_of(total):
    return [1 << power for power in range(total.bit_length() - 1)]


def sum_small(values, total):
    for step in steps_of(total):
        values = values + swap_with(values, step, total)
    return values


def gather_matrices(shard, total):
    place = lax.axis_index(axis_names)
    mats, width = shard.shape
    held = shard[None]
    for step in reversed(steps_of(total)):
        other = swap_with(held, step, total)
        upper = (place & step) != 0
        held = jnp.concatenate(
            [jnp.where(upper, other, held), jnp.where(upper, held, other)], axis=0
        )
    bits = total.bit_length() - 1
    held = held.reshape((2,) * bits + (mats, width))
    held = held.transpose((bits,) + tuple(reversed(range(bits))) + (bits + 1,))
    return held.reshape(mats, total * width)


def scatter_sum(grads, total):
    place = lax.axis_index(axis_names)
    mats, width = grads.shape
    bits = total.bit_length() - 1
    held = grads.reshape((mats,) + (2,) * bits + (width // total,))
    held = held.transpose(tuple(reversed(range(1, bits + 1))) + (0, bits + 1))
    for step in steps_of(total):
        mine = ((place & step) != 0).astype(jnp.int32)
        sent = lax.dynamic_index_in_dim(held, 1 - mine, 0, keepdims=False)
        kept = lax.dynamic_index_in_dim(held, mine, 0, keepdims=False)
        held = kept.astype(f32) + swap_with(sent, step, total).astype(f32)
        if step * 2 < total:
            held = low(held)
    return held


def adamw(params, gradient, moment_one, moment_two, rate, decay):
    first = beta_one * moment_one + (1.0 - beta_one) * gradient
    second = beta_two * moment_two + (1.0 - beta_two) * gradient * gradient
    first_hat = first / (1.0 - beta_one**STEP)
    second_hat = second / (1.0 - beta_two**STEP)
    updated = params - rate * (first_hat / (jnp.sqrt(second_hat) + adam_eps) + decay * params)
    return (updated, first, second)


def own_half(values, branch_index):
    half = values.shape[0] // 2
    return lax.dynamic_slice_in_dim(values, branch_index * half, half, 0)


def per_device(
    node_feats,
    edge_feats,
    cotangent,
    graph_ids,
    node_mask,
    edge_src,
    edge_dst,
    edge_mask,
    weights,
    weight_moment1,
    weight_moment2,
    vectors,
    vector_moment1,
    vector_moment2,
):
    total = lax.axis_size("rows") * lax.axis_size("branch")
    branch_index = lax.axis_index("branch")
    width = node_feats.shape[1]
    rows = node_feats.shape[0] // 2
    edges = edge_feats.shape[0] // 2
    blocks = rows // BLOCK
    group = math.gcd(blocks, GROUP)
    steps = blocks // group
    tall = group * BLOCK
    tall_edges = group * EB
    w_bf = low(weights)
    matrices = gather_matrices(w_bf, total).reshape(MATS, width, width)
    counts = jnp.sum(own_half(node_mask, branch_index).reshape(blocks, BLOCK), axis=1)
    info = jnp.concatenate([(branch_index * steps)[None], counts]).astype(jnp.int32)

    def by_step(values, slots):
        return own_half(values, branch_index).reshape(steps, group, slots)

    def step_spec(slots):
        return pl.BlockSpec((1, group, slots), lambda step, info: (step, 0, 0))

    edge_spec = rows_spec(tall_edges, width)
    node_spec = rows_spec(tall, width)
    hot, turned, bias = call(
        prep_kernel,
        steps,
        info,
        [
            (by_step(edge_src, EB), step_spec(EB)),
            (by_step(edge_dst, EB), step_spec(EB)),
            (by_step(edge_mask, EB), step_spec(EB)),
            (by_step(graph_ids, BLOCK), step_spec(BLOCK)),
        ],
        [
            ((edges, EB), bf16, edge_spec),
            ((edges, EB), bf16, edge_spec),
            ((rows, BLOCK), f32, rows_spec(tall, BLOCK)),
        ],
    )
    x_in = (node_feats, rows_spec(tall, width, 1))
    e_in = (edge_feats, rows_spec(tall_edges, width, 1))
    mats_in = (matrices, None)
    vec_in = (vectors, None)
    node_f32 = ((rows, width), f32, node_spec)
    node_bf = ((rows, width), bf16, node_spec)
    sums_out = ((8, width), f32, None)
    local_out, gated, recip, ratio, opened, b_source, local_sums = call(
        local_kernel,
        steps,
        info,
        [x_in, e_in, (hot, edge_spec), (turned, edge_spec), mats_in, vec_in],
        [
            node_f32,
            node_f32,
            node_f32,
            node_f32,
            ((edges, width), f32, edge_spec),
            ((edges, width), bf16, edge_spec),
            sums_out,
        ],
    )
    prob_spec = rows_spec(tall, HEADS * BLOCK)
    global_out, queries, keyed, valued, attended, probs, global_sums = call(
        attend_kernel,
        steps,
        info,
        [x_in, (bias, rows_spec(tall, BLOCK)), mats_in, vec_in],
        [
            node_f32,
            node_bf,
            node_bf,
            node_bf,
            node_bf,
            ((rows, HEADS * BLOCK), bf16, prob_spec),
            sums_out,
        ],
    )
    count_row = jnp.full((1, width), jnp.sum(counts).astype(f32))
    sums = sum_small(
        jnp.concatenate(
            [local_sums[:2], global_sums[:2], count_row, jnp.zeros((3, width), f32)], axis=0
        ),
        total,
    )
    sums_in = (sums, None)
    cot_in = (cotangent, node_spec)
    wide_spec = rows_spec(tall, 2 * width)
    summed_low, hidden, mixed, top_part = call(
        mix_kernel,
        steps,
        info,
        [(local_out, node_spec), (global_out, node_spec), cot_in, sums_in, mats_in, vec_in],
        [node_bf, ((rows, 2 * width), f32, wide_spec), node_f32, sums_out],
    )
    tops = sum_small(top_part, total)
    layer_out, d_mixed, d_hidden, hidden_low, d_summed, back_part = call(
        mix_back_kernel,
        steps,
        info,
        [
            (mixed, node_spec),
            (hidden, wide_spec),
            cot_in,
            (local_out, node_spec),
            (global_out, node_spec),
            sums_in,
            (tops, None),
            mats_in,
            vec_in,
        ],
        [
            node_bf,
            node_bf,
            ((rows, 2 * width), bf16, wide_spec),
            ((rows, 2 * width), bf16, wide_spec),
            node_bf,
            sums_out,
        ],
    )
    backs = sum_small(back_part, total)

    def mat_out(number):
        return ((number, width, width), bf16, None)

    def mat_acc(number):
        return pltpu.VMEM((number, width, width), f32)

    mix_grads = call(
        lambda info_ref, *refs: mix_grad_kernel(*refs),
        steps,
        info,
        [
            (summed_low, node_spec),
            (d_hidden, wide_spec),
            (hidden_low, wide_spec),
            (d_mixed, node_spec),
        ],
        [mat_out(4)],
        [mat_acc(4)],
    )[0]
    backs_in = (backs, None)
    dsum_in = (d_summed, node_spec)
    dnode_spec = rows_spec(tall, 4 * width)
    d_node, d_edge, local_bias, local_grads = call(
        local_back_kernel,
        steps,
        info,
        [
            dsum_in,
            (local_out, node_spec),
            (gated, node_spec),
            (recip, node_spec),
            (ratio, node_spec),
            (opened, edge_spec),
            (b_source, edge_spec),
            (hot, edge_spec),
            (turned, edge_spec),
            x_in,
            e_in,
            sums_in,
            backs_in,
            vec_in,
        ],
        [
            ((rows, 4 * width), bf16, dnode_spec),
            ((edges, width), bf16, edge_spec),
            sums_out,
            mat_out(5),
        ],
        [mat_acc(5)],
    )
    dqkv_spec = rows_spec(tall, 3 * width)
    d_qkv, attend_bias, attend_grads = call(
        attend_back_kernel,
        steps,
        info,
        [
            dsum_in,
            (global_out, node_spec),
            (attended, node_spec),
            (queries, node_spec),
            (keyed, node_spec),
            (valued, node_spec),
            (probs, prob_spec),
            x_in,
            sums_in,
            backs_in,
            mats_in,
            vec_in,
        ],
        [((rows, 3 * width), bf16, dqkv_spec), sums_out, mat_out(4)],
        [mat_acc(4)],
    )
    all_grads = jnp.concatenate([local_grads, attend_grads, mix_grads], axis=0)
    grad_shard = scatter_sum(all_grads.reshape(MATS, width * width), total)
    node_grad, edge_grad = call(
        input_grad_kernel,
        steps,
        info,
        [
            dsum_in,
            (local_out, node_spec),
            (global_out, node_spec),
            (d_node, dnode_spec),
            (d_qkv, dqkv_spec),
            (d_edge, edge_spec),
            sums_in,
            backs_in,
            mats_in,
            vec_in,
        ],
        [node_f32, ((edges, width), f32, edge_spec)],
    )
    square_row = jnp.broadcast_to(jnp.sum(grad_shard * grad_shard), (1, width))
    tail = sum_small(
        jnp.concatenate(
            [local_bias[:2], attend_bias[:3], square_row, jnp.zeros((2, width), f32)], axis=0
        ),
        total,
    )
    top_mean = tops[0:1] / sums[4:5]
    top_rstd = lax.rsqrt(tops[1:2] / sums[4:5] - top_mean * top_mean + eps_norm)
    vector_total = jnp.concatenate(
        [
            tail[:5],
            backs[1:2],
            backs[0:1],
            backs[2:3],
            backs[0:1],
            backs[3:6],
            (tops[3:4] - top_mean * tops[2:3]) * top_rstd,
            tops[2:3],
        ],
        axis=0,
    )
    grad_norm = jnp.sqrt(tail[5, 0] + jnp.sum(vector_total * vector_total))
    factor = jnp.minimum(1.0, clip_limit / (grad_norm + 1e-06))
    new_weights, first_w, second_w = adamw(
        weights, factor * grad_shard, weight_moment1, weight_moment2, rate_mats, decay_mats
    )
    new_vectors, first_v, second_v = adamw(
        vectors, factor * vector_total, vector_moment1, vector_moment2, rate_vecs, 0.0
    )
    return (
        layer_out,
        node_grad,
        edge_grad,
        new_weights,
        first_w,
        second_w,
        new_vectors,
        first_v,
        second_v,
        grad_norm,
    )


def solution(mesh):
    in_specs = (
        P("rows", None),
        P("rows", None),
        P(("rows", "branch"), None),
        P("rows"),
        P("rows"),
        P("rows"),
        P("rows"),
        P("rows"),
        P(None, ("rows", "branch")),
        P(None, ("rows", "branch")),
        P(None, ("rows", "branch")),
        P(),
        P(),
        P(),
    )
    out_specs = (
        P(("rows", "branch"), None),
        P(("rows", "branch"), None),
        P(("rows", "branch"), None),
        P(None, ("rows", "branch")),
        P(None, ("rows", "branch")),
        P(None, ("rows", "branch")),
        P(),
        P(),
        P(),
        P(),
    )
    return jax.shard_map(
        per_device, mesh=mesh, in_specs=in_specs, out_specs=out_specs, check_vma=False
    )
```

profile of v0, /device:TPU:0, one launch (start us, length us, event | category | flops | bytes accessed | tf_op | source)
XLA Modules:
  0.0 272.3 jit_solution(17983104686166287789)
XLA Ops:
  1.6 4.0 %collective-permute-start = (bf16[1,13,2048]{2,1,0:T(8,128)(2,1)S(1)}, bf16[1,13,2048]{2,1,0:T(8,128)(2,1)S(1)}, u32[]{:S(2)}, u32[]{:S(2)}) collective-permute-start(bf16[1,13,2048]{2,1,0:T(8,128)(2,1)S(1)} %convert_bitcast_fusion), channel_id=1, source_target_pairs={{0,16},{1,17},{2,18},{3,19},{4,20},{5,21},{6,22},{7,23},{8,24},{9,... | collective-permute-start | bytes 159752 | tf_op jit(solution)/shard_map/ppermute | solution.py:463
  5.6 3.6 %collective-permute-done = bf16[1,13,2048]{2,1,0:T(8,128)(2,1)S(1)} collective-permute-done((bf16[1,13,2048]{2,1,0:T(8,128)(2,1)S(1)}, bf16[1,13,2048]{2,1,0:T(8,128)(2,1)S(1)}, u32[]{:S(2)}, u32[]{:S(2)}) %collective-permute-start) | collective-permute-done | bytes 53280 | tf_op jit(solution)/shard_map/ppermute | solution.py:463
  10.9 4.4 %collective-permute-done.1 = bf16[2,13,2048]{2,1,0:T(8,128)(2,1)S(1)} collective-permute-done((bf16[2,13,2048]{2,1,0:T(8,128)(2,1)S(1)}, bf16[2,13,2048]{2,1,0:T(8,128)(2,1)S(1)}, u32[]{:S(2)}, u32[]{:S(2)}) %collective-permute-start.1) | collective-permute-done | bytes 106528 | tf_op jit(solution)/shard_map/ppermute | solution.py:463
  17.1 4.6 %collective-permute-done.2 = bf16[4,13,2048]{2,1,0:T(8,128)(2,1)S(1)} collective-permute-done((bf16[4,13,2048]{2,1,0:T(8,128)(2,1)S(1)}, bf16[4,13,2048]{2,1,0:T(8,128)(2,1)S(1)}, u32[]{:S(2)}, u32[]{:S(2)}) %collective-permute-start.2) | collective-permute-done | bytes 213024 | tf_op jit(solution)/shard_map/ppermute | solution.py:463
  23.7 8.2 %collective-permute-done.3 = bf16[8,13,2048]{2,1,0:T(8,128)(2,1)S(1)} collective-permute-done((bf16[8,13,2048]{2,1,0:T(8,128)(2,1)S(1)}, bf16[8,13,2048]{2,1,0:T(8,128)(2,1)S(1)}, u32[]{:S(2)}, u32[]{:S(2)}) %collective-permute-start.3) | collective-permute-done | bytes 426016 | tf_op jit(solution)/shard_map/ppermute | solution.py:463
  43.0 13.1 %shard_map.215 = (f32[2048,256]{1,0:T(8,128)}, bf16[2048,256]{1,0:T(8,128)(2,1)S(1)}, bf16[2048,256]{1,0:T(8,128)(2,1)S(1)}, bf16[2048,256]{1,0:T(8,128)(2,1)S(1...) custom-call(s32[17]{0:T(128)S(1)} %pad_add_fusion.info_ref, ...), custom_call_target="tpu_custom_call" | custom-call | tf_op jit(solution)/shard_map/pallas_call | solution.py:445
  60.0 11.5 %shard_map.214 = (f32[2048,256]{1,0:T(8,128)S(1)}, f32[2048,256]{1,0:T(8,128)S(1)}, f32[2048,256]{1,0:T(8,128)}, f32[2048,256]{1,0:T(8,128)}, f32[4096,256]{1,0:...) custom-call(s32[17]{0:T(128)S(1)} %pad_add_fusion.info_ref, bf16[4096,256]{1,0:T(8,128)(2,1)} %x_ref.7, ...), custom_call_target="tpu_custom_call" | custom-call | tf_op jit(solution)/shard_map/pallas_call | solution.py:445
  86.9 5.2 %collective-permute-start.9 = (f32[8,256]{1,0:T(8,128)S(1)}, f32[8,256]{1,0:T(8,128)S(1)}, u32[]{:S(2)}, u32[]{:S(2)}) collective-permute-start(f32[8,256]{1,0:T(8,128)S(1)} %add.176), channel_id=1, source_target_pairs={{0,16},{1,17},{2,18},{3,19},{4,20},{5,21},{6,22},{7,23},{8,24},{9,... | collective-permute-start | bytes 24584 | tf_op jit(solution)/shard_map/ppermute | solution.py:463
  93.8 6.7 %shard_map.216 = (bf16[2048,256]{1,0:T(8,128)(2,1)S(1)}, f32[2048,512]{1,0:T(8,128)}, f32[2048,256]{1,0:T(8,128)S(1)}, f32[8,256]{1,0:T(8,128)S(1)}) custom-call(s32[17]{0:T(128)S(1)} %pad_add_fusion.info_ref, f32[2048,256]{1,0:T(8,128)} %copy-done.4, f32[2048,256]{1,0:T(8,128)} %get-tuple-element.50.global_ref, bf16[2048,256]{1,0:T(8,128)(2,1)S(1)} %copy-done.9, ...), custom_call_target="tpu_custom_call" | custom-call | tf_op jit(solution)/shard_map/pallas_call | solution.py:445
  113.9 2.9 %collective-permute-start.14 = (f32[8,256]{1,0:T(8,128)S(1)}, f32[8,256]{1,0:T(8,128)S(1)}, u32[]{:S(2)}, u32[]{:S(2)}) collective-permute-start(f32[8,256]{1,0:T(8,128)S(1)} %add.181), channel_id=1, source_target_pairs={{0,16},{1,17},{2,18},{3,19},{4,20},{5,21},{6,22},{7,23},{8,24},{9,... | collective-permute-start | bytes 24584 | tf_op jit(solution)/shard_map/ppermute | solution.py:463
  118.5 9.0 %shard_map.217 = (bf16[2048,256]{1,0:T(8,128)(2,1)}, bf16[2048,256]{1,0:T(8,128)(2,1)S(1)}, bf16[2048,512]{1,0:T(8,128)(2,1)}, bf16[2048,512]{1,0:T(8,128)(2,1)}...) custom-call(s32[17]{0:T(128)S(1)} %pad_add_fusion.info_ref, f32[2048,256]{1,0:T(8,128)} %copy-done.12, ...), custom_call_target="tpu_custom_call" | custom-call | tf_op jit(solution)/shard_map/pallas_call | solution.py:445
  140.6 2.9 %collective-permute-start.19 = (f32[8,256]{1,0:T(8,128)S(1)}, f32[8,256]{1,0:T(8,128)S(1)}, u32[]{:S(2)}, u32[]{:S(2)}) collective-permute-start(f32[8,256]{1,0:T(8,128)S(1)} %add.186), channel_id=1, source_target_pairs={{0,16},{1,17},{2,18},{3,19},{4,20},{5,21},{6,22},{7,23},{8,24},{9,... | collective-permute-start | bytes 24584 | tf_op jit(solution)/shard_map/ppermute | solution.py:463
  147.6 4.8 %shard_map.221 = bf16[4,256,256]{2,1,0:T(8,128)(2,1)S(1)} custom-call(s32[17]{0:T(128)S(1)} %pad_add_fusion.info_ref, bf16[2048,256]{1,0:T(8,128)(2,1)S(1)} %copy-done.23, bf16[2048,512]{1,0:T(8,128)(2,1)S(1)} %copy-done.13, bf16[2048,512]{1,0:T(8,128)(2,1)} %get-tuple-element.80.refs_2_, bf16[2048,256]{1,0:T(8,128)(2,1)S(1)} %copy-done.25), custom_call_target="tpu_custom_call" | custom-call | tf_op jit(solution)/shard_map/pallas_call | solution.py:445
  152.4 17.2 %shard_map.219 = (bf16[2048,768]{1,0:T(8,128)(2,1)}, f32[8,256]{1,0:T(8,128)S(1)}, bf16[4,256,256]{2,1,0:T(8,128)(2,1)S(1)}) custom-call(s32[17]{0:T(128)S(1)} %pad_add_fusion.info_ref, bf16[2048,256]{1,0:T(8,128)(2,1)S(1)} %get-tuple-element.57.dsum_ref, f32[2048,256]{1,0:T(8,128)} %get-tuple-element.50.global_ref, bf16[2048,256]{1,0:T(8,128)(2,1)S(1)} %copy-done.21, ...), custom_call_target="tpu_custom_call" | custom-call | tf_op jit(solution)/shard_map/pallas_call | solution.py:445
  169.6 13.7 %shard_map.218 = (bf16[2048,1024]{1,0:T(8,128)(2,1)}, bf16[4096,256]{1,0:T(8,128)(2,1)S(1)}, f32[8,256]{1,0:T(8,128)S(1)}, bf16[5,256,256]{2,1,0:T(8,128)(2,1)S(1)}) custom-call(s32[17]{0:T(128)S(1)} %pad_add_fusion.info_ref, bf16[2048,256]{1,0:T(8,128)(2,1)S(1)} %get-tuple-element.57.dsum_ref, f32[2048,256]{1,0:T(8,128)S(1)} %copy-done.5, ...), custom_call_target="tpu_custom_call" | custom-call | tf_op jit(solution)/shard_map/pallas_call | solution.py:445
  186.0 3.8 %reshape_reshape.7 = bf16[13,2,2,2,2,2,2048]{6,5,4,3,2,1,0:T(2,128)(2,1)S(1)} reshape(bf16[13,256,256]{2,1,0:T(8,128)(2,1)} %pad_maximum_fusion.1) | data formatting | bytes 3407872 | tf_op jit(solution)/shard_map/reshape;reshape | solution.py:496
  189.8 4.8 %constant_dynamic-slice_fusion = (bf16[13,2,2,2,2,1,2048]{6,5,4,3,2,1,0:T(2,128)(2,1)S(1)}, bf16[13,2,2,2,2,1,2048]{6,5,4,3,2,1,0:T(2,128)(2,1)}) fusion(bf16[13,2,2,2,2,2,2048]{6,5,4,3,2,1,0:T(2,128)(2,1)S(1)} %reshape_reshape.7, s32[]{:T(128)S(6)} %select_n.122, s32[]{:T(128)S(6)} %select_n.121), kind=kLoop, calls=%fused_computation.47 | loop fusion | bytes 3407880 | tf_op jit(solution)/shard_map/dynamic-slice.1
  199.6 3.5 %fusion = bf16[2,2,2,2,13,2048]{5,4,3,2,1,0:T(8,128)(2,1)} fusion(bf16[13,2,2,2,2,1,2048]{6,5,4,3,2,1,0:T(2,128)(2,1)S(1)} %copy-done.27, bf16[2,2,2,2,13,2048]{5,3,4,2,1,0:T(2,128)(2,1)} %collective-permute-done.20), kind=kLoop, calls=%fused_computation.2 | loop fusion | flops 1703936 | bytes 2555904 | tf_op jit(solution)/shard_map/convert_element_type | solution.py:45
  205.7 12.6 %collective-permute-done.21 = bf16[2,2,2,13,2048]{4,3,2,1,0:T(8,128)(2,1)} collective-permute-done((bf16[2,2,2,13,2048]{4,3,2,1,0:T(8,128)(2,1)S(1)}, bf16[2,2,2,13,2048]{4,3,2,1,0:T(8,128)(2,1)}, u32[]{:S(2)}, u32[]{:S(2)}) %collective-permute-start.21) | collective-permute-done | bytes 426016 | tf_op jit(solution)/shard_map/ppermute | solution.py:463
  221.9 6.3 %collective-permute-done.22 = bf16[2,2,13,2048]{3,2,1,0:T(8,128)(2,1)} collective-permute-done((bf16[2,2,13,2048]{3,2,1,0:T(8,128)(2,1)}, bf16[2,2,13,2048]{3,2,1,0:T(8,128)(2,1)}, u32[]{:S(2)}, u32[]{:S(2)}) %collective-permute-start.22) | collective-permute-done | bytes 213024 | tf_op jit(solution)/shard_map/ppermute | solution.py:463
  232.0 3.9 %collective-permute-done.23 = bf16[2,13,2048]{2,1,0:T(8,128)(2,1)S(1)} collective-permute-done((bf16[2,13,2048]{2,1,0:T(8,128)(2,1)S(1)}, bf16[2,13,2048]{2,1,0:T(8,128)(2,1)S(1)}, u32[]{:S(2)}, u32[]{:S(2)}) %collective-permute-start.23) | collective-permute-done | bytes 106528 | tf_op jit(solution)/shard_map/ppermute | solution.py:463
  237.0 5.8 %collective-permute-done.24 = bf16[13,2048]{1,0:T(8,128)(2,1)S(1)} collective-permute-done((bf16[13,2048]{1,0:T(8,128)(2,1)S(1)}, bf16[13,2048]{1,0:T(8,128)(2,1)S(1)}, u32[]{:S(2)}, u32[]{:S(2)}) %collective-permute-start.24) | collective-permute-done | bytes 53280 | tf_op jit(solution)/shard_map/ppermute | solution.py:463
  253.3 3.1 %collective-permute-done.28 = f32[8,256]{1,0:T(8,128)S(1)} collective-permute-done((f32[8,256]{1,0:T(8,128)S(1)}, f32[8,256]{1,0:T(8,128)S(1)}, u32[]{:S(2)}, u32[]{:S(2)}) %collective-permute-start.28) | collective-permute-done | bytes 8224 | tf_op jit(solution)/shard_map/ppermute | solution.py:463
  258.1 9.0 %shard_map.220 = (f32[2048,256]{1,0:T(8,128)}, f32[4096,256]{1,0:T(8,128)}) custom-call(s32[17]{0:T(128)S(1)} %pad_add_fusion.info_ref, bf16[2048,256]{1,0:T(8,128)(2,1)S(1)} %get-tuple-element.57.dsum_ref, f32[2048,256]{1,0:T(8,128)S(1)} %copy-done.6, f32[2048,256]{1,0:T(8,128)} %get-tuple-element.50.global_ref, ...), custom_call_target="tpu_custom_call" | custom-call | tf_op jit(solution)/shard_map/pallas_call | solution.py:445
  (196 shorter events, 103.2 us)
Async XLA Ops:
  1.6 7.7 %collective-permute-start = (bf16[1,13,2048]{2,1,0:T(8,128)(2,1)S(1)}, bf16[1,13,2048]{2,1,0:T(8,128)(2,1)S(1)}, u32[]{:S(2)}, u32[]{:S(2)}) collective-permute-start(bf16[1,13,2048]{2,1,0:T(8,128)(2,1)S(1)} %convert_bitcast_fusion), channel_id=1, source_target_pairs={{0,16},{1,17},{2,18},{3,19},{4,20},{5,21},{6,22},{7,23},{8,24},{9,... | collective-permute-start | bytes 159752 | tf_op jit(solution)/shard_map/ppermute | solution.py:463
  10.2 5.0 %collective-permute-start.1 = (bf16[2,13,2048]{2,1,0:T(8,128)(2,1)S(1)}, bf16[2,13,2048]{2,1,0:T(8,128)(2,1)S(1)}, u32[]{:S(2)}, u32[]{:S(2)}) collective-permute-start(bf16[2,13,2048]{2,1,0:T(8,128)(2,1)S(1)} %pad_maximum_fusion.5), channel_id=1, source_target_pairs={{0,8},{1,9},{2,10},{3,11},{4,12},{5,13},{6,14},{7,15},{8,0},{9,1},... | collective-permute-start | bytes 319496 | tf_op jit(solution)/shard_map/ppermute | solution.py:463
  15.3 6.4 %collective-permute-start.2 = (bf16[4,13,2048]{2,1,0:T(8,128)(2,1)S(1)}, bf16[4,13,2048]{2,1,0:T(8,128)(2,1)S(1)}, u32[]{:S(2)}, u32[]{:S(2)}) collective-permute-start(bf16[4,13,2048]{2,1,0:T(8,128)(2,1)S(1)} %pad_maximum_fusion.4), channel_id=1, source_target_pairs={{0,4},{1,5},{2,6},{3,7},{4,0},{5,1},{6,2},{7,3},{8,12},{9,13},{10,... | collective-permute-start | bytes 638984 | tf_op jit(solution)/shard_map/ppermute | solution.py:463
  21.9 9.9 %collective-permute-start.3 = (bf16[8,13,2048]{2,1,0:T(8,128)(2,1)S(1)}, bf16[8,13,2048]{2,1,0:T(8,128)(2,1)S(1)}, u32[]{:S(2)}, u32[]{:S(2)}) collective-permute-start(bf16[8,13,2048]{2,1,0:T(8,128)(2,1)S(1)} %pad_maximum_fusion.3), channel_id=1, source_target_pairs={{0,2},{1,3},{2,0},{3,1},{4,6},{5,7},{6,4},{7,5},{8,10},{9,11},{10,... | collective-permute-start | bytes 1277960 | tf_op jit(solution)/shard_map/ppermute | solution.py:463
  75.8 3.7 %collective-permute-start.6 = (f32[8,256]{1,0:T(8,128)S(1)}, f32[8,256]{1,0:T(8,128)S(1)}, u32[]{:S(2)}, u32[]{:S(2)}) collective-permute-start(f32[8,256]{1,0:T(8,128)S(1)} %fusion.9), channel_id=1, source_target_pairs={{0,2},{1,3},{2,0},{3,1},{4,6},{5,7},{6,4},{7,5},{8,10},{9,11},{10,... | collective-permute-start | bytes 24584 | tf_op jit(solution)/shard_map/ppermute | solution.py:463
  79.5 3.7 %collective-permute-start.7 = (f32[8,256]{1,0:T(8,128)S(1)}, f32[8,256]{1,0:T(8,128)S(1)}, u32[]{:S(2)}, u32[]{:S(2)}) collective-permute-start(f32[8,256]{1,0:T(8,128)S(1)} %add.174), channel_id=1, source_target_pairs={{0,4},{1,5},{2,6},{3,7},{4,0},{5,1},{6,2},{7,3},{8,12},{9,13},{10,... | collective-permute-start | bytes 24584 | tf_op jit(solution)/shard_map/ppermute | solution.py:463
  83.1 3.8 %collective-permute-start.8 = (f32[8,256]{1,0:T(8,128)S(1)}, f32[8,256]{1,0:T(8,128)S(1)}, u32[]{:S(2)}, u32[]{:S(2)}) collective-permute-start(f32[8,256]{1,0:T(8,128)S(1)} %add.175), channel_id=1, source_target_pairs={{0,8},{1,9},{2,10},{3,11},{4,12},{5,13},{6,14},{7,15},{8,0},{9,1},... | collective-permute-start | bytes 24584 | tf_op jit(solution)/shard_map/ppermute | solution.py:463
  86.9 6.8 %collective-permute-start.9 = (f32[8,256]{1,0:T(8,128)S(1)}, f32[8,256]{1,0:T(8,128)S(1)}, u32[]{:S(2)}, u32[]{:S(2)}) collective-permute-start(f32[8,256]{1,0:T(8,128)S(1)} %add.176), channel_id=1, source_target_pairs={{0,16},{1,17},{2,18},{3,19},{4,20},{5,21},{6,22},{7,23},{8,24},{9,... | collective-permute-start | bytes 24584 | tf_op jit(solution)/shard_map/ppermute | solution.py:463
  103.0 3.7 %collective-permute-start.11 = (f32[8,256]{1,0:T(8,128)S(1)}, f32[8,256]{1,0:T(8,128)S(1)}, u32[]{:S(2)}, u32[]{:S(2)}) collective-permute-start(f32[8,256]{1,0:T(8,128)S(1)} %add.178), channel_id=1, source_target_pairs={{0,2},{1,3},{2,0},{3,1},{4,6},{5,7},{6,4},{7,5},{8,10},{9,11},{10,... | collective-permute-start | bytes 24584 | tf_op jit(solution)/shard_map/ppermute | solution.py:463
  106.6 3.7 %collective-permute-start.12 = (f32[8,256]{1,0:T(8,128)S(1)}, f32[8,256]{1,0:T(8,128)S(1)}, u32[]{:S(2)}, u32[]{:S(2)}) collective-permute-start(f32[8,256]{1,0:T(8,128)S(1)} %add.179), channel_id=1, source_target_pairs={{0,4},{1,5},{2,6},{3,7},{4,0},{5,1},{6,2},{7,3},{8,12},{9,13},{10,... | collective-permute-start | bytes 24584 | tf_op jit(solution)/shard_map/ppermute | solution.py:463
  110.3 3.7 %collective-permute-start.13 = (f32[8,256]{1,0:T(8,128)S(1)}, f32[8,256]{1,0:T(8,128)S(1)}, u32[]{:S(2)}, u32[]{:S(2)}) collective-permute-start(f32[8,256]{1,0:T(8,128)S(1)} %add.180), channel_id=1, source_target_pairs={{0,8},{1,9},{2,10},{3,11},{4,12},{5,13},{6,14},{7,15},{8,0},{9,1},... | collective-permute-start | bytes 24584 | tf_op jit(solution)/shard_map/ppermute | solution.py:463
  113.9 4.5 %collective-permute-start.14 = (f32[8,256]{1,0:T(8,128)S(1)}, f32[8,256]{1,0:T(8,128)S(1)}, u32[]{:S(2)}, u32[]{:S(2)}) collective-permute-start(f32[8,256]{1,0:T(8,128)S(1)} %add.181), channel_id=1, source_target_pairs={{0,16},{1,17},{2,18},{3,19},{4,20},{5,21},{6,22},{7,23},{8,24},{9,... | collective-permute-start | bytes 24584 | tf_op jit(solution)/shard_map/ppermute | solution.py:463
  129.6 3.7 %collective-permute-start.16 = (f32[8,256]{1,0:T(8,128)S(1)}, f32[8,256]{1,0:T(8,128)S(1)}, u32[]{:S(2)}, u32[]{:S(2)}) collective-permute-start(f32[8,256]{1,0:T(8,128)S(1)} %add.183), channel_id=1, source_target_pairs={{0,2},{1,3},{2,0},{3,1},{4,6},{5,7},{6,4},{7,5},{8,10},{9,11},{10,... | collective-permute-start | bytes 24584 | tf_op jit(solution)/shard_map/ppermute | solution.py:463
  133.3 3.7 %collective-permute-start.17 = (f32[8,256]{1,0:T(8,128)S(1)}, f32[8,256]{1,0:T(8,128)S(1)}, u32[]{:S(2)}, u32[]{:S(2)}) collective-permute-start(f32[8,256]{1,0:T(8,128)S(1)} %add.184), channel_id=1, source_target_pairs={{0,4},{1,5},{2,6},{3,7},{4,0},{5,1},{6,2},{7,3},{8,12},{9,13},{10,... | collective-permute-start | bytes 24584 | tf_op jit(solution)/shard_map/ppermute | solution.py:463
  136.9 3.7 %collective-permute-start.18 = (f32[8,256]{1,0:T(8,128)S(1)}, f32[8,256]{1,0:T(8,128)S(1)}, u32[]{:S(2)}, u32[]{:S(2)}) collective-permute-start(f32[8,256]{1,0:T(8,128)S(1)} %add.185), channel_id=1, source_target_pairs={{0,8},{1,9},{2,10},{3,11},{4,12},{5,13},{6,14},{7,15},{8,0},{9,1},... | collective-permute-start | bytes 24584 | tf_op jit(solution)/shard_map/ppermute | solution.py:463
  140.6 11.8 %collective-permute-start.19 = (f32[8,256]{1,0:T(8,128)S(1)}, f32[8,256]{1,0:T(8,128)S(1)}, u32[]{:S(2)}, u32[]{:S(2)}) collective-permute-start(f32[8,256]{1,0:T(8,128)S(1)} %add.186), channel_id=1, source_target_pairs={{0,16},{1,17},{2,18},{3,19},{4,20},{5,21},{6,22},{7,23},{8,24},{9,... | collective-permute-start | bytes 24584 | tf_op jit(solution)/shard_map/ppermute | solution.py:463
  204.2 14.1 %collective-permute-start.21 = (bf16[2,2,2,13,2048]{4,3,2,1,0:T(8,128)(2,1)S(1)}, bf16[2,2,2,13,2048]{4,3,2,1,0:T(8,128)(2,1)}, u32[]{:S(2)}, u32[]{:S(2)}) collective-permute-start(bf16[2,2,2,13,2048]{4,3,2,1,0:T(8,128)(2,1)S(1)} %dynamic-slice_bitcast_fusion), channel_id=1, source_target_pairs={{0,2},{1,3},{2,0},{3,1},{4,6},{5,7},{6,4},{7,5},{8,10},{9,11},{10,... | collective-permute-start | bytes 1277960 | tf_op jit(solution)/shard_map/ppermute | solution.py:463
  220.4 7.8 %collective-permute-start.22 = (bf16[2,2,13,2048]{3,2,1,0:T(8,128)(2,1)}, bf16[2,2,13,2048]{3,2,1,0:T(8,128)(2,1)}, u32[]{:S(2)}, u32[]{:S(2)}) collective-permute-start(bf16[2,2,13,2048]{3,2,1,0:T(8,128)(2,1)} %dynamic-slice_bitcast_fusion.1), channel_id=1, source_target_pairs={{0,4},{1,5},{2,6},{3,7},{4,0},{5,1},{6,2},{7,3},{8,12},{9,13},{10,... | collective-permute-start | bytes 638984 | tf_op jit(solution)/shard_map/ppermute | solution.py:463
  230.9 5.0 %collective-permute-start.23 = (bf16[2,13,2048]{2,1,0:T(8,128)(2,1)S(1)}, bf16[2,13,2048]{2,1,0:T(8,128)(2,1)S(1)}, u32[]{:S(2)}, u32[]{:S(2)}) collective-permute-start(bf16[2,13,2048]{2,1,0:T(8,128)(2,1)S(1)} %dynamic-slice_bitcast_fusion.2), channel_id=1, source_target_pairs={{0,8},{1,9},{2,10},{3,11},{4,12},{5,13},{6,14},{7,15},{8,0},{9,1},... | collective-permute-start | bytes 319496 | tf_op jit(solution)/shard_map/ppermute | solution.py:463
  236.9 5.9 %collective-permute-start.24 = (bf16[13,2048]{1,0:T(8,128)(2,1)S(1)}, bf16[13,2048]{1,0:T(8,128)(2,1)S(1)}, u32[]{:S(2)}, u32[]{:S(2)}) collective-permute-start(bf16[13,2048]{1,0:T(8,128)(2,1)S(1)} %dynamic-slice_bitcast_fusion.3), channel_id=1, source_target_pairs={{0,16},{1,17},{2,18},{3,19},{4,20},{5,21},{6,22},{7,23},{8,24},{9,... | collective-permute-start | bytes 159752 | tf_op jit(solution)/shard_map/ppermute | solution.py:463
  245.5 3.7 %collective-permute-start.26 = (f32[8,256]{1,0:T(8,128)S(1)}, f32[8,256]{1,0:T(8,128)S(1)}, u32[]{:S(2)}, u32[]{:S(2)}) collective-permute-start(f32[8,256]{1,0:T(8,128)S(1)} %fusion.10), channel_id=1, source_target_pairs={{0,2},{1,3},{2,0},{3,1},{4,6},{5,7},{6,4},{7,5},{8,10},{9,11},{10,... | collective-permute-start | bytes 24584 | tf_op jit(solution)/shard_map/ppermute | solution.py:463
  249.1 3.7 %collective-permute-start.27 = (f32[8,256]{1,0:T(8,128)S(1)}, f32[8,256]{1,0:T(8,128)S(1)}, u32[]{:S(2)}, u32[]{:S(2)}) collective-permute-start(f32[8,256]{1,0:T(8,128)S(1)} %add.204), channel_id=1, source_target_pairs={{0,4},{1,5},{2,6},{3,7},{4,0},{5,1},{6,2},{7,3},{8,12},{9,13},{10,... | collective-permute-start | bytes 24584 | tf_op jit(solution)/shard_map/ppermute | solution.py:463
  252.8 3.7 %collective-permute-start.28 = (f32[8,256]{1,0:T(8,128)S(1)}, f32[8,256]{1,0:T(8,128)S(1)}, u32[]{:S(2)}, u32[]{:S(2)}) collective-permute-start(f32[8,256]{1,0:T(8,128)S(1)} %add.205), channel_id=1, source_target_pairs={{0,8},{1,9},{2,10},{3,11},{4,12},{5,13},{6,14},{7,15},{8,0},{9,1},... | collective-permute-start | bytes 24584 | tf_op jit(solution)/shard_map/ppermute | solution.py:463
  256.4 10.7 %collective-permute-start.29 = (f32[8,256]{1,0:T(8,128)S(1)}, f32[8,256]{1,0:T(8,128)S(1)}, u32[]{:S(2)}, u32[]{:S(2)}) collective-permute-start(f32[8,256]{1,0:T(8,128)S(1)} %add.206), channel_id=1, source_target_pairs={{0,16},{1,17},{2,18},{3,19},{4,20},{5,21},{6,22},{7,23},{8,24},{9,... | collective-permute-start | bytes 24584 | tf_op jit(solution)/shard_map/ppermute | solution.py:463
  (43 other events, 315.4 us)
where the time goes:
time: 273 us; the launch traced here: 272 us
  Pallas kernels  86.8 us (32%)
  waiting for transfers between devices  86.7 us (32%)
  starting transfers between devices  41 us (15%)
  local copies, waits for them, and re-layouts  37.1 us (14%)
  other arithmetic  16.3 us (6%)
  between operations  4.33 us (2%)
    pallas_call x9, Pallas kernels, call(): pl.pallas_call(kernel, grid_spec=pltpu.PrefetchScalarGridSpec(num_scalar_...  86.8 us
    ppermute x30, waiting for transfers between devices, swap_with(): lax.ppermute(values, axis_names, [(place, place ^ step) for place in rang...  86.7 us
    ppermute x30, starting transfers between devices, swap_with(): lax.ppermute(values, axis_names, [(place, place ^ step) for place in rang...  41 us
    unnamed x75, local copies, waits for them, and re-layouts  18.9 us
    convert_element_type x4, other arithmetic, low(): return values.astype(bf16)  7.49 us
  transfers between devices with their start and end apart: 30, of which 27 were waited for; matrix products, arithmetic and copies ran while one was open for 0% of the time, Pallas kernels for 6%

commit v1 on v0

--- a/solution.py
+++ b/solution.py
@@ -97,7 +97,7 @@
 
 def local_kernel(
     info_ref, x_ref, e_ref, hot_ref, turned_ref, w_ref, vec_ref,
-    out_ref, gated_ref, recip_ref, ratio_ref, open_ref, bsrc_ref, sums_ref,
+    out_ref, slope_ref, recip_ref, fall_ref, open_ref, bend_ref, bsrc_ref, sums_ref,
 ):
     group = x_ref.shape[0] // BLOCK
     x = x_ref[...]
@@ -115,7 +115,8 @@
         gate = c_part[edges] + mm(hot, jnp.concatenate([d_part[nodes], e_part[nodes]], axis=0))
         opened = sig(gate)
         b_source = mm(hot[:, BLOCK:], b_part[nodes])
-        open_ref[edges, :] = opened
+        open_ref[edges, :] = low(opened)
+        bend_ref[edges, :] = low(opened * (1.0 - opened))
         bsrc_ref[edges, :] = low(b_source)
         dst_turned = turned_ref[place * EB : place * EB + BLOCK, :]
         nums.append(mm(dst_turned, low(opened * b_source)))
@@ -123,10 +124,11 @@
     recip = 1.0 / (jnp.concatenate(dens, axis=0) + 1.0)
     ratio = jnp.concatenate(nums, axis=0) * recip
     gated = a_part + ratio
-    out = x.astype(f32) + gated * sig(gated)
-    gated_ref[...] = gated
-    recip_ref[...] = recip
-    ratio_ref[...] = ratio
+    gated_sig = sig(gated)
+    out = x.astype(f32) + gated * gated_sig
+    slope_ref[...] = low(gated_sig * (1.0 + gated * (1.0 - gated_sig)))
+    recip_ref[...] = low(recip)
+    fall_ref[...] = low(ratio * recip)
     out_ref[...] = out
     live = live_of(info_ref, pl.program_id(0) * group, group, out.shape[1])
     kept = live * out
@@ -165,7 +167,7 @@
             part = jnp.exp((part - jnp.max(part, axis=0, keepdims=True)) * score_scale)
             part = part * (1.0 / jnp.sum(part, axis=0, keepdims=True))
             probs.append(low(part))
-            turned.append(low(part.T))
+            turned.append(low(part).T)
         prob_ref[nodes, :] = jnp.concatenate(probs, axis=1)
         att_ref[nodes, :] = low(
             mm(jnp.concatenate(turned, axis=1), head_stack(valued[nodes]))
@@ -179,7 +181,7 @@
 
 def mix_kernel(
     info_ref, local_ref, global_ref, cot_ref, sums_ref, w_ref, vec_ref,
-    low_ref, hidden_ref, mixed_ref, stat_ref,
+    low_ref, hlow_ref, slope_ref, lhat_ref, ghat_ref, mixed_ref, stat_ref,
 ):
     group = local_ref.shape[0] // BLOCK
     width = local_ref.shape[1]
@@ -187,18 +189,25 @@
     count_row = sums[4:5]
     local_mean, local_rstd = norm_terms(sums, 0, count_row)
     global_mean, global_rstd = norm_terms(sums, 2, count_row)
-    local_norm = (local_ref[...] - local_mean) * (vec_ref[5:6, :] * local_rstd) + vec_ref[6:7, :]
-    global_norm = (global_ref[...] - global_mean) * (vec_ref[7:8, :] * global_rstd) + vec_ref[
-        8:9, :
-    ]
+    local_hat = (local_ref[...] - local_mean) * local_rstd
+    global_hat = (global_ref[...] - global_mean) * global_rstd
+    lhat_ref[...] = low(local_hat)
+    ghat_ref[...] = low(global_hat)
+    local_norm = local_hat * vec_ref[5:6, :] + vec_ref[6:7, :]
+    global_norm = global_hat * vec_ref[7:8, :] + vec_ref[8:9, :]
     summed = low(local_norm).astype(f32) + low(global_norm).astype(f32)
     summed_low = low(summed)
     low_ref[...] = summed_low
     mixed = summed + vec_ref[11:12, :]
     for half in range(2):
         hidden = mm(summed_low, w_ref[9 + half]) + vec_ref[9 + half : 10 + half, :]
-        hidden_ref[:, half * width : (half + 1) * width] = hidden
-        mixed = mixed + mm(low(hidden * sig(hidden)), w_ref[11 + half])
+        sig_value = sig(hidden)
+        hidden_low = low(hidden * sig_value)
+        hlow_ref[:, half * width : (half + 1) * width] = hidden_low
+        slope_ref[:, half * width : (half + 1) * width] = low(
+            sig_value * (1.0 + hidden * (1.0 - sig_value))
+        )
+        mixed = mixed + mm(hidden_low, w_ref[11 + half])
     mixed_ref[...] = mixed
     live = live_of(info_ref, pl.program_id(0) * group, group, width)
     kept = live * mixed
@@ -209,9 +218,9 @@
 
 
 def mix_back_kernel(
-    info_ref, mixed_ref, hidden_ref, cot_ref, local_ref, global_ref, sums_ref, tops_ref, w_ref,
+    info_ref, mixed_ref, slope_ref, cot_ref, lhat_ref, ghat_ref, sums_ref, tops_ref, w_ref,
     vec_ref,
-    layer_ref, dmix_ref, dhid_ref, hlow_ref, dsum_ref, stat_ref,
+    layer_ref, dmix_ref, dhid_ref, dsum_ref, stat_ref,
 ):
     group = mixed_ref.shape[0] // BLOCK
     width = mixed_ref.shape[1]
@@ -234,27 +243,19 @@
     rows = []
     for half in range(2):
         cols = slice(half * width, (half + 1) * width)
-        hidden = hidden_ref[:, cols]
-        sig_value = sig(hidden)
-        hlow_ref[:, cols] = low(hidden * sig_value)
-        d_hidden = low(
-            mm_back(d_mixed_low, w_ref[11 + half])
-            * (sig_value * (1.0 + hidden * (1.0 - sig_value)))
-        )
+        d_hidden = low(mm_back(d_mixed_low, w_ref[11 + half]) * slope_ref[:, cols].astype(f32))
         dhid_ref[:, cols] = d_hidden
         rows.append(col_sum(d_hidden.astype(f32)))
         d_summed = d_summed + mm_back(d_hidden, w_ref[9 + half])
     d_low = low(d_summed)
     dsum_ref[...] = d_low
     d_sum = d_low.astype(f32)
-    local_mean, local_rstd = norm_terms(sums, 0, count_row)
-    global_mean, global_rstd = norm_terms(sums, 2, count_row)
     add_rows(
         stat_ref,
         [
             col_sum(d_sum),
-            col_sum(d_sum * ((local_ref[...] - local_mean) * local_rstd)),
-            col_sum(d_sum * ((global_ref[...] - global_mean) * global_rstd)),
+            col_sum(d_sum * lhat_ref[...].astype(f32)),
+            col_sum(d_sum * ghat_ref[...].astype(f32)),
             rows[0],
             rows[1],
             col_sum(d_mixed),
@@ -274,26 +275,39 @@
 def emit(acc_ref, out_ref):
     @pl.when(pl.program_id(0) == pl.num_programs(0) - 1)
     def _():
-        out_ref[...] = low(acc_ref[...])
-
-
-def mix_grad_kernel(slow_ref, dhid_ref, hlow_ref, dmix_ref, out_ref, acc_ref):
+        out_ref[...] = acc_ref[...]
+
+
+def inner_grad_kernel(info_ref, slow_ref, dhid_ref, out_ref, acc_ref):
     width = slow_ref.shape[1]
-    terms = []
-    for half in range(2):
-        terms.append(mm_rows(slow_ref[...], dhid_ref[:, half * width : (half + 1) * width]))
-    for half in range(2):
-        terms.append(mm_rows(hlow_ref[:, half * width : (half + 1) * width], dmix_ref[...]))
-    accumulate(acc_ref, terms)
+    accumulate(
+        acc_ref,
+        [
+            mm_rows(slow_ref[...], dhid_ref[:, half * width : (half + 1) * width])
+            for half in range(2)
+        ],
+    )
     emit(acc_ref, out_ref)
 
 
-def norm_back(info_ref, dsum_ref, value_ref, sums, backs, first, gain_row, hat_row):
-    group = value_ref.shape[0] // BLOCK
+def outer_grad_kernel(info_ref, hlow_ref, dmix_ref, out_ref, acc_ref):
+    width = dmix_ref.shape[1]
+    accumulate(
+        acc_ref,
+        [
+            mm_rows(hlow_ref[:, half * width : (half + 1) * width], dmix_ref[...])
+            for half in range(2)
+        ],
+    )
+    emit(acc_ref, out_ref)
+
+
+def norm_back(info_ref, dsum_ref, hat_ref, sums, backs, first, gain_row, hat_row):
+    group = hat_ref.shape[0] // BLOCK
     count_row = sums[4:5]
-    mean, rstd = norm_terms(sums, first, count_row)
-    live = live_of(info_ref, pl.program_id(0) * group, group, value_ref.shape[1])
-    hat = (value_ref[...] - mean) * rstd
+    rstd = norm_terms(sums, first, count_row)[1]
+    live = live_of(info_ref, pl.program_id(0) * group, group, hat_ref.shape[1])
+    hat = hat_ref[...].astype(f32)
     return (gain_row * rstd) * (
         dsum_ref[...].astype(f32)
         - live * (backs[0:1] / count_row + hat * (backs[hat_row : hat_row + 1] / count_row))
@@ -301,8 +315,8 @@
 
 
 def local_back_kernel(
-    info_ref, dsum_ref, local_ref, gated_ref, recip_ref, ratio_ref, open_ref, bsrc_ref, hot_ref,
-    turned_ref, x_ref, e_ref, sums_ref, backs_ref, vec_ref,
+    info_ref, dsum_ref, local_ref, slope_ref, recip_ref, fall_ref, open_ref, bend_ref, bsrc_ref,
+    hot_ref, turned_ref, x_ref, e_ref, sums_ref, backs_ref, vec_ref,
     dnode_ref, dedge_ref, stat_ref, out_ref, acc_ref,
 ):
     group = local_ref.shape[0] // BLOCK
@@ -310,23 +324,20 @@
     d_local = norm_back(
         info_ref, dsum_ref, local_ref, sums_ref[...], backs_ref[...], 0, vec_ref[5:6, :], 1
     )
-    gated = gated_ref[...]
-    sig_value = sig(gated)
-    d_gated = d_local * (sig_value * (1.0 + gated * (1.0 - sig_value)))
+    d_gated = d_local * slope_ref[...].astype(f32)
     dnode_ref[:, :width] = low(d_gated)
-    scaled = d_gated * recip_ref[...]
-    d_num = low(scaled)
-    d_den = low(-scaled * ratio_ref[...])
+    d_num = low(d_gated * recip_ref[...].astype(f32))
+    d_den = low(-d_gated * fall_ref[...].astype(f32))
     pre_row = jnp.zeros((1, width), f32)
     for place in range(group):
         nodes = slice(place * BLOCK, (place + 1) * BLOCK)
         edges = slice(place * EB, (place + 1) * EB)
         hot_dst = hot_ref[edges, :BLOCK]
         d_message = mm(hot_dst, d_num[nodes])
-        opened = open_ref[edges, :]
+        opened = open_ref[edges, :].astype(f32)
         d_open = d_message * bsrc_ref[edges, :].astype(f32) + mm(hot_dst, d_den[nodes])
         d_source = low(d_message * opened)
-        d_pre = d_open * (opened * (1.0 - opened))
+        d_pre = d_open * bend_ref[edges, :].astype(f32)
         d_pre_low = low(d_pre)
         pre_row = pre_row + col_sum(d_pre)
         dedge_ref[edges, :] = d_pre_low
@@ -353,9 +364,10 @@
 
 def attend_back_kernel(
     info_ref, dsum_ref, global_ref, att_ref, q_ref, k_ref, v_ref, prob_ref, x_ref, sums_ref,
-    backs_ref, w_ref, vec_ref,
-    dqkv_ref, stat_ref, out_ref, acc_ref,
+    backs_ref, w_ref, vec_ref, lgrad_ref, igrad_ref, ograd_ref,
+    dqkv_ref, stat_ref, *out_and_acc,
 ):
+    acc_ref = out_and_acc[-1]
     group = global_ref.shape[0] // BLOCK
     width = global_ref.shape[1]
     score_scale = (width // HEADS) ** (-0.5)
@@ -377,7 +389,7 @@
             inner = jnp.sum(prob * part, axis=0, keepdims=True)
             d_score = prob * (part - inner) * score_scale
             straight.append(low(d_score))
-            turned.append(low(d_score.T))
+            turned.append(low(d_score).T)
         dqkv_ref[nodes, :width] = low(
             mm(jnp.concatenate(turned, axis=1), head_stack(k_ref[nodes, :]))
         )
@@ -399,24 +411,99 @@
         [mm_rows(x, dqkv_ref[:, part * width : (part + 1) * width]) for part in range(3)]
         + [mm_rows(att_ref[...], d_low)],
     )
-    emit(acc_ref, out_ref)
-
-
-def input_grad_kernel(
-    info_ref, dsum_ref, local_ref, global_ref, dnode_ref, dqkv_ref, dedge_ref, sums_ref,
-    backs_ref, w_ref, vec_ref,
-    node_ref, edge_ref,
+    last = pl.num_programs(0) - 1
+
+    @pl.when(pl.program_id(0) == last)
+    def _():
+        parts = [lgrad_ref.at[place] for place in range(5)]
+        parts = parts + [acc_ref.at[place] for place in range(4)]
+        parts = parts + [ref.at[place] for ref in (igrad_ref, ograd_ref) for place in range(2)]
+        if len(out_and_acc) == 2:
+            for place, part in enumerate(parts):
+                out_and_acc[0][place] = low(part[...])
+        else:
+            pack(info_ref, parts, out_and_acc[0], out_and_acc[1])
+
+
+def reach(order, index):
+    found = 0
+    for place, step in enumerate(order):
+        if index >> (len(order) - 1 - place) & 1:
+            found ^= step >> 1
+    return found
+
+
+def chip_orders(total):
+    chips = steps_of(total)[1:]
+    return (chips, chips[1:-1] + chips[:1] + chips[-1:])
+
+
+def pack(info_ref, parts, keep_ref, send_ref):
+    slots = keep_ref.shape[0]
+    orders = chip_orders(2 * slots)
+    core = info_ref[info_ref.shape[0] - 2]
+    chip = info_ref[info_ref.shape[0] - 1]
+    for slot in range(slots):
+        near = [reach(order, slot) for order in orders]
+        for out_ref, owner in ((keep_ref, core), (send_ref, 1 - core)):
+            step = jnp.where(owner == 0, near[0], near[1])
+            row = pl.multiple_of(16 * jnp.bitwise_xor(chip, step) + 8 * owner, 8)
+            for first in range(0, len(parts), 2):
+                pair = [part[pl.ds(row, 8), :] for part in parts[first : first + 2]]
+                out_ref[slot, first * 8 : first * 8 + 8 * len(pair), :] = low(
+                    jnp.concatenate(pair, axis=0)
+                )
+
+
+def assemble_kernel(info_ref, held_ref, other_ref, out_ref):
+    slots, tall, _ = held_ref.shape
+    orders = chip_orders(2 * slots)
+    core = info_ref[info_ref.shape[0] - 2]
+    chip = info_ref[info_ref.shape[0] - 1]
+
+    def fill(even_ref, odd_ref):
+        for far in range(slots):
+            even, odd = [
+                [slot for slot in range(slots) if reach(order, slot) == far][0] for order in orders
+            ]
+            row = pl.multiple_of(16 * jnp.bitwise_xor(chip, far), 16)
+            for first in range(0, tall, 16):
+                size = min(16, tall - first)
+                upper = even_ref[even, first : first + size, :].astype(f32)
+                lower = odd_ref[odd, first : first + size, :].astype(f32)
+                for half in range(size // 8):
+                    rows = slice(half * 8, half * 8 + 8)
+                    out_ref[first // 8 + half, pl.ds(row, 16), :] = low(
+                        jnp.concatenate([upper[rows], lower[rows]], axis=0)
+                    )
+
+    @pl.when(core == 0)
+    def _():
+        fill(held_ref, other_ref)
+
+    @pl.when(core != 0)
+    def _():
+        fill(other_ref, held_ref)
+
+
+def node_grad_kernel(
+    info_ref, dsum_ref, lhat_ref, ghat_ref, dnode_ref, dqkv_ref, sums_ref, backs_ref, w_ref,
+    vec_ref,
+    node_ref,
 ):
-    width = local_ref.shape[1]
+    width = lhat_ref.shape[1]
     sums = sums_ref[...]
     backs = backs_ref[...]
-    total = norm_back(info_ref, dsum_ref, local_ref, sums, backs, 0, vec_ref[5:6, :], 1)
-    total = total + norm_back(info_ref, dsum_ref, global_ref, sums, backs, 2, vec_ref[7:8, :], 2)
+    total = norm_back(info_ref, dsum_ref, lhat_ref, sums, backs, 0, vec_ref[5:6, :], 1)
+    total = total + norm_back(info_ref, dsum_ref, ghat_ref, sums, backs, 2, vec_ref[7:8, :], 2)
     for place, mat in enumerate((0, 1, 3, 4)):
         total = total + mm_back(dnode_ref[:, place * width : (place + 1) * width], w_ref[mat])
     for place in range(3):
         total = total + mm_back(dqkv_ref[:, place * width : (place + 1) * width], w_ref[5 + place])
     node_ref[...] = total
+
+
+def edge_grad_kernel(info_ref, dedge_ref, w_ref, edge_ref):
     edge_ref[...] = mm_back(dedge_ref[...], w_ref[2])
 
 
@@ -453,7 +540,7 @@
         ),
         out_shape=out_shapes,
         compiler_params=pltpu.CompilerParams(
-            dimension_semantics=("arbitrary",), vmem_limit_bytes=48 * 1024 * 1024
+            dimension_semantics=("arbitrary",), vmem_limit_bytes=12 * 1024 * 1024
         ),
         cost_estimate=cost,
     )(info, *arrays)
@@ -467,33 +554,59 @@
     return [1 << power for power in range(total.bit_length() - 1)]
 
 
-def sum_small(values, total):
+def beside(start, transfer, info, work):
+    info = lax.optimization_barrier((info, start))[0]
+    return lax.optimization_barrier((transfer, work(info)))
+
+
+def sum_small(values, total, info=None, works=()):
+    results = []
+    works = list(works)
     for step in steps_of(total):
-        values = values + swap_with(values, step, total)
-    return values
-
-
-def gather_matrices(shard, total):
+        other = swap_with(values, step, total)
+        if works and step > 1:
+            other, done = beside(values, other, info, works.pop(0))
+            results.append(done)
+        values = values + other
+    return (values, results) if results else values
+
+
+def swap_chips(values, number, total):
+    orders = chip_orders(total)
+    return lax.ppermute(
+        values,
+        axis_names,
+        [(place, place ^ orders[place % 2][number]) for place in range(total)],
+    )
+
+
+def in_rows(total, width):
+    return width * width // total == 8 * width
+
+
+def gather_matrices(shard, info, total, width):
+    mats = shard.shape[0]
+    if not in_rows(total, width):
+        gathered = lax.all_gather(shard, axis_names, axis=1, tiled=True)
+        return gathered.reshape(mats, width, width)
+    held = shard.reshape(1, mats * 8, width)
+    for number in reversed(range(len(chip_orders(total)[0]))):
+        held = jnp.concatenate([held, swap_chips(held, number, total)], axis=0)
+    other = swap_with(held, 1, total)
+    return call(
+        assemble_kernel,
+        1,
+        info,
+        [(held, None), (other, None)],
+        [((mats, width, width), bf16, None)],
+    )[0]
+
+
+def scatter_plain(grads, total):
     place = lax.axis_index(axis_names)
-    mats, width = shard.shape
-    held = shard[None]
-    for step in reversed(steps_of(total)):
-        other = swap_with(held, step, total)
-        upper = (place & step) != 0
-        held = jnp.concatenate(
-            [jnp.where(upper, other, held), jnp.where(upper, held, other)], axis=0
-        )
+    mats, width, _ = grads.shape
     bits = total.bit_length() - 1
-    held = held.reshape((2,) * bits + (mats, width))
-    held = held.transpose((bits,) + tuple(reversed(range(bits))) + (bits + 1,))
-    return held.reshape(mats, total * width)
-
-
-def scatter_sum(grads, total):
-    place = lax.axis_index(axis_names)
-    mats, width = grads.shape
-    bits = total.bit_length() - 1
-    held = grads.reshape((mats,) + (2,) * bits + (width // total,))
+    held = grads.reshape((mats,) + (2,) * bits + (width * width // total,))
     held = held.transpose(tuple(reversed(range(1, bits + 1))) + (0, bits + 1))
     for step in steps_of(total):
         mine = ((place & step) != 0).astype(jnp.int32)
@@ -503,6 +616,20 @@
         if step * 2 < total:
             held = low(held)
     return held
+
+
+def scatter_packed(kept, sent, total, info, works):
+    got = swap_with(sent, 1, total)
+    results = []
+    for number in range(len(chip_orders(total)[0])):
+        half = kept.shape[0] // 2
+        sent = low(kept[half:].astype(f32) + got[half:].astype(f32))
+        kept = kept[:half].astype(f32) + got[:half].astype(f32)
+        got = swap_chips(sent, number, total)
+        if number < len(works):
+            got, done = beside(sent, got, info, works[number])
+            results.append(done)
+    return ((kept + got.astype(f32)).reshape(-1, 8 * kept.shape[-1]), results)
 
 
 def adamw(params, gradient, moment_one, moment_two, rate, decay):
@@ -546,9 +673,11 @@
     tall = group * BLOCK
     tall_edges = group * EB
     w_bf = low(weights)
-    matrices = gather_matrices(w_bf, total).reshape(MATS, width, width)
     counts = jnp.sum(own_half(node_mask, branch_index).reshape(blocks, BLOCK), axis=1)
-    info = jnp.concatenate([(branch_index * steps)[None], counts]).astype(jnp.int32)
+    info = jnp.concatenate(
+        [(branch_index * steps)[None], counts, branch_index[None], lax.axis_index("rows")[None]]
+    ).astype(jnp.int32)
+    matrices = gather_matrices(w_bf, info, total, width)
 
     def by_step(values, slots):
         return own_half(values, branch_index).reshape(steps, group, slots)
@@ -581,17 +710,18 @@
     node_f32 = ((rows, width), f32, node_spec)
     node_bf = ((rows, width), bf16, node_spec)
     sums_out = ((8, width), f32, None)
-    local_out, gated, recip, ratio, opened, b_source, local_sums = call(
+    local_out, gate_slope, recip, fall, opened, bend, b_source, local_sums = call(
         local_kernel,
         steps,
         info,
         [x_in, e_in, (hot, edge_spec), (turned, edge_spec), mats_in, vec_in],
         [
             node_f32,
-            node_f32,
-            node_f32,
-            node_f32,
-            ((edges, width), f32, edge_spec),
+            node_bf,
+            node_bf,
+            node_bf,
+            ((edges, width), bf16, edge_spec),
+            ((edges, width), bf16, edge_spec),
             ((edges, width), bf16, edge_spec),
             sums_out,
         ],
@@ -622,24 +752,32 @@
     sums_in = (sums, None)
     cot_in = (cotangent, node_spec)
     wide_spec = rows_spec(tall, 2 * width)
-    summed_low, hidden, mixed, top_part = call(
+    summed_low, hidden_low, hidden_slope, local_hat, global_hat, mixed, top_part = call(
         mix_kernel,
         steps,
         info,
         [(local_out, node_spec), (global_out, node_spec), cot_in, sums_in, mats_in, vec_in],
-        [node_bf, ((rows, 2 * width), f32, wide_spec), node_f32, sums_out],
+        [
+            node_bf,
+            ((rows, 2 * width), bf16, wide_spec),
+            ((rows, 2 * width), bf16, wide_spec),
+            node_bf,
+            node_bf,
+            node_f32,
+            sums_out,
+        ],
     )
     tops = sum_small(top_part, total)
-    layer_out, d_mixed, d_hidden, hidden_low, d_summed, back_part = call(
+    layer_out, d_mixed, d_hidden, d_summed, back_part = call(
         mix_back_kernel,
         steps,
         info,
         [
             (mixed, node_spec),
-            (hidden, wide_spec),
+            (hidden_slope, wide_spec),
             cot_in,
-            (local_out, node_spec),
-            (global_out, node_spec),
+            (local_hat, node_spec),
+            (global_hat, node_spec),
             sums_in,
             (tops, None),
             mats_in,
@@ -649,32 +787,38 @@
             node_bf,
             node_bf,
             ((rows, 2 * width), bf16, wide_spec),
-            ((rows, 2 * width), bf16, wide_spec),
             node_bf,
             sums_out,
         ],
     )
-    backs = sum_small(back_part, total)
 
     def mat_out(number):
-        return ((number, width, width), bf16, None)
+        return ((number, width, width), f32, None)
 
     def mat_acc(number):
         return pltpu.VMEM((number, width, width), f32)
 
-    mix_grads = call(
-        lambda info_ref, *refs: mix_grad_kernel(*refs),
-        steps,
-        info,
-        [
-            (summed_low, node_spec),
-            (d_hidden, wide_spec),
-            (hidden_low, wide_spec),
-            (d_mixed, node_spec),
-        ],
-        [mat_out(4)],
-        [mat_acc(4)],
-    )[0]
+    def inner_work(info):
+        return call(
+            inner_grad_kernel,
+            steps,
+            info,
+            [(summed_low, node_spec), (d_hidden, wide_spec)],
+            [mat_out(2)],
+            [mat_acc(2)],
+        )[0]
+
+    def outer_work(info):
+        return call(
+            outer_grad_kernel,
+            steps,
+            info,
+            [(hidden_low, wide_spec), (d_mixed, node_spec)],
+            [mat_out(2)],
+            [mat_acc(2)],
+        )[0]
+
+    backs, (inner_grads, outer_grads) = sum_small(back_part, total, info, [inner_work, outer_work])
     backs_in = (backs, None)
     dsum_in = (d_summed, node_spec)
     dnode_spec = rows_spec(tall, 4 * width)
@@ -684,11 +828,12 @@
         info,
         [
             dsum_in,
-            (local_out, node_spec),
-            (gated, node_spec),
+            (local_hat, node_spec),
+            (gate_slope, node_spec),
             (recip, node_spec),
-            (ratio, node_spec),
+            (fall, node_spec),
             (opened, edge_spec),
+            (bend, edge_spec),
             (b_source, edge_spec),
             (hot, edge_spec),
             (turned, edge_spec),
@@ -707,13 +852,18 @@
         [mat_acc(5)],
     )
     dqkv_spec = rows_spec(tall, 3 * width)
-    d_qkv, attend_bias, attend_grads = call(
+    slots = total // 2
+    packed = in_rows(total, width)
+    grad_outs = [((MATS, width, width), bf16, None)]
+    if packed:
+        grad_outs = [((slots, MATS * 8, width), bf16, None)] * 2
+    d_qkv, attend_bias, *grads = call(
         attend_back_kernel,
         steps,
         info,
         [
             dsum_in,
-            (global_out, node_spec),
+            (global_hat, node_spec),
             (attended, node_spec),
             (queries, node_spec),
             (keyed, node_spec),
@@ -724,30 +874,48 @@
             backs_in,
             mats_in,
             vec_in,
-        ],
-        [((rows, 3 * width), bf16, dqkv_spec), sums_out, mat_out(4)],
+            (local_grads, None),
+            (inner_grads, None),
+            (outer_grads, None),
+        ],
+        [((rows, 3 * width), bf16, dqkv_spec), sums_out] + grad_outs,
         [mat_acc(4)],
     )
-    all_grads = jnp.concatenate([local_grads, attend_grads, mix_grads], axis=0)
-    grad_shard = scatter_sum(all_grads.reshape(MATS, width * width), total)
-    node_grad, edge_grad = call(
-        input_grad_kernel,
-        steps,
-        info,
-        [
-            dsum_in,
-            (local_out, node_spec),
-            (global_out, node_spec),
-            (d_node, dnode_spec),
-            (d_qkv, dqkv_spec),
-            (d_edge, edge_spec),
-            sums_in,
-            backs_in,
-            mats_in,
-            vec_in,
-        ],
-        [node_f32, ((edges, width), f32, edge_spec)],
-    )
+    def node_work(info):
+        return call(
+            node_grad_kernel,
+            steps,
+            info,
+            [
+                dsum_in,
+                (local_hat, node_spec),
+                (global_hat, node_spec),
+                (d_node, dnode_spec),
+                (d_qkv, dqkv_spec),
+                sums_in,
+                backs_in,
+                mats_in,
+                vec_in,
+            ],
+            [node_f32],
+        )[0]
+
+    def edge_work(info):
+        return call(
+            edge_grad_kernel,
+            steps,
+            info,
+            [(d_edge, edge_spec), mats_in],
+            [((edges, width), f32, edge_spec)],
+        )[0]
+
+    if packed:
+        grad_shard, (node_grad, edge_grad) = scatter_packed(
+            *grads, total, info, [node_work, edge_work]
+        )
+    else:
+        grad_shard = scatter_plain(grads[0], total)
+        node_grad, edge_grad = node_work(info), edge_work(info)
     square_row = jnp.broadcast_to(jnp.sum(grad_shard * grad_shard), (1, width))
     tail = sum_small(
         jnp.concatenate(

time: 273 us -> 188 us (0.69)
  local copies, waits for them, and re-layouts: 37.1 us -> 3.14 us
  Pallas kernels: 86.8 us -> 65.6 us
  waiting for transfers between devices: 86.7 us -> 71.4 us
  other arithmetic: 16.3 us -> 5.26 us
  starting transfers between devices: 41 us -> 37.8 us
    ppermute x30 -> x22, waiting for transfers between devices: 86.7 us -> 42.4 us  [swap_with(): lax.ppermute(values, axis_names, [(place, place ^ step) for place in rang...]
    ppermute x0 -> x8, waiting for transfers between devices: none -> 28.9 us  [swap_chips(): lax.ppermute(values, axis_names, [(place, place ^ orders[place % 2][numbe...]
    pallas_call x9 -> x12, Pallas kernels: 86.8 us -> 65.6 us  [call(): pl.pallas_call(kernel, grid_spec=pltpu.PrefetchScalarGridSpec(num_scalar_...]
    ppermute x30 -> x22, starting transfers between devices: 41 us -> 23.3 us  [swap_with(): lax.ppermute(values, axis_names, [(place, place ^ step) for place in rang...]
    unnamed x75 -> x38, local copies, waits for them, and re-layouts: 18.9 us -> 1.43 us
    ppermute x0 -> x8, starting transfers between devices: none -> 14.5 us  [swap_chips(): lax.ppermute(values, axis_names, [(place, place ^ orders[place % 2][numbe...]
    another operation x3 -> x0, local copies, waits for them, and re-layouts: 10.7 us -> none
    convert_element_type x4 -> x3, other arithmetic: 7.49 us -> 1 us  [low(): return values.astype(bf16)]
  transfers between devices with their start and end apart: 30 -> 30, of which waited for: 27 -> 27; matrix products, arithmetic and copies ran while one was open for 0% -> 1% of each run, Pallas kernels for 6% -> 7%
where the time goes in v1:
time: 188 us; the launch traced here: 187 us
  waiting for transfers between devices  71.4 us (38%)
  Pallas kernels  65.6 us (35%)
  starting transfers between devices  37.8 us (20%)
  other arithmetic  5.26 us (3%)
  between operations  4.32 us (2%)
  local copies, waits for them, and re-layouts  3.14 us (2%)
    pallas_call x12, Pallas kernels, call(): pl.pallas_call(kernel, grid_spec=pltpu.PrefetchScalarGridSpec(num_scalar_...  65.6 us
    ppermute x22, waiting for transfers between devices, swap_with(): lax.ppermute(values, axis_names, [(place, place ^ step) for place in rang...  42.4 us
    ppermute x8, waiting for transfers between devices, swap_chips(): lax.ppermute(values, axis_names, [(place, place ^ orders[place % 2][numbe...  28.9 us
    ppermute x22, starting transfers between devices, swap_with(): lax.ppermute(values, axis_names, [(place, place ^ step) for place in rang...  23.3 us
    ppermute x8, starting transfers between devices, swap_chips(): lax.ppermute(values, axis_names, [(place, place ^ orders[place % 2][numbe...  14.5 us
  transfers between devices with their start and end apart: 30, of which 27 were waited for; matrix products, arithmetic and copies ran while one was open for 1% of the time, Pallas kernels for 7%

profile of v1, /device:TPU:0, one launch (start us, length us, event | category | flops | bytes accessed | tf_op | source)
XLA Modules:
  0.0 187.4 jit_solution(9335903803912108547)
XLA Ops:
  1.7 4.1 %collective-permute-start = (bf16[1,104,256]{2,1,0:T(8,128)(2,1)S(1)}, bf16[1,104,256]{2,1,0:T(8,128)(2,1)S(1)}, u32[]{:S(2)}, u32[]{:S(2)}) collective-permute-start(bf16[1,104,256]{2,1,0:T(8,128)(2,1)S(1)} %reshape.46), channel_id=1, source_target_pairs={{0,16},{1,17},{2,18},{3,19},{4,20},{5,21},{6,22},{7,23},{8,24},{9,... | collective-permute-start | bytes 159752 | tf_op jit(solution)/shard_map/ppermute | solution.py:576
  5.8 2.7 %collective-permute-done = bf16[1,104,256]{2,1,0:T(8,128)(2,1)S(1)} collective-permute-done((bf16[1,104,256]{2,1,0:T(8,128)(2,1)S(1)}, bf16[1,104,256]{2,1,0:T(8,128)(2,1)S(1)}, u32[]{:S(2)}, u32[]{:S(2)}) %collective-permute-start) | collective-permute-done | bytes 53280 | tf_op jit(solution)/shard_map/ppermute | solution.py:576
  9.9 3.4 %collective-permute-done.1 = bf16[2,104,256]{2,1,0:T(8,128)(2,1)S(1)} collective-permute-done((bf16[2,104,256]{2,1,0:T(8,128)(2,1)S(1)}, bf16[2,104,256]{2,1,0:T(8,128)(2,1)S(1)}, u32[]{:S(2)}, u32[]{:S(2)}) %collective-permute-start.1) | collective-permute-done | bytes 106528 | tf_op jit(solution)/shard_map/ppermute | solution.py:576
  15.4 5.1 %collective-permute-done.2 = bf16[4,104,256]{2,1,0:T(8,128)(2,1)S(1)} collective-permute-done((bf16[4,104,256]{2,1,0:T(8,128)(2,1)S(1)}, bf16[4,104,256]{2,1,0:T(8,128)(2,1)S(1)}, u32[]{:S(2)}, u32[]{:S(2)}) %collective-permute-start.2) | collective-permute-done | bytes 213024 | tf_op jit(solution)/shard_map/ppermute | solution.py:576
  22.8 6.0 %collective-permute-done.3 = bf16[8,104,256]{2,1,0:T(8,128)(2,1)S(1)} collective-permute-done((bf16[8,104,256]{2,1,0:T(8,128)(2,1)S(1)}, bf16[8,104,256]{2,1,0:T(8,128)(2,1)S(1)}, u32[]{:S(2)}, u32[]{:S(2)}) %collective-permute-start.3) | collective-permute-done | bytes 426016 | tf_op jit(solution)/shard_map/ppermute | solution.py:576
  34.4 10.0 %shard_map.216 = (f32[2048,256]{1,0:T(8,128)S(1)}, bf16[2048,256]{1,0:T(8,128)(2,1)S(1)}, bf16[2048,256]{1,0:T(8,128)(2,1)S(1)}, bf16[2048,256]{1,0:T(8,128)(2,1...) custom-call(s32[19]{0:T(128)S(1)} %pad_add_fusion.info_ref, ...), custom_call_target="tpu_custom_call" | custom-call | tf_op jit(solution)/shard_map/pallas_call | solution.py:532
  44.4 8.5 %shard_map.215 = (f32[2048,256]{1,0:T(8,128)S(1)}, bf16[2048,256]{1,0:T(8,128)(2,1)S(1)}, bf16[2048,256]{1,0:T(8,128)(2,1)S(1)}, bf16[2048,256]{1,0:T(8,128)(2,1...) custom-call(s32[19]{0:T(128)S(1)} %pad_add_fusion.info_ref, ...), custom_call_target="tpu_custom_call" | custom-call | tf_op jit(solution)/shard_map/pallas_call | solution.py:532
  63.7 2.9 %collective-permute-done.8 = f32[8,256]{1,0:T(8,128)S(1)} collective-permute-done((f32[8,256]{1,0:T(8,128)S(1)}, f32[8,256]{1,0:T(8,128)S(1)}, u32[]{:S(2)}, u32[]{:S(2)}) %collective-permute-start.8) | collective-permute-done | bytes 8224 | tf_op jit(solution)/shard_map/ppermute | solution.py:550
  68.5 2.7 %collective-permute-done.9 = f32[8,256]{1,0:T(8,128)S(1)} collective-permute-done((f32[8,256]{1,0:T(8,128)S(1)}, f32[8,256]{1,0:T(8,128)S(1)}, u32[]{:S(2)}, u32[]{:S(2)}) %collective-permute-start.9) | collective-permute-done | bytes 8224 | tf_op jit(solution)/shard_map/ppermute | solution.py:550
  71.2 4.3 %shard_map.217 = (bf16[2048,256]{1,0:T(8,128)(2,1)S(1)}, bf16[2048,512]{1,0:T(8,128)(2,1)S(1)}, bf16[2048,512]{1,0:T(8,128)(2,1)S(1)}, bf16[2048,256]{1,0:T(8,12...) custom-call(s32[19]{0:T(128)S(1)} %pad_add_fusion.info_ref, ...), custom_call_target="tpu_custom_call" | custom-call | tf_op jit(solution)/shard_map/pallas_call | solution.py:532
  85.0 2.7 %collective-permute-done.13 = f32[8,256]{1,0:T(8,128)S(1)} collective-permute-done((f32[8,256]{1,0:T(8,128)S(1)}, f32[8,256]{1,0:T(8,128)S(1)}, u32[]{:S(2)}, u32[]{:S(2)}) %collective-permute-start.13) | collective-permute-done | bytes 8224 | tf_op jit(solution)/shard_map/ppermute | solution.py:550
  89.6 2.7 %collective-permute-done.14 = f32[8,256]{1,0:T(8,128)S(1)} collective-permute-done((f32[8,256]{1,0:T(8,128)S(1)}, f32[8,256]{1,0:T(8,128)S(1)}, u32[]{:S(2)}, u32[]{:S(2)}) %collective-permute-start.14) | collective-permute-done | bytes 8224 | tf_op jit(solution)/shard_map/ppermute | solution.py:550
  92.3 4.4 %shard_map.218 = (bf16[2048,256]{1,0:T(8,128)(2,1)}, bf16[2048,256]{1,0:T(8,128)(2,1)S(1)}, bf16[2048,512]{1,0:T(8,128)(2,1)S(1)}, bf16[2048,256]{1,0:T(8,128)(2,1)S(1)}, f32[8,256]{1,0:T(8,128)S(1)}) custom-call(s32[19]{0:T(128)S(1)} %pad_add_fusion.info_ref, f32[2048,256]{1,0:T(8,128)S(1)} %get-tuple-element.67.mixed_ref, ...), custom_call_target="tpu_custom_call" | custom-call | tf_op jit(solution)/shard_map/pallas_call | solution.py:532
  106.4 3.2 %collective-permute-done.18 = f32[8,256]{1,0:T(8,128)S(1)} collective-permute-done((f32[8,256]{1,0:T(8,128)S(1)}, f32[8,256]{1,0:T(8,128)S(1)}, u32[]{:S(2)}, u32[]{:S(2)}) %collective-permute-start.18) | collective-permute-done | bytes 8224 | tf_op jit(solution)/shard_map/ppermute | solution.py:550
  110.9 3.2 %collective-permute-done.19 = f32[8,256]{1,0:T(8,128)S(1)} collective-permute-done((f32[8,256]{1,0:T(8,128)S(1)}, f32[8,256]{1,0:T(8,128)S(1)}, u32[]{:S(2)}, u32[]{:S(2)}) %collective-permute-start.19) | collective-permute-done | bytes 8224 | tf_op jit(solution)/shard_map/ppermute | solution.py:550
  114.1 9.2 %shard_map.221 = (bf16[2048,1024]{1,0:T(8,128)(2,1)S(1)}, bf16[4096,256]{1,0:T(8,128)(2,1)S(1)}, f32[8,256]{1,0:T(8,128)S(1)}, f32[5,256,256]{2,1,0:T(8,128)S(1)}) custom-call(s32[19]{0:T(128)S(1)} %pad_add_fusion.info_ref, bf16[2048,256]{1,0:T(8,128)(2,1)S(1)} %get-tuple-element.73.dsum_ref, bf16[2048,256]{1,0:T(8,128)(2,1)S(1)} %get-tuple-element.69.lhat_ref.local_ref, ...), custom_call_target="tpu_custom_call" | custom-call | tf_op jit(solution)/shard_map/pallas_call | solution.py:532
  123.3 13.4 %shard_map.222 = (bf16[2048,768]{1,0:T(8,128)(2,1)S(1)}, f32[8,256]{1,0:T(8,128)S(1)}, bf16[16,104,256]{2,1,0:T(8,128)(2,1)S(1)}, bf16[16,104,256]{2,1,0:T(8,128)(2,1)S(1)}) custom-call(s32[19]{0:T(128)S(1)} %pad_add_fusion.info_ref, bf16[2048,256]{1,0:T(8,128)(2,1)S(1)} %get-tuple-element.73.dsum_ref, ...), custom_call_target="tpu_custom_call" | custom-call | tf_op jit(solution)/shard_map/pallas_call | solution.py:532
  140.8 4.3 %shard_map.223 = f32[2048,256]{1,0:T(8,128)} custom-call(s32[19]{0:T(128)S(1)} %pad_add_fusion.info_ref, bf16[2048,256]{1,0:T(8,128)(2,1)S(1)} %get-tuple-element.73.dsum_ref, bf16[2048,256]{1,0:T(8,128)(2,1)S(1)} %get-tuple-element.69.lhat_ref.local_ref, bf16[2048,256]{1,0:T(8,128)(2,1)S(1)} %get-tuple-element.70.ghat_ref.global_ref, ...), custom_call_target="tpu_custom_call" | custom-call | tf_op jit(solution)/shard_map/pallas_call | solution.py:532
  145.2 2.4 %collective-permute-done.21 = bf16[8,104,256]{2,1,0:T(8,128)(2,1)S(1)} collective-permute-done((bf16[8,104,256]{2,1,0:T(8,128)(2,1)S(1)}, bf16[8,104,256]{2,1,0:T(8,128)(2,1)S(1)}, u32[]{:S(2)}, u32[]{:S(2)}) %collective-permute-start.21) | collective-permute-done | bytes 426016 | tf_op jit(solution)/shard_map/ppermute | solution.py:576
  149.1 3.5 %shard_map.224 = f32[4096,256]{1,0:T(8,128)} custom-call(s32[19]{0:T(128)S(1)} %pad_add_fusion.info_ref, bf16[4096,256]{1,0:T(8,128)(2,1)S(1)} %get-tuple-element.105.dedge_ref, bf16[13,256,256]{2,1,0:T(8,128)(2,1)S(1)} %shard_map.214.w_ref), custom_call_target="tpu_custom_call" | custom-call | tf_op jit(solution)/shard_map/pallas_call | solution.py:532
  154.2 4.2 %collective-permute-done.23 = bf16[2,104,256]{2,1,0:T(8,128)(2,1)S(1)} collective-permute-done((bf16[2,104,256]{2,1,0:T(8,128)(2,1)S(1)}, bf16[2,104,256]{2,1,0:T(8,128)(2,1)S(1)}, u32[]{:S(2)}, u32[]{:S(2)}) %collective-permute-start.23) | collective-permute-done | bytes 106528 | tf_op jit(solution)/shard_map/ppermute | solution.py:576
  159.9 4.1 %collective-permute-done.24 = bf16[1,104,256]{2,1,0:T(8,128)(2,1)S(1)} collective-permute-done((bf16[1,104,256]{2,1,0:T(8,128)(2,1)S(1)}, bf16[1,104,256]{2,1,0:T(8,128)(2,1)S(1)}, u32[]{:S(2)}, u32[]{:S(2)}) %collective-permute-start.24) | collective-permute-done | bytes 53280 | tf_op jit(solution)/shard_map/ppermute | solution.py:576
  174.0 3.6 %collective-permute-done.28 = f32[8,256]{1,0:T(8,128)S(1)} collective-permute-done((f32[8,256]{1,0:T(8,128)S(1)}, f32[8,256]{1,0:T(8,128)S(1)}, u32[]{:S(2)}, u32[]{:S(2)}) %collective-permute-start.28) | collective-permute-done | bytes 8224 | tf_op jit(solution)/shard_map/ppermute | solution.py:550
  178.6 3.6 %collective-permute-done.29 = f32[8,256]{1,0:T(8,128)S(1)} collective-permute-done((f32[8,256]{1,0:T(8,128)S(1)}, f32[8,256]{1,0:T(8,128)S(1)}, u32[]{:S(2)}, u32[]{:S(2)}) %collective-permute-start.29) | collective-permute-done | bytes 8224 | tf_op jit(solution)/shard_map/ppermute | solution.py:550
  (149 shorter events, 68.9 us)
Async XLA Ops:
  1.7 6.8 %collective-permute-start = (bf16[1,104,256]{2,1,0:T(8,128)(2,1)S(1)}, bf16[1,104,256]{2,1,0:T(8,128)(2,1)S(1)}, u32[]{:S(2)}, u32[]{:S(2)}) collective-permute-start(bf16[1,104,256]{2,1,0:T(8,128)(2,1)S(1)} %reshape.46), channel_id=1, source_target_pairs={{0,16},{1,17},{2,18},{3,19},{4,20},{5,21},{6,22},{7,23},{8,24},{9,... | collective-permute-start | bytes 159752 | tf_op jit(solution)/shard_map/ppermute | solution.py:576
  8.5 4.8 %collective-permute-start.1 = (bf16[2,104,256]{2,1,0:T(8,128)(2,1)S(1)}, bf16[2,104,256]{2,1,0:T(8,128)(2,1)S(1)}, u32[]{:S(2)}, u32[]{:S(2)}) collective-permute-start(bf16[2,104,256]{2,1,0:T(8,128)(2,1)S(1)} %pad_maximum_fusion.2), channel_id=1, source_target_pairs={{0,8},{1,3},{2,10},{3,1},{4,12},{5,7},{6,14},{7,5},{8,0},{9,11},{1... | collective-permute-start | bytes 319496 | tf_op jit(solution)/shard_map/ppermute | solution.py:576
  13.4 7.1 %collective-permute-start.2 = (bf16[4,104,256]{2,1,0:T(8,128)(2,1)S(1)}, bf16[4,104,256]{2,1,0:T(8,128)(2,1)S(1)}, u32[]{:S(2)}, u32[]{:S(2)}) collective-permute-start(bf16[4,104,256]{2,1,0:T(8,128)(2,1)S(1)} %pad_maximum_fusion.1), channel_id=1, source_target_pairs={{0,4},{1,9},{2,6},{3,11},{4,0},{5,13},{6,2},{7,15},{8,12},{9,1},{1... | collective-permute-start | bytes 638984 | tf_op jit(solution)/shard_map/ppermute | solution.py:576
  20.5 8.3 %collective-permute-start.3 = (bf16[8,104,256]{2,1,0:T(8,128)(2,1)S(1)}, bf16[8,104,256]{2,1,0:T(8,128)(2,1)S(1)}, u32[]{:S(2)}, u32[]{:S(2)}) collective-permute-start(bf16[8,104,256]{2,1,0:T(8,128)(2,1)S(1)} %pad_maximum_fusion), channel_id=1, source_target_pairs={{0,2},{1,5},{2,0},{3,7},{4,6},{5,1},{6,4},{7,3},{8,10},{9,13},{10,... | collective-permute-start | bytes 1277960 | tf_op jit(solution)/shard_map/ppermute | solution.py:576
  28.8 3.7 %collective-permute-start.4 = (bf16[16,104,256]{2,1,0:T(8,128)(2,1)S(1)}, bf16[16,104,256]{2,1,0:T(8,128)(2,1)}, u32[]{:S(2)}, u32[]{:S(2)}) collective-permute-start(bf16[16,104,256]{2,1,0:T(8,128)(2,1)S(1)} %constant_dynamic-update-slice_fusion.held_ref), channel_id=1, source_target_pairs={{0,1},{1,0},{2,3},{3,2},{4,5},{5,4},{6,7},{7,6},{8,9},{9,8},{10,11... | collective-permute-start | bytes 2555912 | tf_op jit(solution)/shard_map/ppermute | solution.py:550
  55.7 3.7 %collective-permute-start.6 = (f32[8,256]{1,0:T(8,128)S(1)}, f32[8,256]{1,0:T(8,128)S(1)}, u32[]{:S(2)}, u32[]{:S(2)}) collective-permute-start(f32[8,256]{1,0:T(8,128)S(1)} %fusion.8), channel_id=1, source_target_pairs={{0,2},{1,3},{2,0},{3,1},{4,6},{5,7},{6,4},{7,5},{8,10},{9,11},{10,... | collective-permute-start | bytes 24584 | tf_op jit(solution)/shard_map/ppermute | solution.py:550
  59.3 3.7 %collective-permute-start.7 = (f32[8,256]{1,0:T(8,128)S(1)}, f32[8,256]{1,0:T(8,128)S(1)}, u32[]{:S(2)}, u32[]{:S(2)}) collective-permute-start(f32[8,256]{1,0:T(8,128)S(1)} %add.141), channel_id=1, source_target_pairs={{0,4},{1,5},{2,6},{3,7},{4,0},{5,1},{6,2},{7,3},{8,12},{9,13},{10,... | collective-permute-start | bytes 24584 | tf_op jit(solution)/shard_map/ppermute | solution.py:550
  63.0 3.7 %collective-permute-start.8 = (f32[8,256]{1,0:T(8,128)S(1)}, f32[8,256]{1,0:T(8,128)S(1)}, u32[]{:S(2)}, u32[]{:S(2)}) collective-permute-start(f32[8,256]{1,0:T(8,128)S(1)} %add.142), channel_id=1, source_target_pairs={{0,8},{1,9},{2,10},{3,11},{4,12},{5,13},{6,14},{7,15},{8,0},{9,1},... | collective-permute-start | bytes 24584 | tf_op jit(solution)/shard_map/ppermute | solution.py:550
  66.7 4.5 %collective-permute-start.9 = (f32[8,256]{1,0:T(8,128)S(1)}, f32[8,256]{1,0:T(8,128)S(1)}, u32[]{:S(2)}, u32[]{:S(2)}) collective-permute-start(f32[8,256]{1,0:T(8,128)S(1)} %add.143), channel_id=1, source_target_pairs={{0,16},{1,17},{2,18},{3,19},{4,20},{5,21},{6,22},{7,23},{8,24},{9,... | collective-permute-start | bytes 24584 | tf_op jit(solution)/shard_map/ppermute | solution.py:550
  76.7 3.7 %collective-permute-start.11 = (f32[8,256]{1,0:T(8,128)S(1)}, f32[8,256]{1,0:T(8,128)S(1)}, u32[]{:S(2)}, u32[]{:S(2)}) collective-permute-start(f32[8,256]{1,0:T(8,128)S(1)} %add.145), channel_id=1, source_target_pairs={{0,2},{1,3},{2,0},{3,1},{4,6},{5,7},{6,4},{7,5},{8,10},{9,11},{10,... | collective-permute-start | bytes 24584 | tf_op jit(solution)/shard_map/ppermute | solution.py:550
  80.4 3.7 %collective-permute-start.12 = (f32[8,256]{1,0:T(8,128)S(1)}, f32[8,256]{1,0:T(8,128)S(1)}, u32[]{:S(2)}, u32[]{:S(2)}) collective-permute-start(f32[8,256]{1,0:T(8,128)S(1)} %add.146), channel_id=1, source_target_pairs={{0,4},{1,5},{2,6},{3,7},{4,0},{5,1},{6,2},{7,3},{8,12},{9,13},{10,... | collective-permute-start | bytes 24584 | tf_op jit(solution)/shard_map/ppermute | solution.py:550
  87.7 4.5 %collective-permute-start.14 = (f32[8,256]{1,0:T(8,128)S(1)}, f32[8,256]{1,0:T(8,128)S(1)}, u32[]{:S(2)}, u32[]{:S(2)}) collective-permute-start(f32[8,256]{1,0:T(8,128)S(1)} %add.148), channel_id=1, source_target_pairs={{0,16},{1,17},{2,18},{3,19},{4,20},{5,21},{6,22},{7,23},{8,24},{9,... | collective-permute-start | bytes 24584 | tf_op jit(solution)/shard_map/ppermute | solution.py:550
  97.8 4.1 %collective-permute-start.16 = (f32[8,256]{1,0:T(8,128)S(1)}, f32[8,256]{1,0:T(8,128)S(1)}, u32[]{:S(2)}, u32[]{:S(2)}) collective-permute-start(f32[8,256]{1,0:T(8,128)S(1)} %add.150), channel_id=1, source_target_pairs={{0,2},{1,3},{2,0},{3,1},{4,6},{5,7},{6,4},{7,5},{8,10},{9,11},{10,... | collective-permute-start | bytes 24584 | tf_op jit(solution)/shard_map/ppermute | solution.py:550
  102.0 3.8 %collective-permute-start.17 = (f32[8,256]{1,0:T(8,128)S(1)}, f32[8,256]{1,0:T(8,128)S(1)}, u32[]{:S(2)}, u32[]{:S(2)}) collective-permute-start(f32[8,256]{1,0:T(8,128)S(1)} %add.151), channel_id=1, source_target_pairs={{0,4},{1,5},{2,6},{3,7},{4,0},{5,1},{6,2},{7,3},{8,12},{9,13},{10,... | collective-permute-start | bytes 24584 | tf_op jit(solution)/shard_map/ppermute | solution.py:550
  105.8 3.7 %collective-permute-start.18 = (f32[8,256]{1,0:T(8,128)S(1)}, f32[8,256]{1,0:T(8,128)S(1)}, u32[]{:S(2)}, u32[]{:S(2)}) collective-permute-start(f32[8,256]{1,0:T(8,128)S(1)} %add.152), channel_id=1, source_target_pairs={{0,8},{1,9},{2,10},{3,11},{4,12},{5,13},{6,14},{7,15},{8,0},{9,1},... | collective-permute-start | bytes 24584 | tf_op jit(solution)/shard_map/ppermute | solution.py:550
  109.5 4.5 %collective-permute-start.19 = (f32[8,256]{1,0:T(8,128)S(1)}, f32[8,256]{1,0:T(8,128)S(1)}, u32[]{:S(2)}, u32[]{:S(2)}) collective-permute-start(f32[8,256]{1,0:T(8,128)S(1)} %add.153), channel_id=1, source_target_pairs={{0,16},{1,17},{2,18},{3,19},{4,20},{5,21},{6,22},{7,23},{8,24},{9,... | collective-permute-start | bytes 24584 | tf_op jit(solution)/shard_map/ppermute | solution.py:550
  139.4 8.2 %collective-permute-start.21 = (bf16[8,104,256]{2,1,0:T(8,128)(2,1)S(1)}, bf16[8,104,256]{2,1,0:T(8,128)(2,1)S(1)}, u32[]{:S(2)}, u32[]{:S(2)}) collective-permute-start(bf16[8,104,256]{2,1,0:T(8,128)(2,1)S(1)} %get-tuple-element.117), channel_id=1, source_target_pairs={{0,2},{1,5},{2,0},{3,7},{4,6},{5,1},{6,4},{7,3},{8,10},{9,13},{10,... | collective-permute-start | bytes 1277960 | tf_op jit(solution)/shard_map/ppermute | solution.py:576
  147.7 5.9 %collective-permute-start.22 = (bf16[4,104,256]{2,1,0:T(8,128)(2,1)S(1)}, bf16[4,104,256]{2,1,0:T(8,128)(2,1)S(1)}, u32[]{:S(2)}, u32[]{:S(2)}) collective-permute-start(bf16[4,104,256]{2,1,0:T(8,128)(2,1)S(1)} %get-tuple-element.119), channel_id=1, source_target_pairs={{0,4},{1,9},{2,6},{3,11},{4,0},{5,13},{6,2},{7,15},{8,12},{9,1},{1... | collective-permute-start | bytes 638984 | tf_op jit(solution)/shard_map/ppermute | solution.py:576
  153.6 4.8 %collective-permute-start.23 = (bf16[2,104,256]{2,1,0:T(8,128)(2,1)S(1)}, bf16[2,104,256]{2,1,0:T(8,128)(2,1)S(1)}, u32[]{:S(2)}, u32[]{:S(2)}) collective-permute-start(bf16[2,104,256]{2,1,0:T(8,128)(2,1)S(1)} %get-tuple-element.120), channel_id=1, source_target_pairs={{0,8},{1,3},{2,10},{3,1},{4,12},{5,7},{6,14},{7,5},{8,0},{9,11},{1... | collective-permute-start | bytes 319496 | tf_op jit(solution)/shard_map/ppermute | solution.py:576
  158.4 5.6 %collective-permute-start.24 = (bf16[1,104,256]{2,1,0:T(8,128)(2,1)S(1)}, bf16[1,104,256]{2,1,0:T(8,128)(2,1)S(1)}, u32[]{:S(2)}, u32[]{:S(2)}) collective-permute-start(bf16[1,104,256]{2,1,0:T(8,128)(2,1)S(1)} %fusion.3), channel_id=1, source_target_pairs={{0,16},{1,17},{2,18},{3,19},{4,20},{5,21},{6,22},{7,23},{8,24},{9,... | collective-permute-start | bytes 159752 | tf_op jit(solution)/shard_map/ppermute | solution.py:576
  166.7 3.7 %collective-permute-start.26 = (f32[8,256]{1,0:T(8,128)S(1)}, f32[8,256]{1,0:T(8,128)S(1)}, u32[]{:S(2)}, u32[]{:S(2)}) collective-permute-start(f32[8,256]{1,0:T(8,128)S(1)} %fusion.9), channel_id=1, source_target_pairs={{0,2},{1,3},{2,0},{3,1},{4,6},{5,7},{6,4},{7,5},{8,10},{9,11},{10,... | collective-permute-start | bytes 24584 | tf_op jit(solution)/shard_map/ppermute | solution.py:550
  170.3 3.7 %collective-permute-start.27 = (f32[8,256]{1,0:T(8,128)S(1)}, f32[8,256]{1,0:T(8,128)S(1)}, u32[]{:S(2)}, u32[]{:S(2)}) collective-permute-start(f32[8,256]{1,0:T(8,128)S(1)} %add.165), channel_id=1, source_target_pairs={{0,4},{1,5},{2,6},{3,7},{4,0},{5,1},{6,2},{7,3},{8,12},{9,13},{10,... | collective-permute-start | bytes 24584 | tf_op jit(solution)/shard_map/ppermute | solution.py:550
  174.0 3.7 %collective-permute-start.28 = (f32[8,256]{1,0:T(8,128)S(1)}, f32[8,256]{1,0:T(8,128)S(1)}, u32[]{:S(2)}, u32[]{:S(2)}) collective-permute-start(f32[8,256]{1,0:T(8,128)S(1)} %add.166), channel_id=1, source_target_pairs={{0,8},{1,9},{2,10},{3,11},{4,12},{5,13},{6,14},{7,15},{8,0},{9,1},... | collective-permute-start | bytes 24584 | tf_op jit(solution)/shard_map/ppermute | solution.py:550
  177.6 4.5 %collective-permute-start.29 = (f32[8,256]{1,0:T(8,128)S(1)}, f32[8,256]{1,0:T(8,128)S(1)}, u32[]{:S(2)}, u32[]{:S(2)}) collective-permute-start(f32[8,256]{1,0:T(8,128)S(1)} %add.167), channel_id=1, source_target_pairs={{0,16},{1,17},{2,18},{3,19},{4,20},{5,21},{6,22},{7,23},{8,24},{9,... | collective-permute-start | bytes 24584 | tf_op jit(solution)/shard_map/ppermute | solution.py:550
  (23 other events, 426.5 us)

commit v2 on v1

--- a/solution.py
+++ b/solution.py
@@ -13,7 +13,7 @@
 EB = 256
 MATS = 13
 STEP = 7
-GROUP = 4
+GROUP = 8
 
 eps_norm = 1e-05
 clip_limit = 1.0
@@ -62,6 +62,14 @@
         ],
         axis=0,
     )
+
+
+def nodes_of(place):
+    return slice(place * BLOCK, (place + 1) * BLOCK)
+
+
+def edges_of(place):
+    return slice(place * EB, (place + 1) * EB)
 
 
 def add_rows(out_ref, rows):
@@ -106,23 +114,30 @@
     d_part = low(mm(x, w_ref[3]))
     e_part = low(mm(x, w_ref[4]))
     c_part = mm(e_ref[...], w_ref[2]) + vec_ref[1:2, :]
-    nums = []
-    dens = []
+    gates = []
+    picks = []
     for place in range(group):
-        nodes = slice(place * BLOCK, (place + 1) * BLOCK)
-        edges = slice(place * EB, (place + 1) * EB)
-        hot = hot_ref[edges, :]
-        gate = c_part[edges] + mm(hot, jnp.concatenate([d_part[nodes], e_part[nodes]], axis=0))
-        opened = sig(gate)
-        b_source = mm(hot[:, BLOCK:], b_part[nodes])
-        open_ref[edges, :] = low(opened)
+        nodes = nodes_of(place)
+        hot = hot_ref[edges_of(place), :]
+        gates.append(mm(hot, jnp.concatenate([d_part[nodes], e_part[nodes]], axis=0)))
+        picks.append(mm(hot[:, BLOCK:], b_part[nodes]))
+    sums = []
+    for place in range(group):
+        edges = edges_of(place)
+        opened = sig(c_part[edges] + gates[place])
+        b_source = picks[place]
+        opened_low = low(opened)
+        open_ref[edges, :] = opened_low
         bend_ref[edges, :] = low(opened * (1.0 - opened))
         bsrc_ref[edges, :] = low(b_source)
         dst_turned = turned_ref[place * EB : place * EB + BLOCK, :]
-        nums.append(mm(dst_turned, low(opened * b_source)))
-        dens.append(mm(dst_turned, low(opened)))
-    recip = 1.0 / (jnp.concatenate(dens, axis=0) + 1.0)
-    ratio = jnp.concatenate(nums, axis=0) * recip
+        sums.append(
+            mm(dst_turned, jnp.concatenate([low(opened * b_source), opened_low], axis=1))
+        )
+    both = jnp.concatenate(sums, axis=0)
+    width = x.shape[1]
+    recip = 1.0 / (both[:, width:] + 1.0)
+    ratio = both[:, :width] * recip
     gated = a_part + ratio
     gated_sig = sig(gated)
     out = x.astype(f32) + gated * gated_sig
@@ -135,12 +150,22 @@
     add_rows(sums_ref, [col_sum(kept), col_sum(kept * out)])
 
 
-def head_stack(values):
-    head = lax.broadcasted_iota(jnp.int32, values.shape, 1) // (values.shape[1] // HEADS)
-    wide = values.astype(f32)
-    return jnp.concatenate(
-        [low(jnp.where(head == place, wide, 0.0)) for place in range(HEADS)], axis=0
-    )
+def head_masks(width):
+    head = lax.broadcasted_iota(jnp.int32, (16, width), 1) // (width // HEADS)
+    return [low(jnp.where(head == place, 1.0, 0.0))[:1] for place in range(HEADS)]
+
+
+def head_stack(values, masks):
+    return jnp.concatenate([values * mask for mask in masks], axis=0)
+
+
+def tall_masks(width):
+    head = lax.broadcasted_iota(jnp.int32, (width, BLOCK), 0) // (width // HEADS)
+    return [low(jnp.where(head == place, 1.0, 0.0)) for place in range(HEADS)]
+
+
+def side_stack(turned, masks):
+    return jnp.concatenate([turned * mask for mask in masks], axis=1)
 
 
 def attend_kernel(
@@ -155,23 +180,30 @@
     q_ref[...] = queries
     k_ref[...] = keyed
     v_ref[...] = valued
-    score_scale = (x.shape[1] // HEADS) ** (-0.5)
+    score_scale = (x.shape[1] // HEADS) ** (-0.5) * math.log2(math.e)
+    masks = head_masks(x.shape[1])
+    tall = tall_masks(x.shape[1])
+    queries_turned = queries.T
+    raws = [
+        mm(keyed[nodes_of(place)], side_stack(queries_turned[:, nodes_of(place)], tall))
+        for place in range(group)
+    ]
+    turns = []
     for place in range(group):
-        nodes = slice(place * BLOCK, (place + 1) * BLOCK)
-        raw = mm_back(keyed[nodes], head_stack(queries[nodes]))
+        nodes = nodes_of(place)
         bias = bias_ref[nodes, :]
-        probs = []
         turned = []
         for head in range(HEADS):
-            part = raw[:, head * BLOCK : (head + 1) * BLOCK] + bias
-            part = jnp.exp((part - jnp.max(part, axis=0, keepdims=True)) * score_scale)
-            part = part * (1.0 / jnp.sum(part, axis=0, keepdims=True))
-            probs.append(low(part))
-            turned.append(low(part).T)
-        prob_ref[nodes, :] = jnp.concatenate(probs, axis=1)
-        att_ref[nodes, :] = low(
-            mm(jnp.concatenate(turned, axis=1), head_stack(valued[nodes]))
-        )
+            cols = nodes_of(head)
+            part = raws[place][:, cols] + bias
+            part = jnp.exp2((part - jnp.max(part, axis=0, keepdims=True)) * score_scale)
+            part = low(part * (1.0 / jnp.sum(part, axis=0, keepdims=True)))
+            prob_ref[nodes, cols] = part
+            turned.append(part.T)
+        turns.append(jnp.concatenate(turned, axis=1))
+    for place in range(group):
+        nodes = nodes_of(place)
+        att_ref[nodes, :] = low(mm(turns[place], head_stack(valued[nodes], masks)))
     out = x.astype(f32) + mm(att_ref[...], w_ref[8]) + vec_ref[4:5, :]
     out_ref[...] = out
     live = live_of(info_ref, pl.program_id(0) * group, group, out.shape[1])
@@ -220,7 +252,7 @@
 def mix_back_kernel(
     info_ref, mixed_ref, slope_ref, cot_ref, lhat_ref, ghat_ref, sums_ref, tops_ref, w_ref,
     vec_ref,
-    layer_ref, dmix_ref, dhid_ref, dsum_ref, stat_ref,
+    dmix_ref, dhid_ref, dsum_ref, stat_ref,
 ):
     group = mixed_ref.shape[0] // BLOCK
     width = mixed_ref.shape[1]
@@ -230,7 +262,6 @@
     mean, rstd = norm_terms(tops, 0, count_row)
     live = live_of(info_ref, pl.program_id(0) * group, group, width)
     hat = (mixed_ref[...] - mean) * rstd
-    layer_ref[...] = low(live * (vec_ref[12:13, :] * hat + vec_ref[13:14, :]))
     d_norm = live * cot_ref[...].astype(f32)
     dz_sum = tops[2:3]
     dz_hat = (tops[3:4] - mean * dz_sum) * rstd
@@ -240,12 +271,10 @@
     d_mixed_low = low(d_mixed)
     dmix_ref[...] = d_mixed_low
     d_summed = d_mixed
-    rows = []
     for half in range(2):
         cols = slice(half * width, (half + 1) * width)
         d_hidden = low(mm_back(d_mixed_low, w_ref[11 + half]) * slope_ref[:, cols].astype(f32))
         dhid_ref[:, cols] = d_hidden
-        rows.append(col_sum(d_hidden.astype(f32)))
         d_summed = d_summed + mm_back(d_hidden, w_ref[9 + half])
     d_low = low(d_summed)
     dsum_ref[...] = d_low
@@ -256,50 +285,38 @@
             col_sum(d_sum),
             col_sum(d_sum * lhat_ref[...].astype(f32)),
             col_sum(d_sum * ghat_ref[...].astype(f32)),
-            rows[0],
-            rows[1],
             col_sum(d_mixed),
         ],
     )
 
 
-def accumulate(acc_ref, terms):
+def accumulate(acc_ref, term):
     @pl.when(pl.program_id(0) == 0)
     def _():
         acc_ref[...] = jnp.zeros_like(acc_ref)
 
-    for place, term in enumerate(terms):
-        acc_ref[place] += term
-
-
-def emit(acc_ref, out_ref):
-    @pl.when(pl.program_id(0) == pl.num_programs(0) - 1)
-    def _():
-        out_ref[...] = acc_ref[...]
-
-
-def inner_grad_kernel(info_ref, slow_ref, dhid_ref, out_ref, acc_ref):
-    width = slow_ref.shape[1]
-    accumulate(
-        acc_ref,
-        [
-            mm_rows(slow_ref[...], dhid_ref[:, half * width : (half + 1) * width])
-            for half in range(2)
-        ],
-    )
-    emit(acc_ref, out_ref)
-
-
-def outer_grad_kernel(info_ref, hlow_ref, dmix_ref, out_ref, acc_ref):
-    width = dmix_ref.shape[1]
-    accumulate(
-        acc_ref,
-        [
-            mm_rows(hlow_ref[:, half * width : (half + 1) * width], dmix_ref[...])
-            for half in range(2)
-        ],
-    )
-    emit(acc_ref, out_ref)
+    acc_ref[...] += term
+
+
+def layer_kernel(info_ref, mixed_ref, sums_ref, tops_ref, vec_ref, layer_ref):
+    group = mixed_ref.shape[0] // BLOCK
+    mean, rstd = norm_terms(tops_ref[...], 0, sums_ref[4:5, :])
+    live = live_of(info_ref, pl.program_id(0) * group, group, mixed_ref.shape[1])
+    hat = (mixed_ref[...] - mean) * rstd
+    layer_ref[...] = low(live * (vec_ref[12:13, :] * hat + vec_ref[13:14, :]))
+
+
+def ones_sum(ref, cols):
+    return mm(jnp.ones((8, ref.shape[0]), bf16), ref[:, cols])
+
+
+def inner_grad_kernel(info_ref, slow_ref, dhid_ref, out_ref, bias_ref):
+    accumulate(out_ref, mm_rows(slow_ref[...], dhid_ref[...]))
+    accumulate(bias_ref, ones_sum(dhid_ref, slice(None)))
+
+
+def outer_grad_kernel(info_ref, hlow_ref, dmix_ref, out_ref):
+    accumulate(out_ref, mm_rows(hlow_ref[...], dmix_ref[...]))
 
 
 def norm_back(info_ref, dsum_ref, hat_ref, sums, backs, first, gain_row, hat_row):
@@ -316,8 +333,8 @@
 
 def local_back_kernel(
     info_ref, dsum_ref, local_ref, slope_ref, recip_ref, fall_ref, open_ref, bend_ref, bsrc_ref,
-    hot_ref, turned_ref, x_ref, e_ref, sums_ref, backs_ref, vec_ref,
-    dnode_ref, dedge_ref, stat_ref, out_ref, acc_ref,
+    hot_ref, turned_ref, sums_ref, backs_ref, vec_ref,
+    dnode_ref, dedge_ref, stat_ref,
 ):
     group = local_ref.shape[0] // BLOCK
     width = local_ref.shape[1]
@@ -329,45 +346,37 @@
     d_num = low(d_gated * recip_ref[...].astype(f32))
     d_den = low(-d_gated * fall_ref[...].astype(f32))
     pre_row = jnp.zeros((1, width), f32)
+    picks = [
+        mm(
+            hot_ref[edges_of(place), :BLOCK],
+            jnp.concatenate([d_num[nodes_of(place)], d_den[nodes_of(place)]], axis=1),
+        )
+        for place in range(group)
+    ]
+    sources = []
     for place in range(group):
-        nodes = slice(place * BLOCK, (place + 1) * BLOCK)
-        edges = slice(place * EB, (place + 1) * EB)
-        hot_dst = hot_ref[edges, :BLOCK]
-        d_message = mm(hot_dst, d_num[nodes])
-        opened = open_ref[edges, :].astype(f32)
-        d_open = d_message * bsrc_ref[edges, :].astype(f32) + mm(hot_dst, d_den[nodes])
-        d_source = low(d_message * opened)
+        edges = edges_of(place)
+        d_message = picks[place][:, :width]
+        d_open = d_message * bsrc_ref[edges, :].astype(f32) + picks[place][:, width:]
+        sources.append(low(d_message * open_ref[edges, :].astype(f32)))
         d_pre = d_open * bend_ref[edges, :].astype(f32)
-        d_pre_low = low(d_pre)
         pre_row = pre_row + col_sum(d_pre)
-        dedge_ref[edges, :] = d_pre_low
-        turned = turned_ref[edges, :]
-        d_b = low(mm(turned[BLOCK:], d_source))
-        d_both = low(mm(turned, d_pre_low))
-        dnode_ref[nodes, width : 2 * width] = d_b
+        dedge_ref[edges, :] = low(d_pre)
+    for place in range(group):
+        nodes = nodes_of(place)
+        turned = turned_ref[edges_of(place), :]
+        d_both = low(mm(turned, dedge_ref[edges_of(place), :]))
+        dnode_ref[nodes, width : 2 * width] = low(mm(turned[BLOCK:], sources[place]))
         dnode_ref[nodes, 2 * width : 3 * width] = d_both[:BLOCK]
         dnode_ref[nodes, 3 * width :] = d_both[BLOCK:]
-    x = x_ref[...]
     add_rows(stat_ref, [col_sum(d_gated), pre_row])
-    accumulate(
-        acc_ref,
-        [
-            mm_rows(x, dnode_ref[:, :width]),
-            mm_rows(x, dnode_ref[:, width : 2 * width]),
-            mm_rows(e_ref[...], dedge_ref[...]),
-            mm_rows(x, dnode_ref[:, 2 * width : 3 * width]),
-            mm_rows(x, dnode_ref[:, 3 * width :]),
-        ],
-    )
-    emit(acc_ref, out_ref)
 
 
 def attend_back_kernel(
-    info_ref, dsum_ref, global_ref, att_ref, q_ref, k_ref, v_ref, prob_ref, x_ref, sums_ref,
-    backs_ref, w_ref, vec_ref, lgrad_ref, igrad_ref, ograd_ref,
-    dqkv_ref, stat_ref, *out_and_acc,
+    info_ref, dsum_ref, global_ref, q_ref, k_ref, v_ref, prob_ref, sums_ref,
+    backs_ref, w_ref, vec_ref,
+    dqkv_ref, dlow_ref, stat_ref,
 ):
-    acc_ref = out_and_acc[-1]
     group = global_ref.shape[0] // BLOCK
     width = global_ref.shape[1]
     score_scale = (width // HEADS) ** (-0.5)
@@ -375,54 +384,74 @@
         info_ref, dsum_ref, global_ref, sums_ref[...], backs_ref[...], 2, vec_ref[7:8, :], 2
     )
     d_low = low(d_global)
+    dlow_ref[...] = d_low
     d_att = low(mm_back(d_low, w_ref[8]))
+    masks = head_masks(width)
+    tall = tall_masks(width)
+    turned_att = low(mm_back(w_ref[8], d_low))
+    d_probs = [
+        mm(v_ref[nodes_of(place), :], side_stack(turned_att[:, nodes_of(place)], tall))
+        for place in range(group)
+    ]
+    straights = []
+    turns = []
     for place in range(group):
-        nodes = slice(place * BLOCK, (place + 1) * BLOCK)
-        att_stack = head_stack(d_att[nodes])
-        d_prob = mm_back(v_ref[nodes, :], att_stack)
+        nodes = nodes_of(place)
+        straight = []
         turned = []
-        straight = []
         for head in range(HEADS):
-            cols = slice(head * BLOCK, (head + 1) * BLOCK)
+            cols = nodes_of(head)
             prob = prob_ref[nodes, cols].astype(f32)
-            part = d_prob[:, cols]
+            part = d_probs[place][:, cols]
             inner = jnp.sum(prob * part, axis=0, keepdims=True)
-            d_score = prob * (part - inner) * score_scale
-            straight.append(low(d_score))
-            turned.append(low(d_score).T)
-        dqkv_ref[nodes, :width] = low(
-            mm(jnp.concatenate(turned, axis=1), head_stack(k_ref[nodes, :]))
+            d_score = low(prob * ((part - inner) * score_scale))
+            straight.append(d_score)
+            turned.append(d_score.T)
+        straights.append(jnp.concatenate(straight, axis=1))
+        turns.append(jnp.concatenate(turned, axis=1))
+    for place in range(group):
+        nodes = nodes_of(place)
+        dqkv_ref[nodes, :width] = low(mm(turns[place], head_stack(k_ref[nodes, :], masks)))
+        dqkv_ref[nodes, width : 2 * width] = low(
+            mm(straights[place], head_stack(q_ref[nodes, :], masks))
         )
-        dqkv_ref[nodes, width : 2 * width] = low(
-            mm(jnp.concatenate(straight, axis=1), head_stack(q_ref[nodes, :]))
+        dqkv_ref[nodes, 2 * width :] = low(
+            mm(prob_ref[nodes, :], head_stack(d_att[nodes], masks))
         )
-        dqkv_ref[nodes, 2 * width :] = low(mm(prob_ref[nodes, :], att_stack))
-    x = x_ref[...]
     add_rows(
         stat_ref,
         [
-            col_sum(dqkv_ref[:, :width].astype(f32)),
-            col_sum(dqkv_ref[:, 2 * width :].astype(f32)),
             col_sum(d_global),
         ],
     )
-    accumulate(
-        acc_ref,
-        [mm_rows(x, dqkv_ref[:, part * width : (part + 1) * width]) for part in range(3)]
-        + [mm_rows(att_ref[...], d_low)],
-    )
-    last = pl.num_programs(0) - 1
-
-    @pl.when(pl.program_id(0) == last)
-    def _():
-        parts = [lgrad_ref.at[place] for place in range(5)]
-        parts = parts + [acc_ref.at[place] for place in range(4)]
-        parts = parts + [ref.at[place] for ref in (igrad_ref, ograd_ref) for place in range(2)]
-        if len(out_and_acc) == 2:
-            for place, part in enumerate(parts):
-                out_and_acc[0][place] = low(part[...])
-        else:
-            pack(info_ref, parts, out_and_acc[0], out_and_acc[1])
+
+
+def branch_grad_kernel(
+    info_ref, x_ref, e_ref, att_ref, dnode_ref, dedge_ref, dqkv_ref, dlow_ref, igrad_ref, ograd_ref,
+    *outs,
+):
+    outs, bias_ref, (node_ref, wide_ref, edge_ref, acc_ref) = outs[:-5], outs[-5], outs[-4:]
+    width = x_ref.shape[1]
+    for place in (0, 2):
+        bias_ref[:, place // 2 * width : (place // 2 + 1) * width] = ones_sum(
+            dqkv_ref, slice(place * width, (place + 1) * width)
+        )
+    x = x_ref[...]
+    node_ref[...] = mm_rows(x, dnode_ref[...])
+    wide_ref[...] = mm_rows(x, dqkv_ref[...])
+    edge_ref[...] = mm_rows(e_ref[...], dedge_ref[...])
+    acc_ref[...] = mm_rows(att_ref[...], dlow_ref[...])
+    cols = [slice(place * width, (place + 1) * width) for place in range(4)]
+    parts = [node_ref.at[:, cols[0]], node_ref.at[:, cols[1]], edge_ref]
+    parts = parts + [node_ref.at[:, cols[2]], node_ref.at[:, cols[3]]]
+    parts = parts + [wide_ref.at[:, cols[place]] for place in range(3)] + [acc_ref]
+    parts = parts + [igrad_ref.at[:, cols[place]] for place in range(2)]
+    parts = parts + [ograd_ref.at[cols[place], :] for place in range(2)]
+    if len(outs) == 1:
+        for place, part in enumerate(parts):
+            outs[0][place] = low(part[...])
+    else:
+        pack(info_ref, parts, outs[0], outs[1])
 
 
 def reach(order, index):
@@ -507,6 +536,68 @@
     edge_ref[...] = mm_back(dedge_ref[...], w_ref[2])
 
 
+def square_kernel(
+    info_ref, kept_ref, got_ref, local_ref, attend_ref, inner_ref, wide_ref, grad_ref, tail_ref
+):
+    width = tail_ref.shape[1]
+    grad = kept_ref[...].astype(f32) + got_ref[...].astype(f32)
+    half = grad.shape[1] // 2
+    grad_ref[0] = grad[:, :half]
+    grad_ref[1] = grad[:, half:]
+    squares = grad * grad
+    square = jnp.sum(jnp.sum(squares, axis=0, keepdims=True), axis=1, keepdims=True)
+    tail_ref[0:2, :] = local_ref[0:2, :]
+    tail_ref[2:3, :] = wide_ref[0:1, :width]
+    tail_ref[3:4, :] = wide_ref[0:1, width:]
+    tail_ref[4:5, :] = attend_ref[0:1, :]
+    tail_ref[5:6, :] = inner_ref[0:1, :width]
+    tail_ref[6:7, :] = inner_ref[0:1, width:]
+    tail_ref[7:8, :] = jnp.broadcast_to(square, (1, width))
+
+
+def update_kernel(
+    info_ref, grad_ref, tail_ref, sums_ref, tops_ref, backs_ref, w_ref, w1_ref, w2_ref, v_ref,
+    v1_ref, v2_ref,
+    new_w_ref, new_w1_ref, new_w2_ref, new_v_ref, new_v1_ref, new_v2_ref, norm_ref,
+):
+    tail = tail_ref[...]
+    tops = tops_ref[...]
+    backs = backs_ref[...]
+    mean, rstd = norm_terms(tops, 0, sums_ref[4:5, :])
+    grad_v = jnp.concatenate(
+        [
+            tail[0:5],
+            backs[1:2],
+            backs[0:1],
+            backs[2:3],
+            backs[0:1],
+            tail[5:7],
+            backs[3:4],
+            (tops[3:4] - mean * tops[2:3]) * rstd,
+            tops[2:3],
+        ],
+        axis=0,
+    )
+    square = jnp.sum(jnp.sum(grad_v * grad_v, axis=0, keepdims=True), axis=1, keepdims=True)
+    norm = jnp.sqrt(tail[7:8, 0:1] + square)
+    norm_ref[...] = norm
+    factor = jnp.minimum(1.0, clip_limit / (norm + 1e-06))
+    new_v_ref[...], new_v1_ref[...], new_v2_ref[...] = adamw(
+        v_ref[...], factor * grad_v, v1_ref[...], v2_ref[...], rate_vecs, 0.0
+    )
+    mats, span = w_ref.shape
+    _, rows, half = grad_ref.shape
+    for piece in range(span // half):
+        cols = slice(piece * half, (piece + 1) * half)
+        if rows == mats:
+            grad = grad_ref[piece]
+        else:
+            grad = grad_ref[piece % 2, pl.ds(piece // 2, mats, rows // mats), :]
+        new_w_ref[:, cols], new_w1_ref[:, cols], new_w2_ref[:, cols] = adamw(
+            w_ref[:, cols], factor * grad, w1_ref[:, cols], w2_ref[:, cols], rate_mats, decay_mats
+        )
+
+
 def rows_spec(rows, width, offset=0):
     if offset:
         return pl.BlockSpec((rows, width), lambda step, info: (step + info[0], 0))
@@ -518,7 +609,7 @@
     return pl.BlockSpec(shape, lambda step, info: zeros)
 
 
-def call(kernel, steps, info, inputs, outputs, scratch=(), cost=None):
+def call(kernel, steps, info, inputs, outputs, scratch=(), room=12, cost=5):
     in_specs = []
     arrays = []
     for array, spec in inputs:
@@ -526,9 +617,9 @@
         in_specs.append(whole_spec(array.shape) if spec is None else spec)
     out_specs = []
     out_shapes = []
-    for shape, dtype, spec in outputs:
+    for shape, dtype, spec, *far in outputs:
         out_specs.append(whole_spec(shape) if spec is None else spec)
-        out_shapes.append(jax.ShapeDtypeStruct(shape, dtype))
+        out_shapes.append(pltpu.HBM(shape, dtype) if far else jax.ShapeDtypeStruct(shape, dtype))
     return pl.pallas_call(
         kernel,
         grid_spec=pltpu.PrefetchScalarGridSpec(
@@ -540,9 +631,12 @@
         ),
         out_shape=out_shapes,
         compiler_params=pltpu.CompilerParams(
-            dimension_semantics=("arbitrary",), vmem_limit_bytes=12 * 1024 * 1024
+            dimension_semantics=("arbitrary",), vmem_limit_bytes=room * 1024 * 1024
         ),
-        cost_estimate=cost,
+        name=kernel.__name__,
+        cost_estimate=pl.CostEstimate(
+            flops=cost * 1000000000, bytes_accessed=cost * 1000000, transcendentals=0
+        ),
     )(info, *arrays)
 
 
@@ -584,22 +678,26 @@
     return width * width // total == 8 * width
 
 
-def gather_matrices(shard, info, total, width):
+def gather_matrices(shard, info, total, width, work):
     mats = shard.shape[0]
     if not in_rows(total, width):
         gathered = lax.all_gather(shard, axis_names, axis=1, tiled=True)
-        return gathered.reshape(mats, width, width)
+        return (gathered.reshape(mats, width, width), work(info))
     held = shard.reshape(1, mats * 8, width)
     for number in reversed(range(len(chip_orders(total)[0]))):
-        held = jnp.concatenate([held, swap_chips(held, number, total)], axis=0)
+        got = swap_chips(held, number, total)
+        if number == 0:
+            got, done = beside(held, got, info, work)
+        held = jnp.concatenate([held, got], axis=0)
     other = swap_with(held, 1, total)
-    return call(
+    matrices = call(
         assemble_kernel,
         1,
         info,
         [(held, None), (other, None)],
         [((mats, width, width), bf16, None)],
     )[0]
+    return (matrices, done)
 
 
 def scatter_plain(grads, total):
@@ -612,10 +710,10 @@
         mine = ((place & step) != 0).astype(jnp.int32)
         sent = lax.dynamic_index_in_dim(held, 1 - mine, 0, keepdims=False)
         kept = lax.dynamic_index_in_dim(held, mine, 0, keepdims=False)
-        held = kept.astype(f32) + swap_with(sent, step, total).astype(f32)
+        got = swap_with(sent, step, total)
         if step * 2 < total:
-            held = low(held)
-    return held
+            held = low(kept.astype(f32) + got.astype(f32))
+    return (kept, got)
 
 
 def scatter_packed(kept, sent, total, info, works):
@@ -629,7 +727,7 @@
         if number < len(works):
             got, done = beside(sent, got, info, works[number])
             results.append(done)
-    return ((kept + got.astype(f32)).reshape(-1, 8 * kept.shape[-1]), results)
+    return ((kept[0], got[0]), results)
 
 
 def adamw(params, gradient, moment_one, moment_two, rate, decay):
@@ -677,7 +775,6 @@
     info = jnp.concatenate(
         [(branch_index * steps)[None], counts, branch_index[None], lax.axis_index("rows")[None]]
     ).astype(jnp.int32)
-    matrices = gather_matrices(w_bf, info, total, width)
 
     def by_step(values, slots):
         return own_half(values, branch_index).reshape(steps, group, slots)
@@ -687,22 +784,25 @@
 
     edge_spec = rows_spec(tall_edges, width)
     node_spec = rows_spec(tall, width)
-    hot, turned, bias = call(
-        prep_kernel,
-        steps,
-        info,
-        [
-            (by_step(edge_src, EB), step_spec(EB)),
-            (by_step(edge_dst, EB), step_spec(EB)),
-            (by_step(edge_mask, EB), step_spec(EB)),
-            (by_step(graph_ids, BLOCK), step_spec(BLOCK)),
-        ],
-        [
-            ((edges, EB), bf16, edge_spec),
-            ((edges, EB), bf16, edge_spec),
-            ((rows, BLOCK), f32, rows_spec(tall, BLOCK)),
-        ],
-    )
+    def prep_work(info):
+        return call(
+            prep_kernel,
+            steps,
+            info,
+            [
+                (by_step(edge_src, EB), step_spec(EB)),
+                (by_step(edge_dst, EB), step_spec(EB)),
+                (by_step(edge_mask, EB), step_spec(EB)),
+                (by_step(graph_ids, BLOCK), step_spec(BLOCK)),
+            ],
+            [
+                ((edges, EB), bf16, edge_spec, True),
+                ((edges, EB), bf16, edge_spec, True),
+                ((rows, BLOCK), f32, rows_spec(tall, BLOCK)),
+            ],
+        )
+
+    matrices, (hot, turned, bias) = gather_matrices(w_bf, info, total, width, prep_work)
     x_in = (node_feats, rows_spec(tall, width, 1))
     e_in = (edge_feats, rows_spec(tall_edges, width, 1))
     mats_in = (matrices, None)
@@ -768,7 +868,7 @@
         ],
     )
     tops = sum_small(top_part, total)
-    layer_out, d_mixed, d_hidden, d_summed, back_part = call(
+    d_mixed, d_hidden, d_summed, back_part = call(
         mix_back_kernel,
         steps,
         info,
@@ -785,18 +885,14 @@
         ],
         [
             node_bf,
-            node_bf,
             ((rows, 2 * width), bf16, wide_spec),
             node_bf,
             sums_out,
         ],
     )
 
-    def mat_out(number):
-        return ((number, width, width), f32, None)
-
-    def mat_acc(number):
-        return pltpu.VMEM((number, width, width), f32)
+    def mat_out(tall_by, wide_by):
+        return ((tall_by * width, wide_by * width), f32, None)
 
     def inner_work(info):
         return call(
@@ -804,9 +900,8 @@
             steps,
             info,
             [(summed_low, node_spec), (d_hidden, wide_spec)],
-            [mat_out(2)],
-            [mat_acc(2)],
-        )[0]
+            [mat_out(1, 2), ((8, 2 * width), f32, None)],
+        )
 
     def outer_work(info):
         return call(
@@ -814,15 +909,25 @@
             steps,
             info,
             [(hidden_low, wide_spec), (d_mixed, node_spec)],
-            [mat_out(2)],
-            [mat_acc(2)],
+            [mat_out(2, 1)],
         )[0]
 
-    backs, (inner_grads, outer_grads) = sum_small(back_part, total, info, [inner_work, outer_work])
+    def layer_work(info):
+        return call(
+            layer_kernel,
+            steps,
+            info,
+            [(mixed, node_spec), sums_in, (tops, None), vec_in],
+            [node_bf],
+        )[0]
+
+    backs, ((inner_grads, inner_bias), outer_grads, layer_out) = sum_small(
+        back_part, total, info, [inner_work, outer_work, layer_work]
+    )
     backs_in = (backs, None)
     dsum_in = (d_summed, node_spec)
     dnode_spec = rows_spec(tall, 4 * width)
-    d_node, d_edge, local_bias, local_grads = call(
+    d_node, d_edge, local_bias = call(
         local_back_kernel,
         steps,
         info,
@@ -837,8 +942,6 @@
             (b_source, edge_spec),
             (hot, edge_spec),
             (turned, edge_spec),
-            x_in,
-            e_in,
             sums_in,
             backs_in,
             vec_in,
@@ -847,9 +950,7 @@
             ((rows, 4 * width), bf16, dnode_spec),
             ((edges, width), bf16, edge_spec),
             sums_out,
-            mat_out(5),
-        ],
-        [mat_acc(5)],
+        ],
     )
     dqkv_spec = rows_spec(tall, 3 * width)
     slots = total // 2
@@ -857,30 +958,48 @@
     grad_outs = [((MATS, width, width), bf16, None)]
     if packed:
         grad_outs = [((slots, MATS * 8, width), bf16, None)] * 2
-    d_qkv, attend_bias, *grads = call(
+    d_qkv, d_low, attend_bias = call(
         attend_back_kernel,
         steps,
         info,
         [
             dsum_in,
             (global_hat, node_spec),
-            (attended, node_spec),
             (queries, node_spec),
             (keyed, node_spec),
             (valued, node_spec),
             (probs, prob_spec),
-            x_in,
             sums_in,
             backs_in,
             mats_in,
             vec_in,
-            (local_grads, None),
+        ],
+        [((rows, 3 * width), bf16, dqkv_spec), node_bf, sums_out],
+    )
+    *grads, wide_bias = call(
+        branch_grad_kernel,
+        1,
+        info,
+        [
+            (node_feats, pl.BlockSpec((rows, width), lambda step, info: (info[0] // steps, 0))),
+            (edge_feats, pl.BlockSpec((edges, width), lambda step, info: (info[0] // steps, 0))),
+            (attended, None),
+            (d_node, None),
+            (d_edge, None),
+            (d_qkv, None),
+            (d_low, None),
             (inner_grads, None),
             (outer_grads, None),
         ],
-        [((rows, 3 * width), bf16, dqkv_spec), sums_out] + grad_outs,
-        [mat_acc(4)],
-    )
+        grad_outs + [((8, 2 * width), f32, None)],
+        [
+            pltpu.VMEM((width, 4 * width), f32),
+            pltpu.VMEM((width, 3 * width), f32),
+            pltpu.VMEM((width, width), f32),
+            pltpu.VMEM((width, width), f32),
+        ],
+    )
+
     def node_work(info):
         return call(
             node_grad_kernel,
@@ -916,36 +1035,31 @@
     else:
         grad_shard = scatter_plain(grads[0], total)
         node_grad, edge_grad = node_work(info), edge_work(info)
-    square_row = jnp.broadcast_to(jnp.sum(grad_shard * grad_shard), (1, width))
-    tail = sum_small(
-        jnp.concatenate(
-            [local_bias[:2], attend_bias[:3], square_row, jnp.zeros((2, width), f32)], axis=0
-        ),
-        total,
-    )
-    top_mean = tops[0:1] / sums[4:5]
-    top_rstd = lax.rsqrt(tops[1:2] / sums[4:5] - top_mean * top_mean + eps_norm)
-    vector_total = jnp.concatenate(
-        [
-            tail[:5],
-            backs[1:2],
-            backs[0:1],
-            backs[2:3],
-            backs[0:1],
-            backs[3:6],
-            (tops[3:4] - top_mean * tops[2:3]) * top_rstd,
-            tops[2:3],
-        ],
-        axis=0,
-    )
-    grad_norm = jnp.sqrt(tail[5, 0] + jnp.sum(vector_total * vector_total))
-    factor = jnp.minimum(1.0, clip_limit / (grad_norm + 1e-06))
-    new_weights, first_w, second_w = adamw(
-        weights, factor * grad_shard, weight_moment1, weight_moment2, rate_mats, decay_mats
-    )
-    new_vectors, first_v, second_v = adamw(
-        vectors, factor * vector_total, vector_moment1, vector_moment2, rate_vecs, 0.0
-    )
+    grad_rows, tail_part = call(
+        square_kernel,
+        1,
+        info,
+        [(part, None) for part in grad_shard]
+        + [(local_bias, None), (attend_bias, None), (inner_bias, None), (wide_bias, None)],
+        [((2, grad_shard[0].shape[0], grad_shard[0].shape[1] // 2), f32, None), sums_out],
+    )
+    tail = sum_small(tail_part, total)
+    like_mats = (weights.shape, f32, None)
+    like_vecs = (vectors.shape, f32, None)
+    new_weights, first_w, second_w, new_vectors, first_v, second_v, norm = call(
+        update_kernel,
+        1,
+        info,
+        [
+            (array, None)
+            for array in (
+                grad_rows, tail, sums, tops, backs, weights, weight_moment1, weight_moment2,
+                vectors, vector_moment1, vector_moment2,
+            )
+        ],
+        [like_mats] * 3 + [like_vecs] * 3 + [((1, 1), f32, None)],
+    )
+    grad_norm = norm.reshape(())
     return (
         layer_out,
         node_grad,

time: 188 us -> 166 us (0.88)
  waiting for transfers between devices: 71.4 us -> 52 us
  starting transfers between devices: 37.8 us -> 48.6 us
  Pallas kernels: 65.6 us -> 55.8 us
  between operations: 4.32 us -> 1.67 us
  other arithmetic: 5.26 us -> 3.04 us
    ppermute x8, waiting for transfers between devices: 28.9 us -> 18.7 us  [swap_chips(): lax.ppermute(values, axis_names, [(place, place ^ orders[place % 2][numbe...]
    pallas_call x12 -> x16, Pallas kernels: 65.6 us -> 55.8 us  [call(): pl.pallas_call(kernel, grid_spec=pltpu.PrefetchScalarGridSpec(num_scalar_...]
    ppermute x22, waiting for transfers between devices: 42.4 us -> 33.2 us  [swap_with(): lax.ppermute(values, axis_names, [(place, place ^ step) for place in rang...]
    ppermute x22, starting transfers between devices: 23.3 us -> 31.7 us  [swap_with(): lax.ppermute(values, axis_names, [(place, place ^ step) for place in rang...]
    ppermute x8, starting transfers between devices: 14.5 us -> 16.8 us  [swap_chips(): lax.ppermute(values, axis_names, [(place, place ^ orders[place % 2][numbe...]
    dynamic_slice x4 -> x3, local copies, waits for them, and re-layouts: 0.04 us -> 2.16 us  [own_half(): return lax.dynamic_slice_in_dim(values, branch_index * half, half, 0)]
  transfers between devices with their start and end apart: 30 -> 30, of which waited for: 27 -> 27; matrix products, arithmetic and copies ran while one was open for 1% -> 2% of each run, Pallas kernels for 7% -> 10%
where the time goes in v2:
time: 166 us
  Pallas kernels  55.8 us (34%)
  waiting for transfers between devices  52 us (31%)
  starting transfers between devices  48.6 us (29%)
  local copies, waits for them, and re-layouts  4.85 us (3%)
  other arithmetic  3.04 us (2%)
  between operations  1.67 us (1%)
    pallas_call x16, Pallas kernels, call(): pl.pallas_call(kernel, grid_spec=pltpu.PrefetchScalarGridSpec(num_scalar_...  55.8 us
    ppermute x22, waiting for transfers between devices, swap_with(): lax.ppermute(values, axis_names, [(place, place ^ step) for place in rang...  33.2 us
    ppermute x22, starting transfers between devices, swap_with(): lax.ppermute(values, axis_names, [(place, place ^ step) for place in rang...  31.7 us
    ppermute x8, waiting for transfers between devices, swap_chips(): lax.ppermute(values, axis_names, [(place, place ^ orders[place % 2][numbe...  18.7 us
    ppermute x8, starting transfers between devices, swap_chips(): lax.ppermute(values, axis_names, [(place, place ^ orders[place % 2][numbe...  16.8 us
  transfers between devices with their start and end apart: 30, of which 27 were waited for; matrix products, arithmetic and copies ran while one was open for 2% of the time, Pallas kernels for 10%

profile of v2, /device:TPU:0, one launch (start us, length us, event | category | flops | bytes accessed | tf_op | source)
XLA Modules:
  0.0 166.0 jit_solution(17414761021186872991)
XLA Ops:
  1.6 4.1 %collective-permute-start = (bf16[1,104,256]{2,1,0:T(8,128)(2,1)S(1)}, bf16[1,104,256]{2,1,0:T(8,128)(2,1)S(1)}, u32[]{:S(2)}, u32[]{:S(2)}) collective-permute-start(bf16[1,104,256]{2,1,0:T(8,128)(2,1)S(1)} %reshape.42), channel_id=1, source_target_pairs={{0,16},{1,17},{2,18},{3,19},{4,20},{5,21},{6,22},{7,23},{8,24},{9,... | collective-permute-start | bytes 159752 | tf_op jit(solution)/shard_map/ppermute | solution.py:670
  10.5 3.1 %collective-permute-done.1 = bf16[2,104,256]{2,1,0:T(8,128)(2,1)S(1)} collective-permute-done((bf16[2,104,256]{2,1,0:T(8,128)(2,1)S(1)}, bf16[2,104,256]{2,1,0:T(8,128)(2,1)S(1)}, u32[]{:S(2)}, u32[]{:S(2)}) %collective-permute-start.1) | collective-permute-done | bytes 106528 | tf_op jit(solution)/shard_map/ppermute | solution.py:670
  15.2 4.3 %collective-permute-done.2 = bf16[4,104,256]{2,1,0:T(8,128)(2,1)S(1)} collective-permute-done((bf16[4,104,256]{2,1,0:T(8,128)(2,1)S(1)}, bf16[4,104,256]{2,1,0:T(8,128)(2,1)S(1)}, u32[]{:S(2)}, u32[]{:S(2)}) %collective-permute-start.2) | collective-permute-done | bytes 213024 | tf_op jit(solution)/shard_map/ppermute | solution.py:670
  21.1 3.0 %prep_kernel.1 = (bf16[4096,256]{1,0:T(8,128)(2,1)}, bf16[4096,256]{1,0:T(8,128)(2,1)}, f32[2048,128]{1,0:T(8,128)S(1)}) custom-call(s32[19]{0:T(128)S(1)} %pad_add_fusion.info_ref, s32[2,8,256]{2,1,0:T(8,128)S(1)} %reshape.43.src_ref, s32[2,8,256]{2,1,0:T(8,128)S(1)} %reshape.44.dst_ref, s32[2,8,256]{2,1,0:T(8,128)S(1)} %reshape.45.mask_ref, ...), custom_call_target="tpu_custom_call" | custom-call | flops 5000000000 | bytes 5000000 | tf_op jit(solution)/shard_map/prep_kernel/pallas_call | solution.py:623
  25.1 2.7 %collective-permute-done.3 = bf16[8,104,256]{2,1,0:T(8,128)(2,1)S(1)} collective-permute-done((bf16[8,104,256]{2,1,0:T(8,128)(2,1)S(1)}, bf16[8,104,256]{2,1,0:T(8,128)(2,1)S(1)}, u32[]{:S(2)}, u32[]{:S(2)}) %collective-permute-start.3) | collective-permute-done | bytes 426016 | tf_op jit(solution)/shard_map/ppermute | solution.py:670
  31.2 6.7 %attend_kernel.1 = (f32[2048,256]{1,0:T(8,128)S(1)}, bf16[2048,256]{1,0:T(8,128)(2,1)S(1)}, bf16[2048,256]{1,0:T(8,128)(2,1)S(1)}, bf16[2048,256]{1,0:T(8,128)(2...) custom-call(s32[19]{0:T(128)S(1)} %pad_add_fusion.info_ref, ...), custom_call_target="tpu_custom_call" | custom-call | flops 5000000000 | bytes 5000000 | tf_op jit(solution)/shard_map/attend_kernel/pallas_call | solution.py:623
  39.0 6.6 %local_kernel.1 = (f32[2048,256]{1,0:T(8,128)S(1)}, bf16[2048,256]{1,0:T(8,128)(2,1)S(1)}, bf16[2048,256]{1,0:T(8,128)(2,1)S(1)}, bf16[2048,256]{1,0:T(8,128)(2,...) custom-call(s32[19]{0:T(128)S(1)} %pad_add_fusion.info_ref, ...), custom_call_target="tpu_custom_call" | custom-call | flops 5000000000 | bytes 5000000 | tf_op jit(solution)/shard_map/local_kernel/pallas_call | solution.py:623
  48.6 2.2 %collective-permute-done.6 = f32[8,256]{1,0:T(8,128)S(1)} collective-permute-done((f32[8,256]{1,0:T(8,128)S(1)}, f32[8,256]{1,0:T(8,128)S(1)}, u32[]{:S(2)}, u32[]{:S(2)}) %collective-permute-start.6) | collective-permute-done | bytes 8224 | tf_op jit(solution)/shard_map/ppermute | solution.py:644
  58.1 2.9 %collective-permute-start.9 = (f32[8,256]{1,0:T(8,128)S(1)}, f32[8,256]{1,0:T(8,128)S(1)}, u32[]{:S(2)}, u32[]{:S(2)}) collective-permute-start(f32[8,256]{1,0:T(8,128)S(1)} %add.98), channel_id=1, source_target_pairs={{0,16},{1,17},{2,18},{3,19},{4,20},{5,21},{6,22},{7,23},{8,24},{9,... | collective-permute-start | bytes 24584 | tf_op jit(solution)/shard_map/ppermute | solution.py:644
  62.7 4.1 %mix_kernel.1 = (bf16[2048,256]{1,0:T(8,128)(2,1)S(1)}, bf16[2048,512]{1,0:T(8,128)(2,1)S(1)}, bf16[2048,512]{1,0:T(8,128)(2,1)S(1)}, bf16[2048,256]{1,0:T(8,128...) custom-call(s32[19]{0:T(128)S(1)} %pad_add_fusion.info_ref, ...), custom_call_target="tpu_custom_call" | custom-call | flops 5000000000 | bytes 5000000 | tf_op jit(solution)/shard_map/mix_kernel/pallas_call | solution.py:623
  79.0 2.9 %collective-permute-start.14 = (f32[8,256]{1,0:T(8,128)S(1)}, f32[8,256]{1,0:T(8,128)S(1)}, u32[]{:S(2)}, u32[]{:S(2)}) collective-permute-start(f32[8,256]{1,0:T(8,128)S(1)} %add.103), channel_id=1, source_target_pairs={{0,16},{1,17},{2,18},{3,19},{4,20},{5,21},{6,22},{7,23},{8,24},{9,... | collective-permute-start | bytes 24584 | tf_op jit(solution)/shard_map/ppermute | solution.py:644
  83.6 2.9 %mix_back_kernel.1 = (bf16[2048,256]{1,0:T(8,128)(2,1)S(1)}, bf16[2048,512]{1,0:T(8,128)(2,1)S(1)}, bf16[2048,256]{1,0:T(8,128)(2,1)S(1)}, f32[8,256]{1,0:T(8,128)S(1)}) custom-call(s32[19]{0:T(128)S(1)} %pad_add_fusion.info_ref, f32[2048,256]{1,0:T(8,128)S(1)} %get-tuple-element.92.mixed_ref, bf16[2048,512]{1,0:T(8,128)(2,1)S(1)} %get-tuple-element.93.slope_ref, ...), custom_call_target="tpu_custom_call" | custom-call | flops 5000000000 | bytes 5000000 | tf_op jit(solution)/shard_map/mix_back_kernel/pallas_call | solution.py:623
  99.0 2.9 %collective-permute-start.19 = (f32[8,256]{1,0:T(8,128)S(1)}, f32[8,256]{1,0:T(8,128)S(1)}, u32[]{:S(2)}, u32[]{:S(2)}) collective-permute-start(f32[8,256]{1,0:T(8,128)S(1)} %add.108), channel_id=1, source_target_pairs={{0,16},{1,17},{2,18},{3,19},{4,20},{5,21},{6,22},{7,23},{8,24},{9,... | collective-permute-start | bytes 24584 | tf_op jit(solution)/shard_map/ppermute | solution.py:644
  103.6 8.2 %attend_back_kernel.1 = (bf16[2048,768]{1,0:T(8,128)(2,1)S(1)}, bf16[2048,256]{1,0:T(8,128)(2,1)S(1)}, f32[8,256]{1,0:T(8,128)S(1)}) custom-call(s32[19]{0:T(128)S(1)} %pad_add_fusion.info_ref, bf16[2048,256]{1,0:T(8,128)(2,1)S(1)} %get-tuple-element.111.dsum_ref, bf16[2048,256]{1,0:T(8,128)(2,1)S(1)} %get-tuple-element.95.ghat_ref.global_ref, ...), custom_call_target="tpu_custom_call" | custom-call | flops 5000000000 | bytes 5000000 | tf_op jit(solution)/shard_map/attend_back_kernel/pallas_call | solution.py:623
  111.8 4.5 %local_back_kernel.1 = (bf16[2048,1024]{1,0:T(8,128)(2,1)S(1)}, bf16[4096,256]{1,0:T(8,128)(2,1)S(1)}, f32[8,256]{1,0:T(8,128)S(1)}) custom-call(s32[19]{0:T(128)S(1)} %pad_add_fusion.info_ref, bf16[2048,256]{1,0:T(8,128)(2,1)S(1)} %get-tuple-element.111.dsum_ref, bf16[2048,256]{1,0:T(8,128)(2,1)S(1)} %get-tuple-element.94.lhat_ref.local_ref, ...), custom_call_target="tpu_custom_call" | custom-call | flops 5000000000 | bytes 5000000 | tf_op jit(solution)/shard_map/local_back_kernel/pallas_call | solution.py:623
  116.3 3.8 %branch_grad_kernel.1 = (bf16[16,104,256]{2,1,0:T(8,128)(2,1)S(1)}, bf16[16,104,256]{2,1,0:T(8,128)(2,1)S(1)}, f32[8,512]{1,0:T(8,128)S(1)}) custom-call(s32[19]{0:T(128)S(1)} %pad_add_fusion.info_ref, bf16[4096,256]{1,0:T(8,128)(2,1)S(1)} %copy-done.3, bf16[8192,256]{1,0:T(8,128)(2,1)S(1)} %copy-done.2, bf16[2048,256]{1,0:T(8,128)(2,1)S(1)} %get-tuple-element.110.att_ref, ...), custom_call_target="tpu_custom_call" | custom-call | flops 5000000000 | bytes 5000000 | tf_op jit(solution)/shard_map/branch_grad_kernel/pallas_call | solution.py:623
  120.3 2.4 %collective-permute-done.20 = bf16[16,104,256]{2,1,0:T(8,128)(2,1)S(1)} collective-permute-done((bf16[16,104,256]{2,1,0:T(8,128)(2,1)S(1)}, bf16[16,104,256]{2,1,0:T(8,128)(2,1)S(1)}, u32[]{:S(2)}, u32[]{:S(2)}) %collective-permute-start.20) | collective-permute-done | bytes 852000 | tf_op jit(solution)/shard_map/ppermute | solution.py:644
  124.3 4.3 %node_grad_kernel.1 = f32[2048,256]{1,0:T(8,128)} custom-call(s32[19]{0:T(128)S(1)} %pad_add_fusion.info_ref, bf16[2048,256]{1,0:T(8,128)(2,1)S(1)} %get-tuple-element.111.dsum_ref, bf16[2048,256]{1,0:T(8,128)(2,1)S(1)} %get-tuple-element.94.lhat_ref.local_ref, bf16[2048,256]{1,0:T(8,128)(2,1)S(1)} %get-tuple-element.95.ghat_ref.global_ref, ...), custom_call_target="tpu_custom_call" | custom-call | flops 5000000000 | bytes 5000000 | tf_op jit(solution)/shard_map/node_grad_kernel/pallas_call | solution.py:623
  128.7 2.4 %collective-permute-done.21 = bf16[8,104,256]{2,1,0:T(8,128)(2,1)S(1)} collective-permute-done((bf16[8,104,256]{2,1,0:T(8,128)(2,1)S(1)}, bf16[8,104,256]{2,1,0:T(8,128)(2,1)S(1)}, u32[]{:S(2)}, u32[]{:S(2)}) %collective-permute-start.21) | collective-permute-done | bytes 426016 | tf_op jit(solution)/shard_map/ppermute | solution.py:670
  132.7 3.0 %edge_grad_kernel.1 = f32[4096,256]{1,0:T(8,128)} custom-call(s32[19]{0:T(128)S(1)} %pad_add_fusion.info_ref, bf16[4096,256]{1,0:T(8,128)(2,1)S(1)} %get-tuple-element.120.dedge_ref, bf16[13,256,256]{2,1,0:T(8,128)(2,1)S(1)} %copy-done.14), custom_call_target="tpu_custom_call" | custom-call | flops 5000000000 | bytes 5000000 | tf_op jit(solution)/shard_map/edge_grad_kernel/pallas_call | solution.py:623
  138.9 2.9 %collective-permute-done.23 = bf16[2,104,256]{2,1,0:T(8,128)(2,1)S(1)} collective-permute-done((bf16[2,104,256]{2,1,0:T(8,128)(2,1)S(1)}, bf16[2,104,256]{2,1,0:T(8,128)(2,1)S(1)}, u32[]{:S(2)}, u32[]{:S(2)}) %collective-permute-start.23) | collective-permute-done | bytes 106528 | tf_op jit(solution)/shard_map/ppermute | solution.py:670
  141.9 3.0 %collective-permute-start.24 = (bf16[1,104,256]{2,1,0:T(8,128)(2,1)S(1)}, bf16[1,104,256]{2,1,0:T(8,128)(2,1)S(1)}, u32[]{:S(2)}, u32[]{:S(2)}) collective-permute-start(bf16[1,104,256]{2,1,0:T(8,128)(2,1)S(1)} %get-tuple-element.156), channel_id=1, source_target_pairs={{0,16},{1,17},{2,18},{3,19},{4,20},{5,21},{6,22},{7,23},{8,24},{9,... | collective-permute-start | bytes 159752 | tf_op jit(solution)/shard_map/ppermute | solution.py:670
  150.3 2.2 %collective-permute-done.26 = f32[8,256]{1,0:T(8,128)S(1)} collective-permute-done((f32[8,256]{1,0:T(8,128)S(1)}, f32[8,256]{1,0:T(8,128)S(1)}, u32[]{:S(2)}, u32[]{:S(2)}) %collective-permute-start.26) | collective-permute-done | bytes 8224 | tf_op jit(solution)/shard_map/ppermute | solution.py:644
  159.8 2.9 %collective-permute-start.29 = (f32[8,256]{1,0:T(8,128)S(1)}, f32[8,256]{1,0:T(8,128)S(1)}, u32[]{:S(2)}, u32[]{:S(2)}) collective-permute-start(f32[8,256]{1,0:T(8,128)S(1)} %add.121), channel_id=1, source_target_pairs={{0,16},{1,17},{2,18},{3,19},{4,20},{5,21},{6,22},{7,23},{8,24},{9,... | collective-permute-start | bytes 24584 | tf_op jit(solution)/shard_map/ppermute | solution.py:644
  (145 shorter events, 76.2 us)
Async XLA Ops:
  1.6 7.2 %collective-permute-start = (bf16[1,104,256]{2,1,0:T(8,128)(2,1)S(1)}, bf16[1,104,256]{2,1,0:T(8,128)(2,1)S(1)}, u32[]{:S(2)}, u32[]{:S(2)}) collective-permute-start(bf16[1,104,256]{2,1,0:T(8,128)(2,1)S(1)} %reshape.42), channel_id=1, source_target_pairs={{0,16},{1,17},{2,18},{3,19},{4,20},{5,21},{6,22},{7,23},{8,24},{9,... | collective-permute-start | bytes 159752 | tf_op jit(solution)/shard_map/ppermute | solution.py:670
  8.8 4.8 %collective-permute-start.1 = (bf16[2,104,256]{2,1,0:T(8,128)(2,1)S(1)}, bf16[2,104,256]{2,1,0:T(8,128)(2,1)S(1)}, u32[]{:S(2)}, u32[]{:S(2)}) collective-permute-start(bf16[2,104,256]{2,1,0:T(8,128)(2,1)S(1)} %pad_maximum_fusion.1), channel_id=1, source_target_pairs={{0,8},{1,3},{2,10},{3,1},{4,12},{5,7},{6,14},{7,5},{8,0},{9,11},{1... | collective-permute-start | bytes 319496 | tf_op jit(solution)/shard_map/ppermute | solution.py:670
  13.6 5.9 %collective-permute-start.2 = (bf16[4,104,256]{2,1,0:T(8,128)(2,1)S(1)}, bf16[4,104,256]{2,1,0:T(8,128)(2,1)S(1)}, u32[]{:S(2)}, u32[]{:S(2)}) collective-permute-start(bf16[4,104,256]{2,1,0:T(8,128)(2,1)S(1)} %pad_maximum_fusion), channel_id=1, source_target_pairs={{0,4},{1,9},{2,6},{3,11},{4,0},{5,13},{6,2},{7,15},{8,12},{9,1},{1... | collective-permute-start | bytes 638984 | tf_op jit(solution)/shard_map/ppermute | solution.py:670
  19.6 8.2 %collective-permute-start.3 = (bf16[8,104,256]{2,1,0:T(8,128)(2,1)S(1)}, bf16[8,104,256]{2,1,0:T(8,128)(2,1)S(1)}, u32[]{:S(2)}, u32[]{:S(2)}) collective-permute-start(bf16[8,104,256]{2,1,0:T(8,128)(2,1)S(1)} %get-tuple-element.159), channel_id=1, source_target_pairs={{0,2},{1,5},{2,0},{3,7},{4,6},{5,1},{6,4},{7,3},{8,10},{9,13},{10,... | collective-permute-start | bytes 1277960 | tf_op jit(solution)/shard_map/ppermute | solution.py:670
  47.1 3.7 %collective-permute-start.6 = (f32[8,256]{1,0:T(8,128)S(1)}, f32[8,256]{1,0:T(8,128)S(1)}, u32[]{:S(2)}, u32[]{:S(2)}) collective-permute-start(f32[8,256]{1,0:T(8,128)S(1)} %fusion.4), channel_id=1, source_target_pairs={{0,2},{1,3},{2,0},{3,1},{4,6},{5,7},{6,4},{7,5},{8,10},{9,11},{10,... | collective-permute-start | bytes 24584 | tf_op jit(solution)/shard_map/ppermute | solution.py:644
  50.8 3.7 %collective-permute-start.7 = (f32[8,256]{1,0:T(8,128)S(1)}, f32[8,256]{1,0:T(8,128)S(1)}, u32[]{:S(2)}, u32[]{:S(2)}) collective-permute-start(f32[8,256]{1,0:T(8,128)S(1)} %add.96), channel_id=1, source_target_pairs={{0,4},{1,5},{2,6},{3,7},{4,0},{5,1},{6,2},{7,3},{8,12},{9,13},{10,... | collective-permute-start | bytes 24584 | tf_op jit(solution)/shard_map/ppermute | solution.py:644
  54.5 3.7 %collective-permute-start.8 = (f32[8,256]{1,0:T(8,128)S(1)}, f32[8,256]{1,0:T(8,128)S(1)}, u32[]{:S(2)}, u32[]{:S(2)}) collective-permute-start(f32[8,256]{1,0:T(8,128)S(1)} %add.97), channel_id=1, source_target_pairs={{0,8},{1,9},{2,10},{3,11},{4,12},{5,13},{6,14},{7,15},{8,0},{9,1},... | collective-permute-start | bytes 24584 | tf_op jit(solution)/shard_map/ppermute | solution.py:644
  58.1 4.5 %collective-permute-start.9 = (f32[8,256]{1,0:T(8,128)S(1)}, f32[8,256]{1,0:T(8,128)S(1)}, u32[]{:S(2)}, u32[]{:S(2)}) collective-permute-start(f32[8,256]{1,0:T(8,128)S(1)} %add.98), channel_id=1, source_target_pairs={{0,16},{1,17},{2,18},{3,19},{4,20},{5,21},{6,22},{7,23},{8,24},{9,... | collective-permute-start | bytes 24584 | tf_op jit(solution)/shard_map/ppermute | solution.py:644
  68.1 3.7 %collective-permute-start.11 = (f32[8,256]{1,0:T(8,128)S(1)}, f32[8,256]{1,0:T(8,128)S(1)}, u32[]{:S(2)}, u32[]{:S(2)}) collective-permute-start(f32[8,256]{1,0:T(8,128)S(1)} %add.100), channel_id=1, source_target_pairs={{0,2},{1,3},{2,0},{3,1},{4,6},{5,7},{6,4},{7,5},{8,10},{9,11},{10,... | collective-permute-start | bytes 24584 | tf_op jit(solution)/shard_map/ppermute | solution.py:644
  71.7 3.7 %collective-permute-start.12 = (f32[8,256]{1,0:T(8,128)S(1)}, f32[8,256]{1,0:T(8,128)S(1)}, u32[]{:S(2)}, u32[]{:S(2)}) collective-permute-start(f32[8,256]{1,0:T(8,128)S(1)} %add.101), channel_id=1, source_target_pairs={{0,4},{1,5},{2,6},{3,7},{4,0},{5,1},{6,2},{7,3},{8,12},{9,13},{10,... | collective-permute-start | bytes 24584 | tf_op jit(solution)/shard_map/ppermute | solution.py:644
  75.4 3.7 %collective-permute-start.13 = (f32[8,256]{1,0:T(8,128)S(1)}, f32[8,256]{1,0:T(8,128)S(1)}, u32[]{:S(2)}, u32[]{:S(2)}) collective-permute-start(f32[8,256]{1,0:T(8,128)S(1)} %add.102), channel_id=1, source_target_pairs={{0,8},{1,9},{2,10},{3,11},{4,12},{5,13},{6,14},{7,15},{8,0},{9,1},... | collective-permute-start | bytes 24584 | tf_op jit(solution)/shard_map/ppermute | solution.py:644
  79.0 4.5 %collective-permute-start.14 = (f32[8,256]{1,0:T(8,128)S(1)}, f32[8,256]{1,0:T(8,128)S(1)}, u32[]{:S(2)}, u32[]{:S(2)}) collective-permute-start(f32[8,256]{1,0:T(8,128)S(1)} %add.103), channel_id=1, source_target_pairs={{0,16},{1,17},{2,18},{3,19},{4,20},{5,21},{6,22},{7,23},{8,24},{9,... | collective-permute-start | bytes 24584 | tf_op jit(solution)/shard_map/ppermute | solution.py:644
  87.8 3.7 %collective-permute-start.16 = (f32[8,256]{1,0:T(8,128)S(1)}, f32[8,256]{1,0:T(8,128)S(1)}, u32[]{:S(2)}, u32[]{:S(2)}) collective-permute-start(f32[8,256]{1,0:T(8,128)S(1)} %add.105), channel_id=1, source_target_pairs={{0,2},{1,3},{2,0},{3,1},{4,6},{5,7},{6,4},{7,5},{8,10},{9,11},{10,... | collective-permute-start | bytes 24584 | tf_op jit(solution)/shard_map/ppermute | solution.py:644
  91.4 3.7 %collective-permute-start.17 = (f32[8,256]{1,0:T(8,128)S(1)}, f32[8,256]{1,0:T(8,128)S(1)}, u32[]{:S(2)}, u32[]{:S(2)}) collective-permute-start(f32[8,256]{1,0:T(8,128)S(1)} %add.106), channel_id=1, source_target_pairs={{0,4},{1,5},{2,6},{3,7},{4,0},{5,1},{6,2},{7,3},{8,12},{9,13},{10,... | collective-permute-start | bytes 24584 | tf_op jit(solution)/shard_map/ppermute | solution.py:644
  95.1 3.9 %collective-permute-start.18 = (f32[8,256]{1,0:T(8,128)S(1)}, f32[8,256]{1,0:T(8,128)S(1)}, u32[]{:S(2)}, u32[]{:S(2)}) collective-permute-start(f32[8,256]{1,0:T(8,128)S(1)} %add.107), channel_id=1, source_target_pairs={{0,8},{1,9},{2,10},{3,11},{4,12},{5,13},{6,14},{7,15},{8,0},{9,1},... | collective-permute-start | bytes 24584 | tf_op jit(solution)/shard_map/ppermute | solution.py:644
  99.0 4.6 %collective-permute-start.19 = (f32[8,256]{1,0:T(8,128)S(1)}, f32[8,256]{1,0:T(8,128)S(1)}, u32[]{:S(2)}, u32[]{:S(2)}) collective-permute-start(f32[8,256]{1,0:T(8,128)S(1)} %add.108), channel_id=1, source_target_pairs={{0,16},{1,17},{2,18},{3,19},{4,20},{5,21},{6,22},{7,23},{8,24},{9,... | collective-permute-start | bytes 24584 | tf_op jit(solution)/shard_map/ppermute | solution.py:644
  122.8 8.2 %collective-permute-start.21 = (bf16[8,104,256]{2,1,0:T(8,128)(2,1)S(1)}, bf16[8,104,256]{2,1,0:T(8,128)(2,1)S(1)}, u32[]{:S(2)}, u32[]{:S(2)}) collective-permute-start(bf16[8,104,256]{2,1,0:T(8,128)(2,1)S(1)} %get-tuple-element.151), channel_id=1, source_target_pairs={{0,2},{1,5},{2,0},{3,7},{4,6},{5,1},{6,4},{7,3},{8,10},{9,13},{10,... | collective-permute-start | bytes 1277960 | tf_op jit(solution)/shard_map/ppermute | solution.py:670
  131.1 5.9 %collective-permute-start.22 = (bf16[4,104,256]{2,1,0:T(8,128)(2,1)S(1)}, bf16[4,104,256]{2,1,0:T(8,128)(2,1)S(1)}, u32[]{:S(2)}, u32[]{:S(2)}) collective-permute-start(bf16[4,104,256]{2,1,0:T(8,128)(2,1)S(1)} %get-tuple-element.153), channel_id=1, source_target_pairs={{0,4},{1,9},{2,6},{3,11},{4,0},{5,13},{6,2},{7,15},{8,12},{9,1},{1... | collective-permute-start | bytes 638984 | tf_op jit(solution)/shard_map/ppermute | solution.py:670
  137.1 4.8 %collective-permute-start.23 = (bf16[2,104,256]{2,1,0:T(8,128)(2,1)S(1)}, bf16[2,104,256]{2,1,0:T(8,128)(2,1)S(1)}, u32[]{:S(2)}, u32[]{:S(2)}) collective-permute-start(bf16[2,104,256]{2,1,0:T(8,128)(2,1)S(1)} %get-tuple-element.154), channel_id=1, source_target_pairs={{0,8},{1,3},{2,10},{3,1},{4,12},{5,7},{6,14},{7,5},{8,0},{9,11},{1... | collective-permute-start | bytes 319496 | tf_op jit(solution)/shard_map/ppermute | solution.py:670
  141.9 5.1 %collective-permute-start.24 = (bf16[1,104,256]{2,1,0:T(8,128)(2,1)S(1)}, bf16[1,104,256]{2,1,0:T(8,128)(2,1)S(1)}, u32[]{:S(2)}, u32[]{:S(2)}) collective-permute-start(bf16[1,104,256]{2,1,0:T(8,128)(2,1)S(1)} %get-tuple-element.156), channel_id=1, source_target_pairs={{0,16},{1,17},{2,18},{3,19},{4,20},{5,21},{6,22},{7,23},{8,24},{9,... | collective-permute-start | bytes 159752 | tf_op jit(solution)/shard_map/ppermute | solution.py:670
  148.8 3.7 %collective-permute-start.26 = (f32[8,256]{1,0:T(8,128)S(1)}, f32[8,256]{1,0:T(8,128)S(1)}, u32[]{:S(2)}, u32[]{:S(2)}) collective-permute-start(f32[8,256]{1,0:T(8,128)S(1)} %add.118), channel_id=1, source_target_pairs={{0,2},{1,3},{2,0},{3,1},{4,6},{5,7},{6,4},{7,5},{8,10},{9,11},{10,... | collective-permute-start | bytes 24584 | tf_op jit(solution)/shard_map/ppermute | solution.py:644
  152.5 3.7 %collective-permute-start.27 = (f32[8,256]{1,0:T(8,128)S(1)}, f32[8,256]{1,0:T(8,128)S(1)}, u32[]{:S(2)}, u32[]{:S(2)}) collective-permute-start(f32[8,256]{1,0:T(8,128)S(1)} %add.119), channel_id=1, source_target_pairs={{0,4},{1,5},{2,6},{3,7},{4,0},{5,1},{6,2},{7,3},{8,12},{9,13},{10,... | collective-permute-start | bytes 24584 | tf_op jit(solution)/shard_map/ppermute | solution.py:644
  156.1 3.7 %collective-permute-start.28 = (f32[8,256]{1,0:T(8,128)S(1)}, f32[8,256]{1,0:T(8,128)S(1)}, u32[]{:S(2)}, u32[]{:S(2)}) collective-permute-start(f32[8,256]{1,0:T(8,128)S(1)} %add.120), channel_id=1, source_target_pairs={{0,8},{1,9},{2,10},{3,11},{4,12},{5,13},{6,14},{7,15},{8,0},{9,1},... | collective-permute-start | bytes 24584 | tf_op jit(solution)/shard_map/ppermute | solution.py:644
  159.8 4.6 %collective-permute-start.29 = (f32[8,256]{1,0:T(8,128)S(1)}, f32[8,256]{1,0:T(8,128)S(1)}, u32[]{:S(2)}, u32[]{:S(2)}) collective-permute-start(f32[8,256]{1,0:T(8,128)S(1)} %add.121), channel_id=1, source_target_pairs={{0,16},{1,17},{2,18},{3,19},{4,20},{5,21},{6,22},{7,23},{8,24},{9,... | collective-permute-start | bytes 24584 | tf_op jit(solution)/shard_map/ppermute | solution.py:644
  (28 other events, 266.0 us)

commit v3 on v2

--- a/solution.py
+++ b/solution.py
@@ -104,7 +104,7 @@
 
 
 def local_kernel(
-    info_ref, x_ref, e_ref, hot_ref, turned_ref, w_ref, vec_ref,
+    info_ref, x_ref, e_ref, hot_ref, turned_ref, w_ref, vec_ref, other_ref,
     out_ref, slope_ref, recip_ref, fall_ref, open_ref, bend_ref, bsrc_ref, sums_ref,
 ):
     group = x_ref.shape[0] // BLOCK
@@ -149,6 +149,14 @@
     kept = live * out
     add_rows(sums_ref, [col_sum(kept), col_sum(kept * out)])
 
+    @pl.when(pl.program_id(0) == 0)
+    def _():
+        sums_ref[2:4, :] = other_ref[0:2, :]
+        count = info_ref[1]
+        for place in range(2, info_ref.shape[0] - 2):
+            count = count + info_ref[place]
+        sums_ref[4:5, :] = jnp.full((1, out.shape[1]), count, jnp.int32).astype(f32)
+
 
 def head_masks(width):
     head = lax.broadcasted_iota(jnp.int32, (16, width), 1) // (width // HEADS)
@@ -166,6 +174,17 @@
 
 def side_stack(turned, masks):
     return jnp.concatenate([turned * mask for mask in masks], axis=1)
+
+
+def turned_product(turned, weight, nodes, size):
+    parts = []
+    for head in range(0, HEADS, 2):
+        both = mm(
+            turned[head * size : (head + 2) * size],
+            weight[nodes, head * BLOCK : (head + 2) * BLOCK],
+        )
+        parts += [both[:size, :BLOCK], both[size:, BLOCK:]]
+    return low(jnp.concatenate(parts, axis=0)).T
 
 
 def attend_kernel(
@@ -181,29 +200,25 @@
     k_ref[...] = keyed
     v_ref[...] = valued
     score_scale = (x.shape[1] // HEADS) ** (-0.5) * math.log2(math.e)
-    masks = head_masks(x.shape[1])
     tall = tall_masks(x.shape[1])
     queries_turned = queries.T
+    valued_turned = valued.T
+    size = x.shape[1] // HEADS
     raws = [
         mm(keyed[nodes_of(place)], side_stack(queries_turned[:, nodes_of(place)], tall))
         for place in range(group)
     ]
-    turns = []
     for place in range(group):
         nodes = nodes_of(place)
         bias = bias_ref[nodes, :]
-        turned = []
         for head in range(HEADS):
             cols = nodes_of(head)
             part = raws[place][:, cols] + bias
             part = jnp.exp2((part - jnp.max(part, axis=0, keepdims=True)) * score_scale)
-            part = low(part * (1.0 / jnp.sum(part, axis=0, keepdims=True)))
-            prob_ref[nodes, cols] = part
-            turned.append(part.T)
-        turns.append(jnp.concatenate(turned, axis=1))
+            prob_ref[nodes, cols] = low(part * (1.0 / jnp.sum(part, axis=0, keepdims=True)))
     for place in range(group):
         nodes = nodes_of(place)
-        att_ref[nodes, :] = low(mm(turns[place], head_stack(valued[nodes], masks)))
+        att_ref[nodes, :] = turned_product(valued_turned[:, nodes], prob_ref, nodes, size)
     out = x.astype(f32) + mm(att_ref[...], w_ref[8]) + vec_ref[4:5, :]
     out_ref[...] = out
     live = live_of(info_ref, pl.program_id(0) * group, group, out.shape[1])
@@ -213,7 +228,7 @@
 
 def mix_kernel(
     info_ref, local_ref, global_ref, cot_ref, sums_ref, w_ref, vec_ref,
-    low_ref, hlow_ref, slope_ref, lhat_ref, ghat_ref, mixed_ref, stat_ref,
+    low_ref, hlow_ref, hidden_ref, mixed_ref, stat_ref,
 ):
     group = local_ref.shape[0] // BLOCK
     width = local_ref.shape[1]
@@ -221,12 +236,10 @@
     count_row = sums[4:5]
     local_mean, local_rstd = norm_terms(sums, 0, count_row)
     global_mean, global_rstd = norm_terms(sums, 2, count_row)
-    local_hat = (local_ref[...] - local_mean) * local_rstd
-    global_hat = (global_ref[...] - global_mean) * global_rstd
-    lhat_ref[...] = low(local_hat)
-    ghat_ref[...] = low(global_hat)
-    local_norm = local_hat * vec_ref[5:6, :] + vec_ref[6:7, :]
-    global_norm = global_hat * vec_ref[7:8, :] + vec_ref[8:9, :]
+    local_gain = vec_ref[5:6, :] * local_rstd
+    global_gain = vec_ref[7:8, :] * global_rstd
+    local_norm = local_ref[...] * local_gain + (vec_ref[6:7, :] - local_mean * local_gain)
+    global_norm = global_ref[...] * global_gain + (vec_ref[8:9, :] - global_mean * global_gain)
     summed = low(local_norm).astype(f32) + low(global_norm).astype(f32)
     summed_low = low(summed)
     low_ref[...] = summed_low
@@ -235,10 +248,8 @@
         hidden = mm(summed_low, w_ref[9 + half]) + vec_ref[9 + half : 10 + half, :]
         sig_value = sig(hidden)
         hidden_low = low(hidden * sig_value)
+        hidden_ref[:, half * width : (half + 1) * width] = hidden
         hlow_ref[:, half * width : (half + 1) * width] = hidden_low
-        slope_ref[:, half * width : (half + 1) * width] = low(
-            sig_value * (1.0 + hidden * (1.0 - sig_value))
-        )
         mixed = mixed + mm(hidden_low, w_ref[11 + half])
     mixed_ref[...] = mixed
     live = live_of(info_ref, pl.program_id(0) * group, group, width)
@@ -247,6 +258,19 @@
     add_rows(
         stat_ref, [col_sum(kept), col_sum(kept * mixed), col_sum(d_norm), col_sum(d_norm * mixed)]
     )
+
+
+def hat_kernel(info_ref, local_ref, global_ref, sums_ref, lhat_ref, ghat_ref):
+    sums = sums_ref[...]
+    for value_ref, hat_ref, first in ((local_ref, lhat_ref, 0), (global_ref, ghat_ref, 2)):
+        mean, rstd = norm_terms(sums, first, sums[4:5])
+        hat_ref[...] = low((value_ref[...] - mean) * rstd)
+
+
+def slope_kernel(info_ref, hidden_ref, slope_ref):
+    hidden = hidden_ref[...]
+    sig_value = sig(hidden)
+    slope_ref[...] = low(sig_value * (1.0 + hidden * (1.0 - sig_value)))
 
 
 def mix_back_kernel(
@@ -375,7 +399,7 @@
 def attend_back_kernel(
     info_ref, dsum_ref, global_ref, q_ref, k_ref, v_ref, prob_ref, sums_ref,
     backs_ref, w_ref, vec_ref,
-    dqkv_ref, dlow_ref, stat_ref,
+    dqkv_ref, dlow_ref, stat_ref, score_ref,
 ):
     group = global_ref.shape[0] // BLOCK
     width = global_ref.shape[1]
@@ -393,27 +417,20 @@
         mm(v_ref[nodes_of(place), :], side_stack(turned_att[:, nodes_of(place)], tall))
         for place in range(group)
     ]
-    straights = []
-    turns = []
     for place in range(group):
         nodes = nodes_of(place)
-        straight = []
-        turned = []
         for head in range(HEADS):
             cols = nodes_of(head)
             prob = prob_ref[nodes, cols].astype(f32)
             part = d_probs[place][:, cols]
             inner = jnp.sum(prob * part, axis=0, keepdims=True)
             d_score = low(prob * ((part - inner) * score_scale))
-            straight.append(d_score)
-            turned.append(d_score.T)
-        straights.append(jnp.concatenate(straight, axis=1))
-        turns.append(jnp.concatenate(turned, axis=1))
+            score_ref[nodes, cols] = d_score
     for place in range(group):
         nodes = nodes_of(place)
-        dqkv_ref[nodes, :width] = low(mm(turns[place], head_stack(k_ref[nodes, :], masks)))
+        dqkv_ref[nodes, :width] = turned_product(k_ref[nodes, :].T, score_ref, nodes, width // HEADS)
         dqkv_ref[nodes, width : 2 * width] = low(
-            mm(straights[place], head_stack(q_ref[nodes, :], masks))
+            mm(score_ref[nodes, :], head_stack(q_ref[nodes, :], masks))
         )
         dqkv_ref[nodes, 2 * width :] = low(
             mm(prob_ref[nodes, :], head_stack(d_att[nodes], masks))
@@ -451,7 +468,7 @@
         for place, part in enumerate(parts):
             outs[0][place] = low(part[...])
     else:
-        pack(info_ref, parts, outs[0], outs[1])
+        pack(info_ref, parts, outs)
 
 
 def reach(order, index):
@@ -467,30 +484,32 @@
     return (chips, chips[1:-1] + chips[:1] + chips[-1:])
 
 
-def pack(info_ref, parts, keep_ref, send_ref):
-    slots = keep_ref.shape[0]
+def pack(info_ref, parts, outs):
+    half = outs[0].shape[0]
+    slots = 2 * half
     orders = chip_orders(2 * slots)
     core = info_ref[info_ref.shape[0] - 2]
     chip = info_ref[info_ref.shape[0] - 1]
     for slot in range(slots):
         near = [reach(order, slot) for order in orders]
-        for out_ref, owner in ((keep_ref, core), (send_ref, 1 - core)):
+        for out_ref, owner in zip(outs[slot // half :: 2], (core, 1 - core)):
             step = jnp.where(owner == 0, near[0], near[1])
             row = pl.multiple_of(16 * jnp.bitwise_xor(chip, step) + 8 * owner, 8)
             for first in range(0, len(parts), 2):
                 pair = [part[pl.ds(row, 8), :] for part in parts[first : first + 2]]
-                out_ref[slot, first * 8 : first * 8 + 8 * len(pair), :] = low(
+                out_ref[slot % half, first * 8 : first * 8 + 8 * len(pair), :] = low(
                     jnp.concatenate(pair, axis=0)
                 )
 
 
-def assemble_kernel(info_ref, held_ref, other_ref, out_ref):
-    slots, tall, _ = held_ref.shape
+def assemble_kernel(info_ref, near_ref, far_ref, near_other_ref, far_other_ref, out_ref):
+    half, tall, _ = near_ref.shape
+    slots = 2 * half
     orders = chip_orders(2 * slots)
     core = info_ref[info_ref.shape[0] - 2]
     chip = info_ref[info_ref.shape[0] - 1]
 
-    def fill(even_ref, odd_ref):
+    def fill(even_refs, odd_refs):
         for far in range(slots):
             even, odd = [
                 [slot for slot in range(slots) if reach(order, slot) == far][0] for order in orders
@@ -498,21 +517,22 @@
             row = pl.multiple_of(16 * jnp.bitwise_xor(chip, far), 16)
             for first in range(0, tall, 16):
                 size = min(16, tall - first)
-                upper = even_ref[even, first : first + size, :].astype(f32)
-                lower = odd_ref[odd, first : first + size, :].astype(f32)
-                for half in range(size // 8):
-                    rows = slice(half * 8, half * 8 + 8)
-                    out_ref[first // 8 + half, pl.ds(row, 16), :] = low(
+                part = slice(first, first + size)
+                upper = even_refs[even // half][even % half, part, :].astype(f32)
+                lower = odd_refs[odd // half][odd % half, part, :].astype(f32)
+                for step in range(size // 8):
+                    rows = slice(step * 8, step * 8 + 8)
+                    out_ref[first // 8 + step, pl.ds(row, 16), :] = low(
                         jnp.concatenate([upper[rows], lower[rows]], axis=0)
                     )
 
     @pl.when(core == 0)
     def _():
-        fill(held_ref, other_ref)
+        fill((near_ref, far_ref), (near_other_ref, far_other_ref))
 
     @pl.when(core != 0)
     def _():
-        fill(other_ref, held_ref)
+        fill((near_other_ref, far_other_ref), (near_ref, far_ref))
 
 
 def node_grad_kernel(
@@ -536,23 +556,58 @@
     edge_ref[...] = mm_back(dedge_ref[...], w_ref[2])
 
 
+def bias_rows(local_ref, attend_ref, inner_ref, wide_ref):
+    width = attend_ref.shape[1]
+    return jnp.concatenate(
+        [
+            local_ref[0:2, :],
+            wide_ref[0:1, :width],
+            wide_ref[0:1, width:],
+            attend_ref[0:1, :],
+            inner_ref[0:1, :width],
+            inner_ref[0:1, width:],
+            jnp.zeros((1, width), f32),
+        ],
+        axis=0,
+    )
+
+
+def last_kernel(
+    info_ref, kept_ref, got_ref, local_ref, attend_ref, inner_ref, wide_ref, out_ref
+):
+    biases = bias_rows(local_ref, attend_ref, inner_ref, wide_ref)
+    upper = low(biases).astype(f32)
+    for slot, extra in enumerate((upper, biases - upper)):
+        total = kept_ref[slot].astype(f32) + got_ref[slot].astype(f32)
+        out_ref[slot] = low(jnp.concatenate([total, extra], axis=0))
+
+
+def total_square(values):
+    return jnp.sum(jnp.sum(values * values, axis=0, keepdims=True), axis=1, keepdims=True)
+
+
+def pair_kernel(info_ref, mine_ref, got_ref, grad_ref, tail_ref):
+    rows = grad_ref.shape[1]
+    half = grad_ref.shape[2]
+    mine = [mine_ref[slot].astype(f32) for slot in range(2)]
+    got = [got_ref[slot].astype(f32) for slot in range(2)]
+    grad = mine[0][:rows] + got[1][:rows]
+    other = mine[1][:rows] + got[0][:rows]
+    grad_ref[0] = grad[:, :half]
+    grad_ref[1] = grad[:, half:]
+    tail_ref[...] = (mine[0][rows:] + mine[1][rows:]) + (got[0][rows:] + got[1][rows:])
+    tail_ref[7:8, :] = jnp.broadcast_to(total_square(grad) + total_square(other), (1, 2 * half))
+
+
 def square_kernel(
     info_ref, kept_ref, got_ref, local_ref, attend_ref, inner_ref, wide_ref, grad_ref, tail_ref
 ):
-    width = tail_ref.shape[1]
     grad = kept_ref[...].astype(f32) + got_ref[...].astype(f32)
     half = grad.shape[1] // 2
     grad_ref[0] = grad[:, :half]
     grad_ref[1] = grad[:, half:]
-    squares = grad * grad
-    square = jnp.sum(jnp.sum(squares, axis=0, keepdims=True), axis=1, keepdims=True)
-    tail_ref[0:2, :] = local_ref[0:2, :]
-    tail_ref[2:3, :] = wide_ref[0:1, :width]
-    tail_ref[3:4, :] = wide_ref[0:1, width:]
-    tail_ref[4:5, :] = attend_ref[0:1, :]
-    tail_ref[5:6, :] = inner_ref[0:1, :width]
-    tail_ref[6:7, :] = inner_ref[0:1, width:]
-    tail_ref[7:8, :] = jnp.broadcast_to(square, (1, width))
+    tail_ref[...] = bias_rows(local_ref, attend_ref, inner_ref, wide_ref)
+    tail_ref[7:8, :] = jnp.broadcast_to(total_square(grad), (1, tail_ref.shape[1]))
 
 
 def update_kernel(
@@ -609,7 +664,7 @@
     return pl.BlockSpec(shape, lambda step, info: zeros)
 
 
-def call(kernel, steps, info, inputs, outputs, scratch=(), room=12, cost=5):
+def call(kernel, steps, info, inputs, outputs, scratch=(), room=10, cost=5):
     in_specs = []
     arrays = []
     for array, spec in inputs:
@@ -684,17 +739,21 @@
         gathered = lax.all_gather(shard, axis_names, axis=1, tiled=True)
         return (gathered.reshape(mats, width, width), work(info))
     held = shard.reshape(1, mats * 8, width)
-    for number in reversed(range(len(chip_orders(total)[0]))):
-        got = swap_chips(held, number, total)
-        if number == 0:
-            got, done = beside(held, got, info, work)
-        held = jnp.concatenate([held, got], axis=0)
+    for number in reversed(range(1, len(chip_orders(total)[0]))):
+        held = jnp.concatenate([held, swap_chips(held, number, total)], axis=0)
+    got = swap_chips(held, 0, total)
     other = swap_with(held, 1, total)
+
+    def both(info):
+        return (work(info), other)
+
+    got, (done, other) = beside(held, got, info, both)
+    far_other = swap_with(got, 1, total)
     matrices = call(
         assemble_kernel,
         1,
         info,
-        [(held, None), (other, None)],
+        [(held, None), (got, None), (other, None), (far_other, None)],
         [((mats, width, width), bf16, None)],
     )[0]
     return (matrices, done)
@@ -716,18 +775,40 @@
     return (kept, got)
 
 
-def scatter_packed(kept, sent, total, info, works):
+def scatter_packed(kept, far_kept, sent, far_sent, total, info, works, biases):
+    far_got = swap_with(far_sent, 1, total)
     got = swap_with(sent, 1, total)
     results = []
-    for number in range(len(chip_orders(total)[0])):
-        half = kept.shape[0] // 2
-        sent = low(kept[half:].astype(f32) + got[half:].astype(f32))
-        kept = kept[:half].astype(f32) + got[:half].astype(f32)
+    rounds = len(chip_orders(total)[0])
+    for number in range(rounds - 1):
+        if number:
+            half = kept.shape[0] // 2
+            far_kept, far_got = kept[half:], got[half:]
+            kept, got = kept[:half], got[:half]
+        sent = low(far_kept.astype(f32) + far_got.astype(f32))
+        kept = kept.astype(f32) + got.astype(f32)
         got = swap_chips(sent, number, total)
         if number < len(works):
             got, done = beside(sent, got, info, works[number])
             results.append(done)
-    return ((kept[0], got[0]), results)
+    mine = call(
+        last_kernel,
+        1,
+        info,
+        [(array, None) for array in (kept, got, *biases)],
+        [((2, kept.shape[1] + 8, kept.shape[2]), bf16, None)],
+    )[0]
+    got = swap_chips(mine, rounds - 1, total)
+    grad_rows, tail = call(
+        pair_kernel,
+        1,
+        info,
+        [(mine, None), (got, None)],
+        [((2, kept.shape[1], kept.shape[2] // 2), f32, None), ((8, kept.shape[2]), f32, None)],
+    )
+    for step in steps_of(total)[:-1]:
+        tail = tail + swap_with(tail, step, total)
+    return (grad_rows, tail, results)
 
 
 def adamw(params, gradient, moment_one, moment_two, rate, decay):
@@ -771,6 +852,8 @@
     tall = group * BLOCK
     tall_edges = group * EB
     w_bf = low(weights)
+    own_nodes = own_half(node_feats, branch_index)
+    own_edges = own_half(edge_feats, branch_index)
     counts = jnp.sum(own_half(node_mask, branch_index).reshape(blocks, BLOCK), axis=1)
     info = jnp.concatenate(
         [(branch_index * steps)[None], counts, branch_index[None], lax.axis_index("rows")[None]]
@@ -803,18 +886,42 @@
         )
 
     matrices, (hot, turned, bias) = gather_matrices(w_bf, info, total, width, prep_work)
-    x_in = (node_feats, rows_spec(tall, width, 1))
-    e_in = (edge_feats, rows_spec(tall_edges, width, 1))
+    x_in = (own_nodes, node_spec)
+    e_in = (own_edges, edge_spec)
     mats_in = (matrices, None)
     vec_in = (vectors, None)
     node_f32 = ((rows, width), f32, node_spec)
     node_bf = ((rows, width), bf16, node_spec)
     sums_out = ((8, width), f32, None)
-    local_out, gate_slope, recip, fall, opened, bend, b_source, local_sums = call(
+    prob_spec = rows_spec(tall, HEADS * BLOCK)
+    global_out, queries, keyed, valued, attended, probs, global_sums = call(
+        attend_kernel,
+        steps,
+        info,
+        [x_in, (bias, rows_spec(tall, BLOCK)), mats_in, vec_in],
+        [
+            node_f32,
+            node_bf,
+            node_bf,
+            node_bf,
+            node_bf,
+            ((rows, HEADS * BLOCK), bf16, prob_spec),
+            sums_out,
+        ],
+    )
+    local_out, gate_slope, recip, fall, opened, bend, b_source, sums_part = call(
         local_kernel,
         steps,
         info,
-        [x_in, e_in, (hot, edge_spec), (turned, edge_spec), mats_in, vec_in],
+        [
+            x_in,
+            e_in,
+            (hot, edge_spec),
+            (turned, edge_spec),
+            mats_in,
+            vec_in,
+            (global_sums, None),
+        ],
         [
             node_f32,
             node_bf,
@@ -826,33 +933,11 @@
             sums_out,
         ],
     )
-    prob_spec = rows_spec(tall, HEADS * BLOCK)
-    global_out, queries, keyed, valued, attended, probs, global_sums = call(
-        attend_kernel,
-        steps,
-        info,
-        [x_in, (bias, rows_spec(tall, BLOCK)), mats_in, vec_in],
-        [
-            node_f32,
-            node_bf,
-            node_bf,
-            node_bf,
-            node_bf,
-            ((rows, HEADS * BLOCK), bf16, prob_spec),
-            sums_out,
-        ],
-    )
-    count_row = jnp.full((1, width), jnp.sum(counts).astype(f32))
-    sums = sum_small(
-        jnp.concatenate(
-            [local_sums[:2], global_sums[:2], count_row, jnp.zeros((3, width), f32)], axis=0
-        ),
-        total,
-    )
+    sums = sum_small(sums_part, total)
     sums_in = (sums, None)
     cot_in = (cotangent, node_spec)
     wide_spec = rows_spec(tall, 2 * width)
-    summed_low, hidden_low, hidden_slope, local_hat, global_hat, mixed, top_part = call(
+    summed_low, hidden_low, hidden, mixed, top_part = call(
         mix_kernel,
         steps,
         info,
@@ -860,14 +945,33 @@
         [
             node_bf,
             ((rows, 2 * width), bf16, wide_spec),
-            ((rows, 2 * width), bf16, wide_spec),
-            node_bf,
-            node_bf,
+            ((rows, 2 * width), f32, wide_spec),
             node_f32,
             sums_out,
         ],
     )
-    tops = sum_small(top_part, total)
+
+    def hat_work(info):
+        return call(
+            hat_kernel,
+            steps,
+            info,
+            [(local_out, node_spec), (global_out, node_spec), sums_in],
+            [node_bf, node_bf],
+        )
+
+    def slope_work(info):
+        return call(
+            slope_kernel,
+            steps,
+            info,
+            [(hidden, wide_spec)],
+            [((rows, 2 * width), bf16, wide_spec)],
+        )[0]
+
+    tops, ((local_hat, global_hat), hidden_slope) = sum_small(
+        top_part, total, info, [hat_work, slope_work]
+    )
     d_mixed, d_hidden, d_summed, back_part = call(
         mix_back_kernel,
         steps,
@@ -957,7 +1061,7 @@
     packed = in_rows(total, width)
     grad_outs = [((MATS, width, width), bf16, None)]
     if packed:
-        grad_outs = [((slots, MATS * 8, width), bf16, None)] * 2
+        grad_outs = [((slots // 2, MATS * 8, width), bf16, None)] * 4
     d_qkv, d_low, attend_bias = call(
         attend_back_kernel,
         steps,
@@ -975,14 +1079,15 @@
             vec_in,
         ],
         [((rows, 3 * width), bf16, dqkv_spec), node_bf, sums_out],
+        [pltpu.VMEM((tall, HEADS * BLOCK), bf16)],
     )
     *grads, wide_bias = call(
         branch_grad_kernel,
         1,
         info,
         [
-            (node_feats, pl.BlockSpec((rows, width), lambda step, info: (info[0] // steps, 0))),
-            (edge_feats, pl.BlockSpec((edges, width), lambda step, info: (info[0] // steps, 0))),
+            (own_nodes, None),
+            (own_edges, None),
             (attended, None),
             (d_node, None),
             (d_edge, None),
@@ -1028,22 +1133,25 @@
             [((edges, width), f32, edge_spec)],
         )[0]
 
+    biases = (local_bias, attend_bias, inner_bias, wide_bias)
     if packed:
-        grad_shard, (node_grad, edge_grad) = scatter_packed(
-            *grads, total, info, [node_work, edge_work]
+        grad_rows, tail, (node_grad, edge_grad) = scatter_packed(
+            *grads, total, info, [node_work, edge_work], biases
         )
     else:
         grad_shard = scatter_plain(grads[0], total)
         node_grad, edge_grad = node_work(info), edge_work(info)
-    grad_rows, tail_part = call(
-        square_kernel,
-        1,
-        info,
-        [(part, None) for part in grad_shard]
-        + [(local_bias, None), (attend_bias, None), (inner_bias, None), (wide_bias, None)],
-        [((2, grad_shard[0].shape[0], grad_shard[0].shape[1] // 2), f32, None), sums_out],
-    )
-    tail = sum_small(tail_part, total)
+        grad_rows, tail_part = call(
+            square_kernel,
+            1,
+            info,
+            [(array, None) for array in (*grad_shard, *biases)],
+            [
+                ((2, grad_shard[0].shape[0], grad_shard[0].shape[1] // 2), f32, None),
+                sums_out,
+            ],
+        )
+        tail = sum_small(tail_part, total)
     like_mats = (weights.shape, f32, None)
     like_vecs = (vectors.shape, f32, None)
     new_weights, first_w, second_w, new_vectors, first_v, second_v, norm = call(

time: 166 us -> 160 us (0.964)
  starting transfers between devices: 48.6 us -> 41.1 us
  waiting for transfers between devices: 52 us -> 55.6 us
  local copies, waits for them, and re-layouts: 4.85 us -> 3.08 us
    ppermute x22 -> x23, starting transfers between devices: 31.7 us -> 25.4 us  [swap_with(): lax.ppermute(values, axis_names, [(place, place ^ step) for place in rang...]
    ppermute x8, waiting for transfers between devices: 18.7 us -> 23.2 us  [swap_chips(): lax.ppermute(values, axis_names, [(place, place ^ orders[place % 2][numbe...]
    dynamic_slice x3 -> x5, local copies, waits for them, and re-layouts: 2.16 us -> 0.24 us  [own_half(): return lax.dynamic_slice_in_dim(values, branch_index * half, half, 0)]
    pallas_call x16 -> x19, Pallas kernels: 55.8 us -> 57.2 us  [call(): pl.pallas_call(kernel, grid_spec=pltpu.PrefetchScalarGridSpec(num_scalar_...]
    ppermute x22 -> x23, waiting for transfers between devices: 33.2 us -> 32.4 us  [swap_with(): lax.ppermute(values, axis_names, [(place, place ^ step) for place in rang...]
  transfers between devices with their start and end apart: 30 -> 31, of which waited for: 27 -> 27; matrix products, arithmetic and copies ran while one was open for 2% -> 2% of each run, Pallas kernels for 10% -> 12%
where the time goes in v3:
time: 160 us
  Pallas kernels  57.2 us (36%)
  waiting for transfers between devices  55.6 us (35%)
  starting transfers between devices  41.1 us (26%)
  local copies, waits for them, and re-layouts  3.08 us (2%)
  other arithmetic  1.69 us (1%)
    pallas_call x19, Pallas kernels, call(): pl.pallas_call(kernel, grid_spec=pltpu.PrefetchScalarGridSpec(num_scalar_...  57.2 us
    ppermute x23, waiting for transfers between devices, swap_with(): lax.ppermute(values, axis_names, [(place, place ^ step) for place in rang...  32.4 us
    ppermute x23, starting transfers between devices, swap_with(): lax.ppermute(values, axis_names, [(place, place ^ step) for place in rang...  25.4 us
    ppermute x8, waiting for transfers between devices, swap_chips(): lax.ppermute(values, axis_names, [(place, place ^ orders[place % 2][numbe...  23.2 us
    ppermute x8, starting transfers between devices, swap_chips(): lax.ppermute(values, axis_names, [(place, place ^ orders[place % 2][numbe...  15.8 us
  transfers between devices with their start and end apart: 31, of which 27 were waited for; matrix products, arithmetic and copies ran while one was open for 2% of the time, Pallas kernels for 12%

profile of v3, /device:TPU:0, one launch (start us, length us, event | category | flops | bytes accessed | tf_op | source)
XLA Modules:
  0.0 159.8 jit_solution(13919225976456864138)
XLA Ops:
  1.8 4.1 %collective-permute-start = (bf16[1,104,256]{2,1,0:T(8,128)(2,1)S(1)}, bf16[1,104,256]{2,1,0:T(8,128)(2,1)S(1)}, u32[]{:S(2)}, u32[]{:S(2)}) collective-permute-start(bf16[1,104,256]{2,1,0:T(8,128)(2,1)S(1)} %reshape.42), channel_id=1, source_target_pairs={{0,16},{1,17},{2,18},{3,19},{4,20},{5,21},{6,22},{7,23},{8,24},{9,... | collective-permute-start | bytes 159752 | tf_op jit(solution)/shard_map/ppermute | solution.py:725
  10.1 3.4 %collective-permute-done.1 = bf16[2,104,256]{2,1,0:T(8,128)(2,1)S(1)} collective-permute-done((bf16[2,104,256]{2,1,0:T(8,128)(2,1)S(1)}, bf16[2,104,256]{2,1,0:T(8,128)(2,1)S(1)}, u32[]{:S(2)}, u32[]{:S(2)}) %collective-permute-start.1) | collective-permute-done | bytes 106528 | tf_op jit(solution)/shard_map/ppermute | solution.py:725
  16.8 2.6 %collective-permute-done.2 = bf16[4,104,256]{2,1,0:T(8,128)(2,1)S(1)} collective-permute-done((bf16[4,104,256]{2,1,0:T(8,128)(2,1)S(1)}, bf16[4,104,256]{2,1,0:T(8,128)(2,1)S(1)}, u32[]{:S(2)}, u32[]{:S(2)}) %collective-permute-start.2) | collective-permute-done | bytes 213024 | tf_op jit(solution)/shard_map/ppermute | solution.py:725
  22.0 3.0 %prep_kernel.1 = (bf16[4096,256]{1,0:T(8,128)(2,1)}, bf16[4096,256]{1,0:T(8,128)(2,1)}, f32[2048,128]{1,0:T(8,128)S(1)}) custom-call(s32[19]{0:T(128)S(1)} %pad_add_fusion.info_ref, s32[2,8,256]{2,1,0:T(8,128)S(1)} %reshape.43.src_ref, s32[2,8,256]{2,1,0:T(8,128)S(1)} %reshape.44.dst_ref, s32[2,8,256]{2,1,0:T(8,128)S(1)} %reshape.45.mask_ref, ...), custom_call_target="tpu_custom_call" | custom-call | flops 5000000000 | bytes 5000000 | tf_op jit(solution)/shard_map/prep_kernel/pallas_call | solution.py:678
  25.0 3.5 %collective-permute-done.3.far_ref = bf16[8,104,256]{2,1,0:T(8,128)(2,1)S(1)} collective-permute-done((bf16[8,104,256]{2,1,0:T(8,128)(2,1)}, bf16[8,104,256]{2,1,0:T(8,128)(2,1)S(1)}, u32[]{:S(2)}, u32[]{:S(2)}) %collective-permute-start.3) | collective-permute-done | bytes 426016 | tf_op jit(solution)/shard_map/ppermute | solution.py:725
  30.9 6.2 %attend_kernel.1 = (f32[2048,256]{1,0:T(8,128)S(1)}, bf16[2048,256]{1,0:T(8,128)(2,1)S(1)}, bf16[2048,256]{1,0:T(8,128)(2,1)S(1)}, bf16[2048,256]{1,0:T(8,128)(2...) custom-call(s32[19]{0:T(128)S(1)} %pad_add_fusion.info_ref, ...), custom_call_target="tpu_custom_call" | custom-call | flops 5000000000 | bytes 5000000 | tf_op jit(solution)/shard_map/attend_kernel/pallas_call | solution.py:678
  37.1 6.6 %local_kernel.1 = (f32[2048,256]{1,0:T(8,128)S(1)}, bf16[2048,256]{1,0:T(8,128)(2,1)S(1)}, bf16[2048,256]{1,0:T(8,128)(2,1)S(1)}, bf16[2048,256]{1,0:T(8,128)(2,...) custom-call(s32[19]{0:T(128)S(1)} %pad_add_fusion.info_ref, ...), custom_call_target="tpu_custom_call" | custom-call | flops 5000000000 | bytes 5000000 | tf_op jit(solution)/shard_map/local_kernel/pallas_call | solution.py:678
  53.6 2.4 %collective-permute-done.9 = f32[8,256]{1,0:T(8,128)S(1)} collective-permute-done((f32[8,256]{1,0:T(8,128)S(1)}, f32[8,256]{1,0:T(8,128)S(1)}, u32[]{:S(2)}, u32[]{:S(2)}) %collective-permute-start.9) | collective-permute-done | bytes 8224 | tf_op jit(solution)/shard_map/ppermute | solution.py:699
  56.0 2.4 %collective-permute-start.10 = (f32[8,256]{1,0:T(8,128)S(1)}, f32[8,256]{1,0:T(8,128)S(1)}, u32[]{:S(2)}, u32[]{:S(2)}) collective-permute-start(f32[8,256]{1,0:T(8,128)S(1)} %add.91), channel_id=1, source_target_pairs={{0,16},{1,17},{2,18},{3,19},{4,20},{5,21},{6,22},{7,23},{8,24},{9,... | collective-permute-start | bytes 24584 | tf_op jit(solution)/shard_map/ppermute | solution.py:699
  58.3 2.2 %collective-permute-done.10 = f32[8,256]{1,0:T(8,128)S(1)} collective-permute-done((f32[8,256]{1,0:T(8,128)S(1)}, f32[8,256]{1,0:T(8,128)S(1)}, u32[]{:S(2)}, u32[]{:S(2)}) %collective-permute-start.10) | collective-permute-done | bytes 8224 | tf_op jit(solution)/shard_map/ppermute | solution.py:699
  60.5 3.2 %mix_kernel.1 = (bf16[2048,256]{1,0:T(8,128)(2,1)S(1)}, bf16[2048,512]{1,0:T(8,128)(2,1)S(1)}, f32[2048,512]{1,0:T(8,128)S(1)}, f32[2048,256]{1,0:T(8,128)S(1)}, f32[8,256]{1,0:T(8,128)S(1)}) custom-call(s32[19]{0:T(128)S(1)} %pad_add_fusion.info_ref, f32[2048,256]{1,0:T(8,128)S(1)} %get-tuple-element.100.local_ref, ...), custom_call_target="tpu_custom_call" | custom-call | flops 5000000000 | bytes 5000000 | tf_op jit(solution)/shard_map/mix_kernel/pallas_call | solution.py:678
  73.7 2.4 %collective-permute-done.14 = f32[8,256]{1,0:T(8,128)S(1)} collective-permute-done((f32[8,256]{1,0:T(8,128)S(1)}, f32[8,256]{1,0:T(8,128)S(1)}, u32[]{:S(2)}, u32[]{:S(2)}) %collective-permute-start.14) | collective-permute-done | bytes 8224 | tf_op jit(solution)/shard_map/ppermute | solution.py:699
  78.3 2.4 %collective-permute-done.15 = f32[8,256]{1,0:T(8,128)S(1)} collective-permute-done((f32[8,256]{1,0:T(8,128)S(1)}, f32[8,256]{1,0:T(8,128)S(1)}, u32[]{:S(2)}, u32[]{:S(2)}) %collective-permute-start.15) | collective-permute-done | bytes 8224 | tf_op jit(solution)/shard_map/ppermute | solution.py:699
  80.7 3.0 %mix_back_kernel.1 = (bf16[2048,256]{1,0:T(8,128)(2,1)S(1)}, bf16[2048,512]{1,0:T(8,128)(2,1)S(1)}, bf16[2048,256]{1,0:T(8,128)(2,1)S(1)}, f32[8,256]{1,0:T(8,128)S(1)}) custom-call(s32[19]{0:T(128)S(1)} %pad_add_fusion.info_ref, f32[2048,256]{1,0:T(8,128)S(1)} %get-tuple-element.103.mixed_ref, bf16[2048,512]{1,0:T(8,128)(2,1)S(1)} %slope_kernel.1.slope_ref, ...), custom_call_target="tpu_custom_call" | custom-call | flops 5000000000 | bytes 5000000 | tf_op jit(solution)/shard_map/mix_back_kernel/pallas_call | solution.py:678
  98.3 2.4 %collective-permute-done.20 = f32[8,256]{1,0:T(8,128)S(1)} collective-permute-done((f32[8,256]{1,0:T(8,128)S(1)}, f32[8,256]{1,0:T(8,128)S(1)}, u32[]{:S(2)}, u32[]{:S(2)}) %collective-permute-start.20) | collective-permute-done | bytes 8224 | tf_op jit(solution)/shard_map/ppermute | solution.py:699
  100.7 7.6 %attend_back_kernel.1 = (bf16[2048,768]{1,0:T(8,128)(2,1)S(1)}, bf16[2048,256]{1,0:T(8,128)(2,1)S(1)}, f32[8,256]{1,0:T(8,128)S(1)}) custom-call(s32[19]{0:T(128)S(1)} %pad_add_fusion.info_ref, bf16[2048,256]{1,0:T(8,128)(2,1)S(1)} %get-tuple-element.129.dsum_ref, bf16[2048,256]{1,0:T(8,128)(2,1)S(1)} %get-tuple-element.113.ghat_ref.global_ref, ...), custom_call_target="tpu_custom_call" | custom-call | flops 5000000000 | bytes 5000000 | tf_op jit(solution)/shard_map/attend_back_kernel/pallas_call | solution.py:678
  108.3 4.6 %local_back_kernel.1 = (bf16[2048,1024]{1,0:T(8,128)(2,1)S(1)}, bf16[4096,256]{1,0:T(8,128)(2,1)S(1)}, f32[8,256]{1,0:T(8,128)S(1)}) custom-call(s32[19]{0:T(128)S(1)} %pad_add_fusion.info_ref, bf16[2048,256]{1,0:T(8,128)(2,1)S(1)} %get-tuple-element.129.dsum_ref, bf16[2048,256]{1,0:T(8,128)(2,1)S(1)} %get-tuple-element.112.lhat_ref.local_ref, ...), custom_call_target="tpu_custom_call" | custom-call | flops 5000000000 | bytes 5000000 | tf_op jit(solution)/shard_map/local_back_kernel/pallas_call | solution.py:678
  112.9 3.9 %branch_grad_kernel.1 = (bf16[8,104,256]{2,1,0:T(8,128)(2,1)S(1)}, bf16[8,104,256]{2,1,0:T(8,128)(2,1)S(1)}, bf16[8,104,256]{2,1,0:T(8,128)(2,1)S(1)}, bf16[8,104,256]{2,1,0:T(8,128)(2,1)S(1)}, f32[8,512]{1,0:T(8,128)S(1)}) custom-call(s32[19]{0:T(128)S(1)} %pad_add_fusion.info_ref, bf16[2048,256]{1,0:T(8,128)(2,1)S(1)} %constant_dynamic-slice_fusion.1.x_ref, ...), custom_call_target="tpu_custom_call" | custom-call | flops 5000000000 | bytes 5000000 | tf_op jit(solution)/shard_map/branch_grad_kernel/pallas_call | solution.py:678
  120.3 4.3 %node_grad_kernel.1 = f32[2048,256]{1,0:T(8,128)} custom-call(s32[19]{0:T(128)S(1)} %pad_add_fusion.info_ref, bf16[2048,256]{1,0:T(8,128)(2,1)S(1)} %get-tuple-element.129.dsum_ref, bf16[2048,256]{1,0:T(8,128)(2,1)S(1)} %get-tuple-element.112.lhat_ref.local_ref, bf16[2048,256]{1,0:T(8,128)(2,1)S(1)} %get-tuple-element.113.ghat_ref.global_ref, ...), custom_call_target="tpu_custom_call" | custom-call | flops 5000000000 | bytes 5000000 | tf_op jit(solution)/shard_map/node_grad_kernel/pallas_call | solution.py:678
  124.6 2.3 %collective-permute-done.22 = bf16[8,104,256]{2,1,0:T(8,128)(2,1)S(1)} collective-permute-done((bf16[8,104,256]{2,1,0:T(8,128)(2,1)S(1)}, bf16[8,104,256]{2,1,0:T(8,128)(2,1)S(1)}, u32[]{:S(2)}, u32[]{:S(2)}) %collective-permute-start.22) | collective-permute-done | bytes 426016 | tf_op jit(solution)/shard_map/ppermute | solution.py:725
  128.6 3.0 %edge_grad_kernel.1 = f32[4096,256]{1,0:T(8,128)} custom-call(s32[19]{0:T(128)S(1)} %pad_add_fusion.info_ref, bf16[4096,256]{1,0:T(8,128)(2,1)S(1)} %get-tuple-element.138.dedge_ref, bf16[13,256,256]{2,1,0:T(8,128)(2,1)S(1)} %assemble_kernel.1.w_ref), custom_call_target="tpu_custom_call" | custom-call | flops 5000000000 | bytes 5000000 | tf_op jit(solution)/shard_map/edge_grad_kernel/pallas_call | solution.py:678
  134.0 3.7 %collective-permute-done.25.got_ref = bf16[2,104,256]{2,1,0:T(8,128)(2,1)S(1)} collective-permute-done((bf16[2,104,256]{2,1,0:T(8,128)(2,1)S(1)}, bf16[2,104,256]{2,1,0:T(8,128)(2,1)S(1)}, u32[]{:S(2)}, u32[]{:S(2)}) %collective-permute-start.25) | collective-permute-done | bytes 106528 | tf_op jit(solution)/shard_map/ppermute | solution.py:725
  140.5 4.8 %collective-permute-done.26.got_ref = bf16[2,112,256]{2,1,0:T(8,128)(2,1)S(1)} collective-permute-done((bf16[2,112,256]{2,1,0:T(8,128)(2,1)S(1)}, bf16[2,112,256]{2,1,0:T(8,128)(2,1)S(1)}, u32[]{:S(2)}, u32[]{:S(2)}) %collective-permute-start.26) | collective-permute-done | bytes 114720 | tf_op jit(solution)/shard_map/ppermute | solution.py:725
  154.7 3.4 %collective-permute-done.30 = f32[8,256]{1,0:T(8,128)S(1)} collective-permute-done((f32[8,256]{1,0:T(8,128)S(1)}, f32[8,256]{1,0:T(8,128)S(1)}, u32[]{:S(2)}, u32[]{:S(2)}) %collective-permute-start.30) | collective-permute-done | bytes 8224 | tf_op jit(solution)/shard_map/ppermute | solution.py:699
  (135 shorter events, 71.4 us)
Async XLA Ops:
  1.8 6.8 %collective-permute-start = (bf16[1,104,256]{2,1,0:T(8,128)(2,1)S(1)}, bf16[1,104,256]{2,1,0:T(8,128)(2,1)S(1)}, u32[]{:S(2)}, u32[]{:S(2)}) collective-permute-start(bf16[1,104,256]{2,1,0:T(8,128)(2,1)S(1)} %reshape.42), channel_id=1, source_target_pairs={{0,16},{1,17},{2,18},{3,19},{4,20},{5,21},{6,22},{7,23},{8,24},{9,... | collective-permute-start | bytes 159752 | tf_op jit(solution)/shard_map/ppermute | solution.py:725
  8.6 4.8 %collective-permute-start.1 = (bf16[2,104,256]{2,1,0:T(8,128)(2,1)S(1)}, bf16[2,104,256]{2,1,0:T(8,128)(2,1)S(1)}, u32[]{:S(2)}, u32[]{:S(2)}) collective-permute-start(bf16[2,104,256]{2,1,0:T(8,128)(2,1)S(1)} %pad_maximum_fusion.1), channel_id=1, source_target_pairs={{0,8},{1,3},{2,10},{3,1},{4,12},{5,7},{6,14},{7,5},{8,0},{9,11},{1... | collective-permute-start | bytes 319496 | tf_op jit(solution)/shard_map/ppermute | solution.py:725
  13.5 5.9 %collective-permute-start.2 = (bf16[4,104,256]{2,1,0:T(8,128)(2,1)S(1)}, bf16[4,104,256]{2,1,0:T(8,128)(2,1)S(1)}, u32[]{:S(2)}, u32[]{:S(2)}) collective-permute-start(bf16[4,104,256]{2,1,0:T(8,128)(2,1)S(1)} %pad_maximum_fusion), channel_id=1, source_target_pairs={{0,4},{1,9},{2,6},{3,11},{4,0},{5,13},{6,2},{7,15},{8,12},{9,1},{1... | collective-permute-start | bytes 638984 | tf_op jit(solution)/shard_map/ppermute | solution.py:725
  20.1 4.9 %collective-permute-start.4 = (bf16[8,104,256]{2,1,0:T(8,128)(2,1)}, bf16[8,104,256]{2,1,0:T(8,128)(2,1)S(1)}, u32[]{:S(2)}, u32[]{:S(2)}) collective-permute-start(bf16[8,104,256]{2,1,0:T(8,128)(2,1)} %constant_dynamic-update-slice_fusion.near_ref), channel_id=1, source_target_pairs={{0,1},{1,0},{2,3},{3,2},{4,5},{5,4},{6,7},{7,6},{8,9},{9,8},{10,11... | collective-permute-start | bytes 1277960 | tf_op jit(solution)/shard_map/ppermute | solution.py:699
  20.1 8.3 %collective-permute-start.3 = (bf16[8,104,256]{2,1,0:T(8,128)(2,1)}, bf16[8,104,256]{2,1,0:T(8,128)(2,1)S(1)}, u32[]{:S(2)}, u32[]{:S(2)}) collective-permute-start(bf16[8,104,256]{2,1,0:T(8,128)(2,1)} %constant_dynamic-update-slice_fusion.near_ref), channel_id=1, source_target_pairs={{0,2},{1,5},{2,0},{3,7},{4,6},{5,1},{6,4},{7,3},{8,10},{9,13},{10,... | collective-permute-start | bytes 1277960 | tf_op jit(solution)/shard_map/ppermute | solution.py:725
  45.0 3.7 %collective-permute-start.7 = (f32[8,256]{1,0:T(8,128)S(1)}, f32[8,256]{1,0:T(8,128)S(1)}, u32[]{:S(2)}, u32[]{:S(2)}) collective-permute-start(f32[8,256]{1,0:T(8,128)S(1)} %add.88), channel_id=1, source_target_pairs={{0,2},{1,3},{2,0},{3,1},{4,6},{5,7},{6,4},{7,5},{8,10},{9,11},{10,... | collective-permute-start | bytes 24584 | tf_op jit(solution)/shard_map/ppermute | solution.py:699
  48.7 3.7 %collective-permute-start.8 = (f32[8,256]{1,0:T(8,128)S(1)}, f32[8,256]{1,0:T(8,128)S(1)}, u32[]{:S(2)}, u32[]{:S(2)}) collective-permute-start(f32[8,256]{1,0:T(8,128)S(1)} %add.89), channel_id=1, source_target_pairs={{0,4},{1,5},{2,6},{3,7},{4,0},{5,1},{6,2},{7,3},{8,12},{9,13},{10,... | collective-permute-start | bytes 24584 | tf_op jit(solution)/shard_map/ppermute | solution.py:699
  52.3 3.7 %collective-permute-start.9 = (f32[8,256]{1,0:T(8,128)S(1)}, f32[8,256]{1,0:T(8,128)S(1)}, u32[]{:S(2)}, u32[]{:S(2)}) collective-permute-start(f32[8,256]{1,0:T(8,128)S(1)} %add.90), channel_id=1, source_target_pairs={{0,8},{1,9},{2,10},{3,11},{4,12},{5,13},{6,14},{7,15},{8,0},{9,1},... | collective-permute-start | bytes 24584 | tf_op jit(solution)/shard_map/ppermute | solution.py:699
  56.0 4.5 %collective-permute-start.10 = (f32[8,256]{1,0:T(8,128)S(1)}, f32[8,256]{1,0:T(8,128)S(1)}, u32[]{:S(2)}, u32[]{:S(2)}) collective-permute-start(f32[8,256]{1,0:T(8,128)S(1)} %add.91), channel_id=1, source_target_pairs={{0,16},{1,17},{2,18},{3,19},{4,20},{5,21},{6,22},{7,23},{8,24},{9,... | collective-permute-start | bytes 24584 | tf_op jit(solution)/shard_map/ppermute | solution.py:699
  65.0 3.7 %collective-permute-start.12 = (f32[8,256]{1,0:T(8,128)S(1)}, f32[8,256]{1,0:T(8,128)S(1)}, u32[]{:S(2)}, u32[]{:S(2)}) collective-permute-start(f32[8,256]{1,0:T(8,128)S(1)} %add.93), channel_id=1, source_target_pairs={{0,2},{1,3},{2,0},{3,1},{4,6},{5,7},{6,4},{7,5},{8,10},{9,11},{10,... | collective-permute-start | bytes 24584 | tf_op jit(solution)/shard_map/ppermute | solution.py:699
  68.7 3.7 %collective-permute-start.13 = (f32[8,256]{1,0:T(8,128)S(1)}, f32[8,256]{1,0:T(8,128)S(1)}, u32[]{:S(2)}, u32[]{:S(2)}) collective-permute-start(f32[8,256]{1,0:T(8,128)S(1)} %add.94), channel_id=1, source_target_pairs={{0,4},{1,5},{2,6},{3,7},{4,0},{5,1},{6,2},{7,3},{8,12},{9,13},{10,... | collective-permute-start | bytes 24584 | tf_op jit(solution)/shard_map/ppermute | solution.py:699
  72.4 3.7 %collective-permute-start.14 = (f32[8,256]{1,0:T(8,128)S(1)}, f32[8,256]{1,0:T(8,128)S(1)}, u32[]{:S(2)}, u32[]{:S(2)}) collective-permute-start(f32[8,256]{1,0:T(8,128)S(1)} %add.95), channel_id=1, source_target_pairs={{0,8},{1,9},{2,10},{3,11},{4,12},{5,13},{6,14},{7,15},{8,0},{9,1},... | collective-permute-start | bytes 24584 | tf_op jit(solution)/shard_map/ppermute | solution.py:699
  76.1 4.5 %collective-permute-start.15 = (f32[8,256]{1,0:T(8,128)S(1)}, f32[8,256]{1,0:T(8,128)S(1)}, u32[]{:S(2)}, u32[]{:S(2)}) collective-permute-start(f32[8,256]{1,0:T(8,128)S(1)} %add.96), channel_id=1, source_target_pairs={{0,16},{1,17},{2,18},{3,19},{4,20},{5,21},{6,22},{7,23},{8,24},{9,... | collective-permute-start | bytes 24584 | tf_op jit(solution)/shard_map/ppermute | solution.py:699
  84.9 3.8 %collective-permute-start.17 = (f32[8,256]{1,0:T(8,128)S(1)}, f32[8,256]{1,0:T(8,128)S(1)}, u32[]{:S(2)}, u32[]{:S(2)}) collective-permute-start(f32[8,256]{1,0:T(8,128)S(1)} %add.98), channel_id=1, source_target_pairs={{0,2},{1,3},{2,0},{3,1},{4,6},{5,7},{6,4},{7,5},{8,10},{9,11},{10,... | collective-permute-start | bytes 24584 | tf_op jit(solution)/shard_map/ppermute | solution.py:699
  88.8 3.7 %collective-permute-start.18 = (f32[8,256]{1,0:T(8,128)S(1)}, f32[8,256]{1,0:T(8,128)S(1)}, u32[]{:S(2)}, u32[]{:S(2)}) collective-permute-start(f32[8,256]{1,0:T(8,128)S(1)} %add.99), channel_id=1, source_target_pairs={{0,4},{1,5},{2,6},{3,7},{4,0},{5,1},{6,2},{7,3},{8,12},{9,13},{10,... | collective-permute-start | bytes 24584 | tf_op jit(solution)/shard_map/ppermute | solution.py:699
  92.5 3.7 %collective-permute-start.19 = (f32[8,256]{1,0:T(8,128)S(1)}, f32[8,256]{1,0:T(8,128)S(1)}, u32[]{:S(2)}, u32[]{:S(2)}) collective-permute-start(f32[8,256]{1,0:T(8,128)S(1)} %add.100), channel_id=1, source_target_pairs={{0,8},{1,9},{2,10},{3,11},{4,12},{5,13},{6,14},{7,15},{8,0},{9,1},... | collective-permute-start | bytes 24584 | tf_op jit(solution)/shard_map/ppermute | solution.py:699
  96.1 4.5 %collective-permute-start.20 = (f32[8,256]{1,0:T(8,128)S(1)}, f32[8,256]{1,0:T(8,128)S(1)}, u32[]{:S(2)}, u32[]{:S(2)}) collective-permute-start(f32[8,256]{1,0:T(8,128)S(1)} %add.101), channel_id=1, source_target_pairs={{0,16},{1,17},{2,18},{3,19},{4,20},{5,21},{6,22},{7,23},{8,24},{9,... | collective-permute-start | bytes 24584 | tf_op jit(solution)/shard_map/ppermute | solution.py:699
  118.7 8.2 %collective-permute-start.22 = (bf16[8,104,256]{2,1,0:T(8,128)(2,1)S(1)}, bf16[8,104,256]{2,1,0:T(8,128)(2,1)S(1)}, u32[]{:S(2)}, u32[]{:S(2)}) collective-permute-start(bf16[8,104,256]{2,1,0:T(8,128)(2,1)S(1)} %add_convert_fusion), channel_id=1, source_target_pairs={{0,2},{1,5},{2,0},{3,7},{4,6},{5,1},{6,4},{7,3},{8,10},{9,13},{10,... | collective-permute-start | bytes 1277960 | tf_op jit(solution)/shard_map/ppermute | solution.py:725
  127.0 5.9 %collective-permute-start.24 = (bf16[4,104,256]{2,1,0:T(8,128)(2,1)S(1)}, bf16[4,104,256]{2,1,0:T(8,128)(2,1)S(1)}, u32[]{:S(2)}, u32[]{:S(2)}) collective-permute-start(bf16[4,104,256]{2,1,0:T(8,128)(2,1)S(1)} %get-tuple-element.171), channel_id=1, source_target_pairs={{0,4},{1,9},{2,6},{3,11},{4,0},{5,13},{6,2},{7,15},{8,12},{9,1},{1... | collective-permute-start | bytes 638984 | tf_op jit(solution)/shard_map/ppermute | solution.py:725
  133.0 4.8 %collective-permute-start.25 = (bf16[2,104,256]{2,1,0:T(8,128)(2,1)S(1)}, bf16[2,104,256]{2,1,0:T(8,128)(2,1)S(1)}, u32[]{:S(2)}, u32[]{:S(2)}) collective-permute-start(bf16[2,104,256]{2,1,0:T(8,128)(2,1)S(1)} %get-tuple-element.172), channel_id=1, source_target_pairs={{0,8},{1,3},{2,10},{3,1},{4,12},{5,7},{6,14},{7,5},{8,0},{9,11},{1... | collective-permute-start | bytes 319496 | tf_op jit(solution)/shard_map/ppermute | solution.py:725
  138.4 7.0 %collective-permute-start.26 = (bf16[2,112,256]{2,1,0:T(8,128)(2,1)S(1)}, bf16[2,112,256]{2,1,0:T(8,128)(2,1)S(1)}, u32[]{:S(2)}, u32[]{:S(2)}) collective-permute-start(bf16[2,112,256]{2,1,0:T(8,128)(2,1)S(1)} %last_kernel.1.mine_ref), channel_id=1, source_target_pairs={{0,16},{1,17},{2,18},{3,19},{4,20},{5,21},{6,22},{7,23},{8,24},{9,... | collective-permute-start | bytes 344072 | tf_op jit(solution)/shard_map/ppermute | solution.py:725
  147.2 3.7 %collective-permute-start.28 = (f32[8,256]{1,0:T(8,128)S(1)}, f32[8,256]{1,0:T(8,128)S(1)}, u32[]{:S(2)}, u32[]{:S(2)}) collective-permute-start(f32[8,256]{1,0:T(8,128)S(1)} %add.109), channel_id=1, source_target_pairs={{0,2},{1,3},{2,0},{3,1},{4,6},{5,7},{6,4},{7,5},{8,10},{9,11},{10,... | collective-permute-start | bytes 24584 | tf_op jit(solution)/shard_map/ppermute | solution.py:699
  150.8 3.7 %collective-permute-start.29 = (f32[8,256]{1,0:T(8,128)S(1)}, f32[8,256]{1,0:T(8,128)S(1)}, u32[]{:S(2)}, u32[]{:S(2)}) collective-permute-start(f32[8,256]{1,0:T(8,128)S(1)} %add.110), channel_id=1, source_target_pairs={{0,4},{1,5},{2,6},{3,7},{4,0},{5,1},{6,2},{7,3},{8,12},{9,13},{10,... | collective-permute-start | bytes 24584 | tf_op jit(solution)/shard_map/ppermute | solution.py:699
  154.5 3.7 %collective-permute-start.30 = (f32[8,256]{1,0:T(8,128)S(1)}, f32[8,256]{1,0:T(8,128)S(1)}, u32[]{:S(2)}, u32[]{:S(2)}) collective-permute-start(f32[8,256]{1,0:T(8,128)S(1)} %add.111), channel_id=1, source_target_pairs={{0,8},{1,9},{2,10},{3,11},{4,12},{5,13},{6,14},{7,15},{8,0},{9,1},... | collective-permute-start | bytes 24584 | tf_op jit(solution)/shard_map/ppermute | solution.py:699
  (25 other events, 197.0 us)

commit v4 on v3

--- a/solution.py
+++ b/solution.py
@@ -14,6 +14,8 @@
 MATS = 13
 STEP = 7
 GROUP = 8
+BACK_ROOM = 12
+FRONT_ROOM = 12
 
 eps_norm = 1e-05
 clip_limit = 1.0
@@ -103,9 +105,9 @@
         )
 
 
-def local_kernel(
-    info_ref, x_ref, e_ref, hot_ref, turned_ref, w_ref, vec_ref, other_ref,
-    out_ref, slope_ref, recip_ref, fall_ref, open_ref, bend_ref, bsrc_ref, sums_ref,
+def local_steps(
+    info_ref, x_ref, e_ref, hot_ref, turned_ref, w_ref, vec_ref,
+    out_ref, slope_ref, recip_ref, fall_ref, open_ref, bend_ref, bsrc_ref, stats,
 ):
     group = x_ref.shape[0] // BLOCK
     x = x_ref[...]
@@ -121,6 +123,7 @@
         hot = hot_ref[edges_of(place), :]
         gates.append(mm(hot, jnp.concatenate([d_part[nodes], e_part[nodes]], axis=0)))
         picks.append(mm(hot[:, BLOCK:], b_part[nodes]))
+    yield
     sums = []
     for place in range(group):
         edges = edges_of(place)
@@ -134,6 +137,7 @@
         sums.append(
             mm(dst_turned, jnp.concatenate([low(opened * b_source), opened_low], axis=1))
         )
+    yield
     both = jnp.concatenate(sums, axis=0)
     width = x.shape[1]
     recip = 1.0 / (both[:, width:] + 1.0)
@@ -147,15 +151,7 @@
     out_ref[...] = out
     live = live_of(info_ref, pl.program_id(0) * group, group, out.shape[1])
     kept = live * out
-    add_rows(sums_ref, [col_sum(kept), col_sum(kept * out)])
-
-    @pl.when(pl.program_id(0) == 0)
-    def _():
-        sums_ref[2:4, :] = other_ref[0:2, :]
-        count = info_ref[1]
-        for place in range(2, info_ref.shape[0] - 2):
-            count = count + info_ref[place]
-        sums_ref[4:5, :] = jnp.full((1, out.shape[1]), count, jnp.int32).astype(f32)
+    stats[0:2] = [col_sum(kept), col_sum(kept * out)]
 
 
 def head_masks(width):
@@ -187,9 +183,9 @@
     return low(jnp.concatenate(parts, axis=0)).T
 
 
-def attend_kernel(
+def attend_steps(
     info_ref, x_ref, bias_ref, w_ref, vec_ref,
-    out_ref, q_ref, k_ref, v_ref, att_ref, prob_ref, sums_ref,
+    out_ref, q_ref, k_ref, v_ref, att_ref, prob_ref, stats,
 ):
     group = x_ref.shape[0] // BLOCK
     x = x_ref[...]
@@ -208,6 +204,7 @@
         mm(keyed[nodes_of(place)], side_stack(queries_turned[:, nodes_of(place)], tall))
         for place in range(group)
     ]
+    yield
     for place in range(group):
         nodes = nodes_of(place)
         bias = bias_ref[nodes, :]
@@ -216,6 +213,7 @@
             part = raws[place][:, cols] + bias
             part = jnp.exp2((part - jnp.max(part, axis=0, keepdims=True)) * score_scale)
             prob_ref[nodes, cols] = low(part * (1.0 / jnp.sum(part, axis=0, keepdims=True)))
+    yield
     for place in range(group):
         nodes = nodes_of(place)
         att_ref[nodes, :] = turned_product(valued_turned[:, nodes], prob_ref, nodes, size)
@@ -223,12 +221,40 @@
     out_ref[...] = out
     live = live_of(info_ref, pl.program_id(0) * group, group, out.shape[1])
     kept = live * out
-    add_rows(sums_ref, [col_sum(kept), col_sum(kept * out)])
+    stats[2:4] = [col_sum(kept), col_sum(kept * out)]
+
+
+def forward_kernel(
+    info_ref, x_ref, e_ref, bias_ref, hot_ref, turned_ref, w_ref, vec_ref,
+    lout_ref, slope_ref, recip_ref, fall_ref, open_ref, bend_ref, bsrc_ref,
+    gout_ref, q_ref, k_ref, v_ref, att_ref, prob_ref, sums_ref,
+):
+    stats = [None] * 4
+    runs = [
+        attend_steps(
+            info_ref, x_ref, bias_ref, w_ref, vec_ref, gout_ref, q_ref, k_ref, v_ref, att_ref,
+            prob_ref, stats,
+        ),
+        local_steps(
+            info_ref, x_ref, e_ref, hot_ref, turned_ref, w_ref, vec_ref, lout_ref, slope_ref,
+            recip_ref, fall_ref, open_ref, bend_ref, bsrc_ref, stats,
+        ),
+    ]
+    while runs:
+        runs = [run for run in runs if next(run, 1) is None]
+    add_rows(sums_ref, stats)
+
+    @pl.when(pl.program_id(0) == 0)
+    def _():
+        count = info_ref[1]
+        for place in range(2, info_ref.shape[0] - 2):
+            count = count + info_ref[place]
+        sums_ref[4:5, :] = jnp.full((1, x_ref.shape[1]), count, jnp.int32).astype(f32)
 
 
 def mix_kernel(
     info_ref, local_ref, global_ref, cot_ref, sums_ref, w_ref, vec_ref,
-    low_ref, hlow_ref, hidden_ref, mixed_ref, stat_ref,
+    low_ref, hlow_ref, slope_ref, mixed_ref, stat_ref,
 ):
     group = local_ref.shape[0] // BLOCK
     width = local_ref.shape[1]
@@ -248,7 +274,9 @@
         hidden = mm(summed_low, w_ref[9 + half]) + vec_ref[9 + half : 10 + half, :]
         sig_value = sig(hidden)
         hidden_low = low(hidden * sig_value)
-        hidden_ref[:, half * width : (half + 1) * width] = hidden
+        slope_ref[:, half * width : (half + 1) * width] = low(
+            sig_value * (1.0 + hidden * (1.0 - sig_value))
+        )
         hlow_ref[:, half * width : (half + 1) * width] = hidden_low
         mixed = mixed + mm(hidden_low, w_ref[11 + half])
     mixed_ref[...] = mixed
@@ -265,12 +293,6 @@
     for value_ref, hat_ref, first in ((local_ref, lhat_ref, 0), (global_ref, ghat_ref, 2)):
         mean, rstd = norm_terms(sums, first, sums[4:5])
         hat_ref[...] = low((value_ref[...] - mean) * rstd)
-
-
-def slope_kernel(info_ref, hidden_ref, slope_ref):
-    hidden = hidden_ref[...]
-    sig_value = sig(hidden)
-    slope_ref[...] = low(sig_value * (1.0 + hidden * (1.0 - sig_value)))
 
 
 def mix_back_kernel(
@@ -355,7 +377,7 @@
     )
 
 
-def local_back_kernel(
+def local_back_steps(
     info_ref, dsum_ref, local_ref, slope_ref, recip_ref, fall_ref, open_ref, bend_ref, bsrc_ref,
     hot_ref, turned_ref, sums_ref, backs_ref, vec_ref,
     dnode_ref, dedge_ref, stat_ref,
@@ -370,6 +392,7 @@
     d_num = low(d_gated * recip_ref[...].astype(f32))
     d_den = low(-d_gated * fall_ref[...].astype(f32))
     pre_row = jnp.zeros((1, width), f32)
+    yield
     picks = [
         mm(
             hot_ref[edges_of(place), :BLOCK],
@@ -377,6 +400,7 @@
         )
         for place in range(group)
     ]
+    yield
     sources = []
     for place in range(group):
         edges = edges_of(place)
@@ -386,6 +410,7 @@
         d_pre = d_open * bend_ref[edges, :].astype(f32)
         pre_row = pre_row + col_sum(d_pre)
         dedge_ref[edges, :] = low(d_pre)
+    yield
     for place in range(group):
         nodes = nodes_of(place)
         turned = turned_ref[edges_of(place), :]
@@ -396,7 +421,7 @@
     add_rows(stat_ref, [col_sum(d_gated), pre_row])
 
 
-def attend_back_kernel(
+def attend_back_steps(
     info_ref, dsum_ref, global_ref, q_ref, k_ref, v_ref, prob_ref, sums_ref,
     backs_ref, w_ref, vec_ref,
     dqkv_ref, dlow_ref, stat_ref, score_ref,
@@ -413,10 +438,12 @@
     masks = head_masks(width)
     tall = tall_masks(width)
     turned_att = low(mm_back(w_ref[8], d_low))
+    yield
     d_probs = [
         mm(v_ref[nodes_of(place), :], side_stack(turned_att[:, nodes_of(place)], tall))
         for place in range(group)
     ]
+    yield
     for place in range(group):
         nodes = nodes_of(place)
         for head in range(HEADS):
@@ -426,6 +453,7 @@
             inner = jnp.sum(prob * part, axis=0, keepdims=True)
             d_score = low(prob * ((part - inner) * score_scale))
             score_ref[nodes, cols] = d_score
+    yield
     for place in range(group):
         nodes = nodes_of(place)
         dqkv_ref[nodes, :width] = turned_product(k_ref[nodes, :].T, score_ref, nodes, width // HEADS)
@@ -441,6 +469,27 @@
             col_sum(d_global),
         ],
     )
+
+
+def back_kernel(
+    info_ref, dsum_ref, lhat_ref, slope_ref, recip_ref, fall_ref, open_ref, bend_ref, bsrc_ref,
+    hot_ref, turned_ref, ghat_ref, q_ref, k_ref, v_ref, prob_ref, sums_ref, backs_ref, w_ref,
+    vec_ref,
+    dnode_ref, dedge_ref, lstat_ref, dqkv_ref, dlow_ref, gstat_ref, score_ref,
+):
+    runs = [
+        attend_back_steps(
+            info_ref, dsum_ref, ghat_ref, q_ref, k_ref, v_ref, prob_ref, sums_ref, backs_ref,
+            w_ref, vec_ref, dqkv_ref, dlow_ref, gstat_ref, score_ref,
+        ),
+        local_back_steps(
+            info_ref, dsum_ref, lhat_ref, slope_ref, recip_ref, fall_ref, open_ref, bend_ref,
+            bsrc_ref, hot_ref, turned_ref, sums_ref, backs_ref, vec_ref, dnode_ref, dedge_ref,
+            lstat_ref,
+        ),
+    ]
+    while runs:
+        runs = [run for run in runs if next(run, 1) is None]
 
 
 def branch_grad_kernel(
@@ -894,12 +943,30 @@
     node_bf = ((rows, width), bf16, node_spec)
     sums_out = ((8, width), f32, None)
     prob_spec = rows_spec(tall, HEADS * BLOCK)
-    global_out, queries, keyed, valued, attended, probs, global_sums = call(
-        attend_kernel,
+    (
+        local_out, gate_slope, recip, fall, opened, bend, b_source,
+        global_out, queries, keyed, valued, attended, probs, sums_part,
+    ) = call(
+        forward_kernel,
         steps,
         info,
-        [x_in, (bias, rows_spec(tall, BLOCK)), mats_in, vec_in],
-        [
+        [
+            x_in,
+            e_in,
+            (bias, rows_spec(tall, BLOCK)),
+            (hot, edge_spec),
+            (turned, edge_spec),
+            mats_in,
+            vec_in,
+        ],
+        [
+            node_f32,
+            node_bf,
+            node_bf,
+            node_bf,
+            ((edges, width), bf16, edge_spec),
+            ((edges, width), bf16, edge_spec),
+            ((edges, width), bf16, edge_spec),
             node_f32,
             node_bf,
             node_bf,
@@ -908,36 +975,13 @@
             ((rows, HEADS * BLOCK), bf16, prob_spec),
             sums_out,
         ],
-    )
-    local_out, gate_slope, recip, fall, opened, bend, b_source, sums_part = call(
-        local_kernel,
-        steps,
-        info,
-        [
-            x_in,
-            e_in,
-            (hot, edge_spec),
-            (turned, edge_spec),
-            mats_in,
-            vec_in,
-            (global_sums, None),
-        ],
-        [
-            node_f32,
-            node_bf,
-            node_bf,
-            node_bf,
-            ((edges, width), bf16, edge_spec),
-            ((edges, width), bf16, edge_spec),
-            ((edges, width), bf16, edge_spec),
-            sums_out,
-        ],
+        room=FRONT_ROOM,
     )
     sums = sum_small(sums_part, total)
     sums_in = (sums, None)
     cot_in = (cotangent, node_spec)
     wide_spec = rows_spec(tall, 2 * width)
-    summed_low, hidden_low, hidden, mixed, top_part = call(
+    summed_low, hidden_low, hidden_slope, mixed, top_part = call(
         mix_kernel,
         steps,
         info,
@@ -945,7 +989,7 @@
         [
             node_bf,
             ((rows, 2 * width), bf16, wide_spec),
-            ((rows, 2 * width), f32, wide_spec),
+            ((rows, 2 * width), bf16, wide_spec),
             node_f32,
             sums_out,
         ],
@@ -960,18 +1004,7 @@
             [node_bf, node_bf],
         )
 
-    def slope_work(info):
-        return call(
-            slope_kernel,
-            steps,
-            info,
-            [(hidden, wide_spec)],
-            [((rows, 2 * width), bf16, wide_spec)],
-        )[0]
-
-    tops, ((local_hat, global_hat), hidden_slope) = sum_small(
-        top_part, total, info, [hat_work, slope_work]
-    )
+    tops, ((local_hat, global_hat),) = sum_small(top_part, total, info, [hat_work])
     d_mixed, d_hidden, d_summed, back_part = call(
         mix_back_kernel,
         steps,
@@ -1031,8 +1064,14 @@
     backs_in = (backs, None)
     dsum_in = (d_summed, node_spec)
     dnode_spec = rows_spec(tall, 4 * width)
-    d_node, d_edge, local_bias = call(
-        local_back_kernel,
+    dqkv_spec = rows_spec(tall, 3 * width)
+    slots = total // 2
+    packed = in_rows(total, width)
+    grad_outs = [((MATS, width, width), bf16, None)]
+    if packed:
+        grad_outs = [((slots // 2, MATS * 8, width), bf16, None)] * 4
+    d_node, d_edge, local_bias, d_qkv, d_low, attend_bias = call(
+        back_kernel,
         steps,
         info,
         [
@@ -1046,28 +1085,6 @@
             (b_source, edge_spec),
             (hot, edge_spec),
             (turned, edge_spec),
-            sums_in,
-            backs_in,
-            vec_in,
-        ],
-        [
-            ((rows, 4 * width), bf16, dnode_spec),
-            ((edges, width), bf16, edge_spec),
-            sums_out,
-        ],
-    )
-    dqkv_spec = rows_spec(tall, 3 * width)
-    slots = total // 2
-    packed = in_rows(total, width)
-    grad_outs = [((MATS, width, width), bf16, None)]
-    if packed:
-        grad_outs = [((slots // 2, MATS * 8, width), bf16, None)] * 4
-    d_qkv, d_low, attend_bias = call(
-        attend_back_kernel,
-        steps,
-        info,
-        [
-            dsum_in,
             (global_hat, node_spec),
             (queries, node_spec),
             (keyed, node_spec),
@@ -1078,8 +1095,16 @@
             mats_in,
             vec_in,
         ],
-        [((rows, 3 * width), bf16, dqkv_spec), node_bf, sums_out],
+        [
+            ((rows, 4 * width), bf16, dnode_spec),
+            ((edges, width), bf16, edge_spec),
+            sums_out,
+            ((rows, 3 * width), bf16, dqkv_spec),
+            node_bf,
+            sums_out,
+        ],
         [pltpu.VMEM((tall, HEADS * BLOCK), bf16)],
+        room=BACK_ROOM,
     )
     *grads, wide_bias = call(
         branch_grad_kernel,

time: 160 us -> 157 us (0.981)
  Pallas kernels: 57.2 us -> 52.2 us
    pallas_call x19 -> x16, Pallas kernels: 57.2 us -> 52.2 us  [call(): pl.pallas_call(kernel, grid_spec=pltpu.PrefetchScalarGridSpec(num_scalar_...]
  transfers between devices with their start and end apart: 31 -> 31, of which waited for: 27 -> 28; matrix products, arithmetic and copies ran while one was open for 2% -> 2% of each run, Pallas kernels for 12% -> 11%
where the time goes in v4:
time: 157 us
  waiting for transfers between devices  57 us (36%)
  Pallas kernels  52.2 us (33%)
  starting transfers between devices  41.6 us (26%)
  local copies, waits for them, and re-layouts  3.08 us (2%)
  other arithmetic  1.69 us (1%)
    pallas_call x16, Pallas kernels, call(): pl.pallas_call(kernel, grid_spec=pltpu.PrefetchScalarGridSpec(num_scalar_...  52.2 us
    ppermute x23, waiting for transfers between devices, swap_with(): lax.ppermute(values, axis_names, [(place, place ^ step) for place in rang...  33.7 us
    ppermute x23, starting transfers between devices, swap_with(): lax.ppermute(values, axis_names, [(place, place ^ step) for place in rang...  25.8 us
    ppermute x8, waiting for transfers between devices, swap_chips(): lax.ppermute(values, axis_names, [(place, place ^ orders[place % 2][numbe...  23.3 us
    ppermute x8, starting transfers between devices, swap_chips(): lax.ppermute(values, axis_names, [(place, place ^ orders[place % 2][numbe...  15.8 us
  transfers between devices with their start and end apart: 31, of which 28 were waited for; matrix products, arithmetic and copies ran while one was open for 2% of the time, Pallas kernels for 11%

profile of v4, /device:TPU:0, one launch (start us, length us, event | category | flops | bytes accessed | tf_op | source)
XLA Modules:
  0.0 156.7 jit_solution(7478997660213858046)
XLA Ops:
  1.8 4.1 %collective-permute-start = (bf16[1,104,256]{2,1,0:T(8,128)(2,1)S(1)}, bf16[1,104,256]{2,1,0:T(8,128)(2,1)S(1)}, u32[]{:S(2)}, u32[]{:S(2)}) collective-permute-start(bf16[1,104,256]{2,1,0:T(8,128)(2,1)S(1)} %reshape.42), channel_id=1, source_target_pairs={{0,16},{1,17},{2,18},{3,19},{4,20},{5,21},{6,22},{7,23},{8,24},{9,... | collective-permute-start | bytes 159752 | tf_op jit(solution)/shard_map/ppermute | solution.py:774
  10.1 3.4 %collective-permute-done.1 = bf16[2,104,256]{2,1,0:T(8,128)(2,1)S(1)} collective-permute-done((bf16[2,104,256]{2,1,0:T(8,128)(2,1)S(1)}, bf16[2,104,256]{2,1,0:T(8,128)(2,1)S(1)}, u32[]{:S(2)}, u32[]{:S(2)}) %collective-permute-start.1) | collective-permute-done | bytes 106528 | tf_op jit(solution)/shard_map/ppermute | solution.py:774
  16.8 2.6 %collective-permute-done.2 = bf16[4,104,256]{2,1,0:T(8,128)(2,1)S(1)} collective-permute-done((bf16[4,104,256]{2,1,0:T(8,128)(2,1)S(1)}, bf16[4,104,256]{2,1,0:T(8,128)(2,1)S(1)}, u32[]{:S(2)}, u32[]{:S(2)}) %collective-permute-start.2) | collective-permute-done | bytes 213024 | tf_op jit(solution)/shard_map/ppermute | solution.py:774
  22.0 3.0 %prep_kernel.1 = (bf16[4096,256]{1,0:T(8,128)(2,1)}, bf16[4096,256]{1,0:T(8,128)(2,1)}, f32[2048,128]{1,0:T(8,128)S(1)}) custom-call(s32[19]{0:T(128)S(1)} %pad_add_fusion.info_ref, s32[2,8,256]{2,1,0:T(8,128)S(1)} %reshape.43.src_ref, s32[2,8,256]{2,1,0:T(8,128)S(1)} %reshape.44.dst_ref, s32[2,8,256]{2,1,0:T(8,128)S(1)} %reshape.45.mask_ref, ...), custom_call_target="tpu_custom_call" | custom-call | flops 5000000000 | bytes 5000000 | tf_op jit(solution)/shard_map/prep_kernel/pallas_call | solution.py:727
  25.0 3.5 %collective-permute-done.3.far_ref = bf16[8,104,256]{2,1,0:T(8,128)(2,1)S(1)} collective-permute-done((bf16[8,104,256]{2,1,0:T(8,128)(2,1)}, bf16[8,104,256]{2,1,0:T(8,128)(2,1)S(1)}, u32[]{:S(2)}, u32[]{:S(2)}) %collective-permute-start.3) | collective-permute-done | bytes 426016 | tf_op jit(solution)/shard_map/ppermute | solution.py:774
  30.9 10.6 %forward_kernel.1 = (f32[2048,256]{1,0:T(8,128)S(1)}, bf16[2048,256]{1,0:T(8,128)(2,1)S(1)}, bf16[2048,256]{1,0:T(8,128)(2,1)S(1)}, bf16[2048,256]{1,0:T(8,128)(...) custom-call(s32[19]{0:T(128)S(1)} %pad_add_fusion.info_ref, ...), custom_call_target="tpu_custom_call" | custom-call | flops 5000000000 | bytes 5000000 | tf_op jit(solution)/shard_map/forward_kernel/pallas_call | solution.py:727
  51.4 2.4 %collective-permute-done.9 = f32[8,256]{1,0:T(8,128)S(1)} collective-permute-done((f32[8,256]{1,0:T(8,128)S(1)}, f32[8,256]{1,0:T(8,128)S(1)}, u32[]{:S(2)}, u32[]{:S(2)}) %collective-permute-start.9) | collective-permute-done | bytes 8224 | tf_op jit(solution)/shard_map/ppermute | solution.py:748
  53.8 2.3 %collective-permute-start.10 = (f32[8,256]{1,0:T(8,128)S(1)}, f32[8,256]{1,0:T(8,128)S(1)}, u32[]{:S(2)}, u32[]{:S(2)}) collective-permute-start(f32[8,256]{1,0:T(8,128)S(1)} %add.91), channel_id=1, source_target_pairs={{0,16},{1,17},{2,18},{3,19},{4,20},{5,21},{6,22},{7,23},{8,24},{9,... | collective-permute-start | bytes 24584 | tf_op jit(solution)/shard_map/ppermute | solution.py:748
  56.1 2.2 %collective-permute-done.10 = f32[8,256]{1,0:T(8,128)S(1)} collective-permute-done((f32[8,256]{1,0:T(8,128)S(1)}, f32[8,256]{1,0:T(8,128)S(1)}, u32[]{:S(2)}, u32[]{:S(2)}) %collective-permute-start.10) | collective-permute-done | bytes 8224 | tf_op jit(solution)/shard_map/ppermute | solution.py:748
  58.3 3.8 %mix_kernel.1 = (bf16[2048,256]{1,0:T(8,128)(2,1)S(1)}, bf16[2048,512]{1,0:T(8,128)(2,1)S(1)}, bf16[2048,512]{1,0:T(8,128)(2,1)S(1)}, f32[2048,256]{1,0:T(8,128)S(1)}, f32[8,256]{1,0:T(8,128)S(1)}) custom-call(s32[19]{0:T(128)S(1)} %pad_add_fusion.info_ref, f32[2048,256]{1,0:T(8,128)S(1)} %get-tuple-element.95.local_ref, ...), custom_call_target="tpu_custom_call" | custom-call | flops 5000000000 | bytes 5000000 | tf_op jit(solution)/shard_map/mix_kernel/pallas_call | solution.py:727
  72.0 2.3 %collective-permute-done.14 = f32[8,256]{1,0:T(8,128)S(1)} collective-permute-done((f32[8,256]{1,0:T(8,128)S(1)}, f32[8,256]{1,0:T(8,128)S(1)}, u32[]{:S(2)}, u32[]{:S(2)}) %collective-permute-start.14) | collective-permute-done | bytes 8224 | tf_op jit(solution)/shard_map/ppermute | solution.py:748
  74.3 2.3 %collective-permute-start.15 = (f32[8,256]{1,0:T(8,128)S(1)}, f32[8,256]{1,0:T(8,128)S(1)}, u32[]{:S(2)}, u32[]{:S(2)}) collective-permute-start(f32[8,256]{1,0:T(8,128)S(1)} %add.96), channel_id=1, source_target_pairs={{0,16},{1,17},{2,18},{3,19},{4,20},{5,21},{6,22},{7,23},{8,24},{9,... | collective-permute-start | bytes 24584 | tf_op jit(solution)/shard_map/ppermute | solution.py:748
  76.6 2.2 %collective-permute-done.15 = f32[8,256]{1,0:T(8,128)S(1)} collective-permute-done((f32[8,256]{1,0:T(8,128)S(1)}, f32[8,256]{1,0:T(8,128)S(1)}, u32[]{:S(2)}, u32[]{:S(2)}) %collective-permute-start.15) | collective-permute-done | bytes 8224 | tf_op jit(solution)/shard_map/ppermute | solution.py:748
  78.9 2.9 %mix_back_kernel.1 = (bf16[2048,256]{1,0:T(8,128)(2,1)S(1)}, bf16[2048,512]{1,0:T(8,128)(2,1)S(1)}, bf16[2048,256]{1,0:T(8,128)(2,1)S(1)}, f32[8,256]{1,0:T(8,128)S(1)}) custom-call(s32[19]{0:T(128)S(1)} %pad_add_fusion.info_ref, f32[2048,256]{1,0:T(8,128)S(1)} %get-tuple-element.98.mixed_ref, bf16[2048,512]{1,0:T(8,128)(2,1)S(1)} %get-tuple-element.99.slope_ref, ...), custom_call_target="tpu_custom_call" | custom-call | flops 5000000000 | bytes 5000000 | tf_op jit(solution)/shard_map/mix_back_kernel/pallas_call | solution.py:727
  96.6 2.4 %collective-permute-done.20 = f32[8,256]{1,0:T(8,128)S(1)} collective-permute-done((f32[8,256]{1,0:T(8,128)S(1)}, f32[8,256]{1,0:T(8,128)S(1)}, u32[]{:S(2)}, u32[]{:S(2)}) %collective-permute-start.20) | collective-permute-done | bytes 8224 | tf_op jit(solution)/shard_map/ppermute | solution.py:748
  99.0 10.9 %back_kernel.1 = (bf16[2048,1024]{1,0:T(8,128)(2,1)S(1)}, bf16[4096,256]{1,0:T(8,128)(2,1)S(1)}, f32[8,256]{1,0:T(8,128)S(1)}, bf16[2048,768]{1,0:T(8,128)(2,1)S...) custom-call(s32[19]{0:T(128)S(1)} %pad_add_fusion.info_ref, bf16[2048,256]{1,0:T(8,128)(2,1)S(1)} %get-tuple-element.121.dsum_ref, ...), custom_call_target="tpu_custom_call" | custom-call | flops 5000000000 | bytes 5000000 | tf_op jit(solution)/shard_map/back_kernel/pallas_call | solution.py:727
  109.8 3.8 %branch_grad_kernel.1 = (bf16[8,104,256]{2,1,0:T(8,128)(2,1)S(1)}, bf16[8,104,256]{2,1,0:T(8,128)(2,1)S(1)}, bf16[8,104,256]{2,1,0:T(8,128)(2,1)S(1)}, bf16[8,104,256]{2,1,0:T(8,128)(2,1)S(1)}, f32[8,512]{1,0:T(8,128)S(1)}) custom-call(s32[19]{0:T(128)S(1)} %pad_add_fusion.info_ref, bf16[2048,256]{1,0:T(8,128)(2,1)S(1)} %constant_dynamic-slice_fusion.1.x_ref, ...), custom_call_target="tpu_custom_call" | custom-call | flops 5000000000 | bytes 5000000 | tf_op jit(solution)/shard_map/branch_grad_kernel/pallas_call | solution.py:727
  117.3 4.2 %node_grad_kernel.1 = f32[2048,256]{1,0:T(8,128)} custom-call(s32[19]{0:T(128)S(1)} %pad_add_fusion.info_ref, bf16[2048,256]{1,0:T(8,128)(2,1)S(1)} %get-tuple-element.121.dsum_ref, bf16[2048,256]{1,0:T(8,128)(2,1)S(1)} %get-tuple-element.104.lhat_ref, bf16[2048,256]{1,0:T(8,128)(2,1)S(1)} %get-tuple-element.105.ghat_ref, ...), custom_call_target="tpu_custom_call" | custom-call | flops 5000000000 | bytes 5000000 | tf_op jit(solution)/shard_map/node_grad_kernel/pallas_call | solution.py:727
  121.5 2.3 %collective-permute-done.22 = bf16[8,104,256]{2,1,0:T(8,128)(2,1)S(1)} collective-permute-done((bf16[8,104,256]{2,1,0:T(8,128)(2,1)S(1)}, bf16[8,104,256]{2,1,0:T(8,128)(2,1)S(1)}, u32[]{:S(2)}, u32[]{:S(2)}) %collective-permute-start.22) | collective-permute-done | bytes 426016 | tf_op jit(solution)/shard_map/ppermute | solution.py:774
  125.5 3.0 %edge_grad_kernel.1 = f32[4096,256]{1,0:T(8,128)} custom-call(s32[19]{0:T(128)S(1)} %pad_add_fusion.info_ref, bf16[4096,256]{1,0:T(8,128)(2,1)S(1)} %get-tuple-element.134.dedge_ref, bf16[13,256,256]{2,1,0:T(8,128)(2,1)S(1)} %assemble_kernel.1.w_ref), custom_call_target="tpu_custom_call" | custom-call | flops 5000000000 | bytes 5000000 | tf_op jit(solution)/shard_map/edge_grad_kernel/pallas_call | solution.py:727
  130.9 3.7 %collective-permute-done.25.got_ref = bf16[2,104,256]{2,1,0:T(8,128)(2,1)S(1)} collective-permute-done((bf16[2,104,256]{2,1,0:T(8,128)(2,1)S(1)}, bf16[2,104,256]{2,1,0:T(8,128)(2,1)S(1)}, u32[]{:S(2)}, u32[]{:S(2)}) %collective-permute-start.25) | collective-permute-done | bytes 106528 | tf_op jit(solution)/shard_map/ppermute | solution.py:774
  137.5 4.8 %collective-permute-done.26.got_ref = bf16[2,112,256]{2,1,0:T(8,128)(2,1)S(1)} collective-permute-done((bf16[2,112,256]{2,1,0:T(8,128)(2,1)S(1)}, bf16[2,112,256]{2,1,0:T(8,128)(2,1)S(1)}, u32[]{:S(2)}, u32[]{:S(2)}) %collective-permute-start.26) | collective-permute-done | bytes 114720 | tf_op jit(solution)/shard_map/ppermute | solution.py:774
  145.5 2.2 %collective-permute-done.28 = f32[8,256]{1,0:T(8,128)S(1)} collective-permute-done((f32[8,256]{1,0:T(8,128)S(1)}, f32[8,256]{1,0:T(8,128)S(1)}, u32[]{:S(2)}, u32[]{:S(2)}) %collective-permute-start.28) | collective-permute-done | bytes 8224 | tf_op jit(solution)/shard_map/ppermute | solution.py:748
  151.6 3.4 %collective-permute-done.30 = f32[8,256]{1,0:T(8,128)S(1)} collective-permute-done((f32[8,256]{1,0:T(8,128)S(1)}, f32[8,256]{1,0:T(8,128)S(1)}, u32[]{:S(2)}, u32[]{:S(2)}) %collective-permute-start.30) | collective-permute-done | bytes 8224 | tf_op jit(solution)/shard_map/ppermute | solution.py:748
  (132 shorter events, 67.2 us)
Async XLA Ops:
  1.8 6.8 %collective-permute-start = (bf16[1,104,256]{2,1,0:T(8,128)(2,1)S(1)}, bf16[1,104,256]{2,1,0:T(8,128)(2,1)S(1)}, u32[]{:S(2)}, u32[]{:S(2)}) collective-permute-start(bf16[1,104,256]{2,1,0:T(8,128)(2,1)S(1)} %reshape.42), channel_id=1, source_target_pairs={{0,16},{1,17},{2,18},{3,19},{4,20},{5,21},{6,22},{7,23},{8,24},{9,... | collective-permute-start | bytes 159752 | tf_op jit(solution)/shard_map/ppermute | solution.py:774
  8.6 4.8 %collective-permute-start.1 = (bf16[2,104,256]{2,1,0:T(8,128)(2,1)S(1)}, bf16[2,104,256]{2,1,0:T(8,128)(2,1)S(1)}, u32[]{:S(2)}, u32[]{:S(2)}) collective-permute-start(bf16[2,104,256]{2,1,0:T(8,128)(2,1)S(1)} %pad_maximum_fusion.1), channel_id=1, source_target_pairs={{0,8},{1,3},{2,10},{3,1},{4,12},{5,7},{6,14},{7,5},{8,0},{9,11},{1... | collective-permute-start | bytes 319496 | tf_op jit(solution)/shard_map/ppermute | solution.py:774
  13.5 5.9 %collective-permute-start.2 = (bf16[4,104,256]{2,1,0:T(8,128)(2,1)S(1)}, bf16[4,104,256]{2,1,0:T(8,128)(2,1)S(1)}, u32[]{:S(2)}, u32[]{:S(2)}) collective-permute-start(bf16[4,104,256]{2,1,0:T(8,128)(2,1)S(1)} %pad_maximum_fusion), channel_id=1, source_target_pairs={{0,4},{1,9},{2,6},{3,11},{4,0},{5,13},{6,2},{7,15},{8,12},{9,1},{1... | collective-permute-start | bytes 638984 | tf_op jit(solution)/shard_map/ppermute | solution.py:774
  20.1 4.9 %collective-permute-start.4 = (bf16[8,104,256]{2,1,0:T(8,128)(2,1)}, bf16[8,104,256]{2,1,0:T(8,128)(2,1)S(1)}, u32[]{:S(2)}, u32[]{:S(2)}) collective-permute-start(bf16[8,104,256]{2,1,0:T(8,128)(2,1)} %constant_dynamic-update-slice_fusion.near_ref), channel_id=1, source_target_pairs={{0,1},{1,0},{2,3},{3,2},{4,5},{5,4},{6,7},{7,6},{8,9},{9,8},{10,11... | collective-permute-start | bytes 1277960 | tf_op jit(solution)/shard_map/ppermute | solution.py:748
  20.1 8.3 %collective-permute-start.3 = (bf16[8,104,256]{2,1,0:T(8,128)(2,1)}, bf16[8,104,256]{2,1,0:T(8,128)(2,1)S(1)}, u32[]{:S(2)}, u32[]{:S(2)}) collective-permute-start(bf16[8,104,256]{2,1,0:T(8,128)(2,1)} %constant_dynamic-update-slice_fusion.near_ref), channel_id=1, source_target_pairs={{0,2},{1,5},{2,0},{3,7},{4,6},{5,1},{6,4},{7,3},{8,10},{9,13},{10,... | collective-permute-start | bytes 1277960 | tf_op jit(solution)/shard_map/ppermute | solution.py:774
  42.8 3.7 %collective-permute-start.7 = (f32[8,256]{1,0:T(8,128)S(1)}, f32[8,256]{1,0:T(8,128)S(1)}, u32[]{:S(2)}, u32[]{:S(2)}) collective-permute-start(f32[8,256]{1,0:T(8,128)S(1)} %add.88), channel_id=1, source_target_pairs={{0,2},{1,3},{2,0},{3,1},{4,6},{5,7},{6,4},{7,5},{8,10},{9,11},{10,... | collective-permute-start | bytes 24584 | tf_op jit(solution)/shard_map/ppermute | solution.py:748
  46.4 3.7 %collective-permute-start.8 = (f32[8,256]{1,0:T(8,128)S(1)}, f32[8,256]{1,0:T(8,128)S(1)}, u32[]{:S(2)}, u32[]{:S(2)}) collective-permute-start(f32[8,256]{1,0:T(8,128)S(1)} %add.89), channel_id=1, source_target_pairs={{0,4},{1,5},{2,6},{3,7},{4,0},{5,1},{6,2},{7,3},{8,12},{9,13},{10,... | collective-permute-start | bytes 24584 | tf_op jit(solution)/shard_map/ppermute | solution.py:748
  50.1 3.7 %collective-permute-start.9 = (f32[8,256]{1,0:T(8,128)S(1)}, f32[8,256]{1,0:T(8,128)S(1)}, u32[]{:S(2)}, u32[]{:S(2)}) collective-permute-start(f32[8,256]{1,0:T(8,128)S(1)} %add.90), channel_id=1, source_target_pairs={{0,8},{1,9},{2,10},{3,11},{4,12},{5,13},{6,14},{7,15},{8,0},{9,1},... | collective-permute-start | bytes 24584 | tf_op jit(solution)/shard_map/ppermute | solution.py:748
  53.8 4.5 %collective-permute-start.10 = (f32[8,256]{1,0:T(8,128)S(1)}, f32[8,256]{1,0:T(8,128)S(1)}, u32[]{:S(2)}, u32[]{:S(2)}) collective-permute-start(f32[8,256]{1,0:T(8,128)S(1)} %add.91), channel_id=1, source_target_pairs={{0,16},{1,17},{2,18},{3,19},{4,20},{5,21},{6,22},{7,23},{8,24},{9,... | collective-permute-start | bytes 24584 | tf_op jit(solution)/shard_map/ppermute | solution.py:748
  63.3 3.7 %collective-permute-start.12 = (f32[8,256]{1,0:T(8,128)S(1)}, f32[8,256]{1,0:T(8,128)S(1)}, u32[]{:S(2)}, u32[]{:S(2)}) collective-permute-start(f32[8,256]{1,0:T(8,128)S(1)} %add.93), channel_id=1, source_target_pairs={{0,2},{1,3},{2,0},{3,1},{4,6},{5,7},{6,4},{7,5},{8,10},{9,11},{10,... | collective-permute-start | bytes 24584 | tf_op jit(solution)/shard_map/ppermute | solution.py:748
  67.0 3.7 %collective-permute-start.13 = (f32[8,256]{1,0:T(8,128)S(1)}, f32[8,256]{1,0:T(8,128)S(1)}, u32[]{:S(2)}, u32[]{:S(2)}) collective-permute-start(f32[8,256]{1,0:T(8,128)S(1)} %add.94), channel_id=1, source_target_pairs={{0,4},{1,5},{2,6},{3,7},{4,0},{5,1},{6,2},{7,3},{8,12},{9,13},{10,... | collective-permute-start | bytes 24584 | tf_op jit(solution)/shard_map/ppermute | solution.py:748
  70.6 3.7 %collective-permute-start.14 = (f32[8,256]{1,0:T(8,128)S(1)}, f32[8,256]{1,0:T(8,128)S(1)}, u32[]{:S(2)}, u32[]{:S(2)}) collective-permute-start(f32[8,256]{1,0:T(8,128)S(1)} %add.95), channel_id=1, source_target_pairs={{0,8},{1,9},{2,10},{3,11},{4,12},{5,13},{6,14},{7,15},{8,0},{9,1},... | collective-permute-start | bytes 24584 | tf_op jit(solution)/shard_map/ppermute | solution.py:748
  74.3 4.5 %collective-permute-start.15 = (f32[8,256]{1,0:T(8,128)S(1)}, f32[8,256]{1,0:T(8,128)S(1)}, u32[]{:S(2)}, u32[]{:S(2)}) collective-permute-start(f32[8,256]{1,0:T(8,128)S(1)} %add.96), channel_id=1, source_target_pairs={{0,16},{1,17},{2,18},{3,19},{4,20},{5,21},{6,22},{7,23},{8,24},{9,... | collective-permute-start | bytes 24584 | tf_op jit(solution)/shard_map/ppermute | solution.py:748
  83.0 4.0 %collective-permute-start.17 = (f32[8,256]{1,0:T(8,128)S(1)}, f32[8,256]{1,0:T(8,128)S(1)}, u32[]{:S(2)}, u32[]{:S(2)}) collective-permute-start(f32[8,256]{1,0:T(8,128)S(1)} %add.98), channel_id=1, source_target_pairs={{0,2},{1,3},{2,0},{3,1},{4,6},{5,7},{6,4},{7,5},{8,10},{9,11},{10,... | collective-permute-start | bytes 24584 | tf_op jit(solution)/shard_map/ppermute | solution.py:748
  87.0 3.7 %collective-permute-start.18 = (f32[8,256]{1,0:T(8,128)S(1)}, f32[8,256]{1,0:T(8,128)S(1)}, u32[]{:S(2)}, u32[]{:S(2)}) collective-permute-start(f32[8,256]{1,0:T(8,128)S(1)} %add.99), channel_id=1, source_target_pairs={{0,4},{1,5},{2,6},{3,7},{4,0},{5,1},{6,2},{7,3},{8,12},{9,13},{10,... | collective-permute-start | bytes 24584 | tf_op jit(solution)/shard_map/ppermute | solution.py:748
  90.8 3.7 %collective-permute-start.19 = (f32[8,256]{1,0:T(8,128)S(1)}, f32[8,256]{1,0:T(8,128)S(1)}, u32[]{:S(2)}, u32[]{:S(2)}) collective-permute-start(f32[8,256]{1,0:T(8,128)S(1)} %add.100), channel_id=1, source_target_pairs={{0,8},{1,9},{2,10},{3,11},{4,12},{5,13},{6,14},{7,15},{8,0},{9,1},... | collective-permute-start | bytes 24584 | tf_op jit(solution)/shard_map/ppermute | solution.py:748
  94.4 4.5 %collective-permute-start.20 = (f32[8,256]{1,0:T(8,128)S(1)}, f32[8,256]{1,0:T(8,128)S(1)}, u32[]{:S(2)}, u32[]{:S(2)}) collective-permute-start(f32[8,256]{1,0:T(8,128)S(1)} %add.101), channel_id=1, source_target_pairs={{0,16},{1,17},{2,18},{3,19},{4,20},{5,21},{6,22},{7,23},{8,24},{9,... | collective-permute-start | bytes 24584 | tf_op jit(solution)/shard_map/ppermute | solution.py:748
  115.6 8.2 %collective-permute-start.22 = (bf16[8,104,256]{2,1,0:T(8,128)(2,1)S(1)}, bf16[8,104,256]{2,1,0:T(8,128)(2,1)S(1)}, u32[]{:S(2)}, u32[]{:S(2)}) collective-permute-start(bf16[8,104,256]{2,1,0:T(8,128)(2,1)S(1)} %add_convert_fusion), channel_id=1, source_target_pairs={{0,2},{1,5},{2,0},{3,7},{4,6},{5,1},{6,4},{7,3},{8,10},{9,13},{10,... | collective-permute-start | bytes 1277960 | tf_op jit(solution)/shard_map/ppermute | solution.py:774
  123.9 5.9 %collective-permute-start.24 = (bf16[4,104,256]{2,1,0:T(8,128)(2,1)S(1)}, bf16[4,104,256]{2,1,0:T(8,128)(2,1)S(1)}, u32[]{:S(2)}, u32[]{:S(2)}) collective-permute-start(bf16[4,104,256]{2,1,0:T(8,128)(2,1)S(1)} %get-tuple-element.163), channel_id=1, source_target_pairs={{0,4},{1,9},{2,6},{3,11},{4,0},{5,13},{6,2},{7,15},{8,12},{9,1},{1... | collective-permute-start | bytes 638984 | tf_op jit(solution)/shard_map/ppermute | solution.py:774
  129.9 4.8 %collective-permute-start.25 = (bf16[2,104,256]{2,1,0:T(8,128)(2,1)S(1)}, bf16[2,104,256]{2,1,0:T(8,128)(2,1)S(1)}, u32[]{:S(2)}, u32[]{:S(2)}) collective-permute-start(bf16[2,104,256]{2,1,0:T(8,128)(2,1)S(1)} %get-tuple-element.164), channel_id=1, source_target_pairs={{0,8},{1,3},{2,10},{3,1},{4,12},{5,7},{6,14},{7,5},{8,0},{9,11},{1... | collective-permute-start | bytes 319496 | tf_op jit(solution)/shard_map/ppermute | solution.py:774
  135.3 7.0 %collective-permute-start.26 = (bf16[2,112,256]{2,1,0:T(8,128)(2,1)S(1)}, bf16[2,112,256]{2,1,0:T(8,128)(2,1)S(1)}, u32[]{:S(2)}, u32[]{:S(2)}) collective-permute-start(bf16[2,112,256]{2,1,0:T(8,128)(2,1)S(1)} %last_kernel.1.mine_ref), channel_id=1, source_target_pairs={{0,16},{1,17},{2,18},{3,19},{4,20},{5,21},{6,22},{7,23},{8,24},{9,... | collective-permute-start | bytes 344072 | tf_op jit(solution)/shard_map/ppermute | solution.py:774
  144.1 3.7 %collective-permute-start.28 = (f32[8,256]{1,0:T(8,128)S(1)}, f32[8,256]{1,0:T(8,128)S(1)}, u32[]{:S(2)}, u32[]{:S(2)}) collective-permute-start(f32[8,256]{1,0:T(8,128)S(1)} %add.109), channel_id=1, source_target_pairs={{0,2},{1,3},{2,0},{3,1},{4,6},{5,7},{6,4},{7,5},{8,10},{9,11},{10,... | collective-permute-start | bytes 24584 | tf_op jit(solution)/shard_map/ppermute | solution.py:748
  147.7 3.7 %collective-permute-start.29 = (f32[8,256]{1,0:T(8,128)S(1)}, f32[8,256]{1,0:T(8,128)S(1)}, u32[]{:S(2)}, u32[]{:S(2)}) collective-permute-start(f32[8,256]{1,0:T(8,128)S(1)} %add.110), channel_id=1, source_target_pairs={{0,4},{1,5},{2,6},{3,7},{4,0},{5,1},{6,2},{7,3},{8,12},{9,13},{10,... | collective-permute-start | bytes 24584 | tf_op jit(solution)/shard_map/ppermute | solution.py:748
  151.4 3.7 %collective-permute-start.30 = (f32[8,256]{1,0:T(8,128)S(1)}, f32[8,256]{1,0:T(8,128)S(1)}, u32[]{:S(2)}, u32[]{:S(2)}) collective-permute-start(f32[8,256]{1,0:T(8,128)S(1)} %add.111), channel_id=1, source_target_pairs={{0,8},{1,9},{2,10},{3,11},{4,12},{5,13},{6,14},{7,15},{8,0},{9,1},... | collective-permute-start | bytes 24584 | tf_op jit(solution)/shard_map/ppermute | solution.py:748
  (25 other events, 193.2 us)

commit v5 on v4

--- a/solution.py
+++ b/solution.py
@@ -757,10 +757,14 @@
     return lax.optimization_barrier((transfer, work(info)))
 
 
+def sum_steps(total):
+    return [step | 1 for step in steps_of(total)]
+
+
 def sum_small(values, total, info=None, works=()):
     results = []
     works = list(works)
-    for step in steps_of(total):
+    for step in sum_steps(total):
         other = swap_with(values, step, total)
         if works and step > 1:
             other, done = beside(values, other, info, works.pop(0))
@@ -855,7 +859,7 @@
         [(mine, None), (got, None)],
         [((2, kept.shape[1], kept.shape[2] // 2), f32, None), ((8, kept.shape[2]), f32, None)],
     )
-    for step in steps_of(total)[:-1]:
+    for step in sum_steps(total)[:-1]:
         tail = tail + swap_with(tail, step, total)
     return (grad_rows, tail, results)
 

time: 157 us -> 149 us (0.949)
  waiting for transfers between devices: 57 us -> 50.1 us
    ppermute x23, waiting for transfers between devices: 33.7 us -> 27.3 us  [swap_with(): lax.ppermute(values, axis_names, [(place, place ^ step) for place in rang...]
    ppermute x23, starting transfers between devices: 25.8 us -> 24.2 us  [swap_with(): lax.ppermute(values, axis_names, [(place, place ^ step) for place in rang...]
where the time goes in v5:
time: 149 us
  Pallas kernels  52.2 us (35%)
  waiting for transfers between devices  50.1 us (34%)
  starting transfers between devices  40.4 us (27%)
  local copies, waits for them, and re-layouts  3.08 us (2%)
  other arithmetic  1.69 us (1%)
    pallas_call x16, Pallas kernels, call(): pl.pallas_call(kernel, grid_spec=pltpu.PrefetchScalarGridSpec(num_scalar_...  52.2 us
    ppermute x23, waiting for transfers between devices, swap_with(): lax.ppermute(values, axis_names, [(place, place ^ step) for place in rang...  27.3 us
    ppermute x23, starting transfers between devices, swap_with(): lax.ppermute(values, axis_names, [(place, place ^ step) for place in rang...  24.2 us
    ppermute x8, waiting for transfers between devices, swap_chips(): lax.ppermute(values, axis_names, [(place, place ^ orders[place % 2][numbe...  22.8 us
    ppermute x8, starting transfers between devices, swap_chips(): lax.ppermute(values, axis_names, [(place, place ^ orders[place % 2][numbe...  16.2 us
  transfers between devices with their start and end apart: 31, of which 28 were waited for; matrix products, arithmetic and copies ran while one was open for 2% of the time, Pallas kernels for 11%

profile of v5, /device:TPU:0, one launch (start us, length us, event | category | flops | bytes accessed | tf_op | source)
XLA Modules:
  0.0 148.6 jit_solution(10674907637570198526)
XLA Ops:
  1.8 4.1 %collective-permute-start = (bf16[1,104,256]{2,1,0:T(8,128)(2,1)S(1)}, bf16[1,104,256]{2,1,0:T(8,128)(2,1)S(1)}, u32[]{:S(2)}, u32[]{:S(2)}) collective-permute-start(bf16[1,104,256]{2,1,0:T(8,128)(2,1)S(1)} %reshape.42), channel_id=1, source_target_pairs={{0,16},{1,17},{2,18},{3,19},{4,20},{5,21},{6,22},{7,23},{8,24},{9,... | collective-permute-start | bytes 159752 | tf_op jit(solution)/shard_map/ppermute | solution.py:778
  10.1 3.4 %collective-permute-done.1 = bf16[2,104,256]{2,1,0:T(8,128)(2,1)S(1)} collective-permute-done((bf16[2,104,256]{2,1,0:T(8,128)(2,1)S(1)}, bf16[2,104,256]{2,1,0:T(8,128)(2,1)S(1)}, u32[]{:S(2)}, u32[]{:S(2)}) %collective-permute-start.1) | collective-permute-done | bytes 106528 | tf_op jit(solution)/shard_map/ppermute | solution.py:778
  13.5 2.0 %collective-permute-start.2 = (bf16[4,104,256]{2,1,0:T(8,128)(2,1)S(1)}, bf16[4,104,256]{2,1,0:T(8,128)(2,1)S(1)}, u32[]{:S(2)}, u32[]{:S(2)}) collective-permute-start(bf16[4,104,256]{2,1,0:T(8,128)(2,1)S(1)} %pad_maximum_fusion), channel_id=1, source_target_pairs={{0,4},{1,9},{2,6},{3,11},{4,0},{5,13},{6,2},{7,15},{8,12},{9,1},{1... | collective-permute-start | bytes 638984 | tf_op jit(solution)/shard_map/ppermute | solution.py:778
  16.8 2.6 %collective-permute-done.2 = bf16[4,104,256]{2,1,0:T(8,128)(2,1)S(1)} collective-permute-done((bf16[4,104,256]{2,1,0:T(8,128)(2,1)S(1)}, bf16[4,104,256]{2,1,0:T(8,128)(2,1)S(1)}, u32[]{:S(2)}, u32[]{:S(2)}) %collective-permute-start.2) | collective-permute-done | bytes 213024 | tf_op jit(solution)/shard_map/ppermute | solution.py:778
  22.0 3.0 %prep_kernel.1 = (bf16[4096,256]{1,0:T(8,128)(2,1)}, bf16[4096,256]{1,0:T(8,128)(2,1)}, f32[2048,128]{1,0:T(8,128)S(1)}) custom-call(s32[19]{0:T(128)S(1)} %pad_add_fusion.info_ref, s32[2,8,256]{2,1,0:T(8,128)S(1)} %reshape.43.src_ref, s32[2,8,256]{2,1,0:T(8,128)S(1)} %reshape.44.dst_ref, s32[2,8,256]{2,1,0:T(8,128)S(1)} %reshape.45.mask_ref, ...), custom_call_target="tpu_custom_call" | custom-call | flops 5000000000 | bytes 5000000 | tf_op jit(solution)/shard_map/prep_kernel/pallas_call | solution.py:727
  25.0 3.5 %collective-permute-done.3.far_ref = bf16[8,104,256]{2,1,0:T(8,128)(2,1)S(1)} collective-permute-done((bf16[8,104,256]{2,1,0:T(8,128)(2,1)}, bf16[8,104,256]{2,1,0:T(8,128)(2,1)S(1)}, u32[]{:S(2)}, u32[]{:S(2)}) %collective-permute-start.3) | collective-permute-done | bytes 426016 | tf_op jit(solution)/shard_map/ppermute | solution.py:778
  30.9 10.6 %forward_kernel.1 = (f32[2048,256]{1,0:T(8,128)S(1)}, bf16[2048,256]{1,0:T(8,128)(2,1)S(1)}, bf16[2048,256]{1,0:T(8,128)(2,1)S(1)}, bf16[2048,256]{1,0:T(8,128)(...) custom-call(s32[19]{0:T(128)S(1)} %pad_add_fusion.info_ref, ...), custom_call_target="tpu_custom_call" | custom-call | flops 5000000000 | bytes 5000000 | tf_op jit(solution)/shard_map/forward_kernel/pallas_call | solution.py:727
  50.2 2.0 %collective-permute-done.9 = f32[8,256]{1,0:T(8,128)S(1)} collective-permute-done((f32[8,256]{1,0:T(8,128)S(1)}, f32[8,256]{1,0:T(8,128)S(1)}, u32[]{:S(2)}, u32[]{:S(2)}) %collective-permute-start.9) | collective-permute-done | bytes 8224 | tf_op jit(solution)/shard_map/ppermute | solution.py:748
  52.2 2.1 %collective-permute-start.10 = (f32[8,256]{1,0:T(8,128)S(1)}, f32[8,256]{1,0:T(8,128)S(1)}, u32[]{:S(2)}, u32[]{:S(2)}) collective-permute-start(f32[8,256]{1,0:T(8,128)S(1)} %add.91), channel_id=1, source_target_pairs={{0,17},{1,16},{2,19},{3,18},{4,21},{5,20},{6,23},{7,22},{8,25},{9,... | collective-permute-start | bytes 24584 | tf_op jit(solution)/shard_map/ppermute | solution.py:748
  56.2 3.8 %mix_kernel.1 = (bf16[2048,256]{1,0:T(8,128)(2,1)S(1)}, bf16[2048,512]{1,0:T(8,128)(2,1)S(1)}, bf16[2048,512]{1,0:T(8,128)(2,1)S(1)}, f32[2048,256]{1,0:T(8,128)S(1)}, f32[8,256]{1,0:T(8,128)S(1)}) custom-call(s32[19]{0:T(128)S(1)} %pad_add_fusion.info_ref, f32[2048,256]{1,0:T(8,128)S(1)} %get-tuple-element.95.local_ref, ...), custom_call_target="tpu_custom_call" | custom-call | flops 5000000000 | bytes 5000000 | tf_op jit(solution)/shard_map/mix_kernel/pallas_call | solution.py:727
  70.4 2.2 %collective-permute-start.15 = (f32[8,256]{1,0:T(8,128)S(1)}, f32[8,256]{1,0:T(8,128)S(1)}, u32[]{:S(2)}, u32[]{:S(2)}) collective-permute-start(f32[8,256]{1,0:T(8,128)S(1)} %add.96), channel_id=1, source_target_pairs={{0,17},{1,16},{2,19},{3,18},{4,21},{5,20},{6,23},{7,22},{8,25},{9,... | collective-permute-start | bytes 24584 | tf_op jit(solution)/shard_map/ppermute | solution.py:748
  74.4 2.9 %mix_back_kernel.1 = (bf16[2048,256]{1,0:T(8,128)(2,1)S(1)}, bf16[2048,512]{1,0:T(8,128)(2,1)S(1)}, bf16[2048,256]{1,0:T(8,128)(2,1)S(1)}, f32[8,256]{1,0:T(8,128)S(1)}) custom-call(s32[19]{0:T(128)S(1)} %pad_add_fusion.info_ref, f32[2048,256]{1,0:T(8,128)S(1)} %get-tuple-element.98.mixed_ref, bf16[2048,512]{1,0:T(8,128)(2,1)S(1)} %get-tuple-element.99.slope_ref, ...), custom_call_target="tpu_custom_call" | custom-call | flops 5000000000 | bytes 5000000 | tf_op jit(solution)/shard_map/mix_back_kernel/pallas_call | solution.py:727
  80.3 2.1 %inner_grad_kernel.1 = (f32[256,512]{1,0:T(8,128)S(1)}, f32[8,512]{1,0:T(8,128)S(1)}) custom-call(s32[19]{0:T(128)S(1)} %pad_add_fusion.info_ref, bf16[2048,256]{1,0:T(8,128)(2,1)S(1)} %get-tuple-element.109.slow_ref, bf16[2048,512]{1,0:T(8,128)(2,1)S(1)} %get-tuple-element.110.dhid_ref), custom_call_target="tpu_custom_call" | custom-call | flops 5000000000 | bytes 5000000 | tf_op jit(solution)/shard_map/inner_grad_kernel/pallas_call | solution.py:727
  88.6 2.4 %collective-permute-start.20 = (f32[8,256]{1,0:T(8,128)S(1)}, f32[8,256]{1,0:T(8,128)S(1)}, u32[]{:S(2)}, u32[]{:S(2)}) collective-permute-start(f32[8,256]{1,0:T(8,128)S(1)} %add.101), channel_id=1, source_target_pairs={{0,17},{1,16},{2,19},{3,18},{4,21},{5,20},{6,23},{7,22},{8,25},{9,... | collective-permute-start | bytes 24584 | tf_op jit(solution)/shard_map/ppermute | solution.py:748
  92.6 10.9 %back_kernel.1 = (bf16[2048,1024]{1,0:T(8,128)(2,1)S(1)}, bf16[4096,256]{1,0:T(8,128)(2,1)S(1)}, f32[8,256]{1,0:T(8,128)S(1)}, bf16[2048,768]{1,0:T(8,128)(2,1)S...) custom-call(s32[19]{0:T(128)S(1)} %pad_add_fusion.info_ref, bf16[2048,256]{1,0:T(8,128)(2,1)S(1)} %get-tuple-element.121.dsum_ref, ...), custom_call_target="tpu_custom_call" | custom-call | flops 5000000000 | bytes 5000000 | tf_op jit(solution)/shard_map/back_kernel/pallas_call | solution.py:727
  103.5 3.8 %branch_grad_kernel.1 = (bf16[8,104,256]{2,1,0:T(8,128)(2,1)S(1)}, bf16[8,104,256]{2,1,0:T(8,128)(2,1)S(1)}, bf16[8,104,256]{2,1,0:T(8,128)(2,1)S(1)}, bf16[8,104,256]{2,1,0:T(8,128)(2,1)S(1)}, f32[8,512]{1,0:T(8,128)S(1)}) custom-call(s32[19]{0:T(128)S(1)} %pad_add_fusion.info_ref, bf16[2048,256]{1,0:T(8,128)(2,1)S(1)} %constant_dynamic-slice_fusion.1.x_ref, ...), custom_call_target="tpu_custom_call" | custom-call | flops 5000000000 | bytes 5000000 | tf_op jit(solution)/shard_map/branch_grad_kernel/pallas_call | solution.py:727
  110.5 4.2 %node_grad_kernel.1 = f32[2048,256]{1,0:T(8,128)} custom-call(s32[19]{0:T(128)S(1)} %pad_add_fusion.info_ref, bf16[2048,256]{1,0:T(8,128)(2,1)S(1)} %get-tuple-element.121.dsum_ref, bf16[2048,256]{1,0:T(8,128)(2,1)S(1)} %get-tuple-element.104.lhat_ref, bf16[2048,256]{1,0:T(8,128)(2,1)S(1)} %get-tuple-element.105.ghat_ref, ...), custom_call_target="tpu_custom_call" | custom-call | flops 5000000000 | bytes 5000000 | tf_op jit(solution)/shard_map/node_grad_kernel/pallas_call | solution.py:727
  114.8 2.7 %collective-permute-done.22 = bf16[8,104,256]{2,1,0:T(8,128)(2,1)S(1)} collective-permute-done((bf16[8,104,256]{2,1,0:T(8,128)(2,1)S(1)}, bf16[8,104,256]{2,1,0:T(8,128)(2,1)S(1)}, u32[]{:S(2)}, u32[]{:S(2)}) %collective-permute-start.22) | collective-permute-done | bytes 426016 | tf_op jit(solution)/shard_map/ppermute | solution.py:778
  119.1 3.0 %edge_grad_kernel.1 = f32[4096,256]{1,0:T(8,128)} custom-call(s32[19]{0:T(128)S(1)} %pad_add_fusion.info_ref, bf16[4096,256]{1,0:T(8,128)(2,1)S(1)} %get-tuple-element.134.dedge_ref, bf16[13,256,256]{2,1,0:T(8,128)(2,1)S(1)} %assemble_kernel.1.w_ref), custom_call_target="tpu_custom_call" | custom-call | flops 5000000000 | bytes 5000000 | tf_op jit(solution)/shard_map/edge_grad_kernel/pallas_call | solution.py:727
  124.8 3.5 %collective-permute-done.25.got_ref = bf16[2,104,256]{2,1,0:T(8,128)(2,1)S(1)} collective-permute-done((bf16[2,104,256]{2,1,0:T(8,128)(2,1)S(1)}, bf16[2,104,256]{2,1,0:T(8,128)(2,1)S(1)}, u32[]{:S(2)}, u32[]{:S(2)}) %collective-permute-start.25) | collective-permute-done | bytes 106528 | tf_op jit(solution)/shard_map/ppermute | solution.py:778
  128.9 2.7 %collective-permute-start.26 = (bf16[2,112,256]{2,1,0:T(8,128)(2,1)S(1)}, bf16[2,112,256]{2,1,0:T(8,128)(2,1)S(1)}, u32[]{:S(2)}, u32[]{:S(2)}) collective-permute-start(bf16[2,112,256]{2,1,0:T(8,128)(2,1)S(1)} %last_kernel.1.mine_ref), channel_id=1, source_target_pairs={{0,16},{1,17},{2,18},{3,19},{4,20},{5,21},{6,22},{7,23},{8,24},{9,... | collective-permute-start | bytes 344072 | tf_op jit(solution)/shard_map/ppermute | solution.py:778
  131.6 4.3 %collective-permute-done.26.got_ref = bf16[2,112,256]{2,1,0:T(8,128)(2,1)S(1)} collective-permute-done((bf16[2,112,256]{2,1,0:T(8,128)(2,1)S(1)}, bf16[2,112,256]{2,1,0:T(8,128)(2,1)S(1)}, u32[]{:S(2)}, u32[]{:S(2)}) %collective-permute-start.26) | collective-permute-done | bytes 114720 | tf_op jit(solution)/shard_map/ppermute | solution.py:778
  138.6 2.2 %collective-permute-done.28 = f32[8,256]{1,0:T(8,128)S(1)} collective-permute-done((f32[8,256]{1,0:T(8,128)S(1)}, f32[8,256]{1,0:T(8,128)S(1)}, u32[]{:S(2)}, u32[]{:S(2)}) %collective-permute-start.28) | collective-permute-done | bytes 8224 | tf_op jit(solution)/shard_map/ppermute | solution.py:748
  144.2 2.8 %collective-permute-done.30 = f32[8,256]{1,0:T(8,128)S(1)} collective-permute-done((f32[8,256]{1,0:T(8,128)S(1)}, f32[8,256]{1,0:T(8,128)S(1)}, u32[]{:S(2)}, u32[]{:S(2)}) %collective-permute-start.30) | collective-permute-done | bytes 8224 | tf_op jit(solution)/shard_map/ppermute | solution.py:748
  (132 shorter events, 60.8 us)
Async XLA Ops:
  1.8 6.8 %collective-permute-start = (bf16[1,104,256]{2,1,0:T(8,128)(2,1)S(1)}, bf16[1,104,256]{2,1,0:T(8,128)(2,1)S(1)}, u32[]{:S(2)}, u32[]{:S(2)}) collective-permute-start(bf16[1,104,256]{2,1,0:T(8,128)(2,1)S(1)} %reshape.42), channel_id=1, source_target_pairs={{0,16},{1,17},{2,18},{3,19},{4,20},{5,21},{6,22},{7,23},{8,24},{9,... | collective-permute-start | bytes 159752 | tf_op jit(solution)/shard_map/ppermute | solution.py:778
  8.6 4.8 %collective-permute-start.1 = (bf16[2,104,256]{2,1,0:T(8,128)(2,1)S(1)}, bf16[2,104,256]{2,1,0:T(8,128)(2,1)S(1)}, u32[]{:S(2)}, u32[]{:S(2)}) collective-permute-start(bf16[2,104,256]{2,1,0:T(8,128)(2,1)S(1)} %pad_maximum_fusion.1), channel_id=1, source_target_pairs={{0,8},{1,3},{2,10},{3,1},{4,12},{5,7},{6,14},{7,5},{8,0},{9,11},{1... | collective-permute-start | bytes 319496 | tf_op jit(solution)/shard_map/ppermute | solution.py:778
  13.5 5.9 %collective-permute-start.2 = (bf16[4,104,256]{2,1,0:T(8,128)(2,1)S(1)}, bf16[4,104,256]{2,1,0:T(8,128)(2,1)S(1)}, u32[]{:S(2)}, u32[]{:S(2)}) collective-permute-start(bf16[4,104,256]{2,1,0:T(8,128)(2,1)S(1)} %pad_maximum_fusion), channel_id=1, source_target_pairs={{0,4},{1,9},{2,6},{3,11},{4,0},{5,13},{6,2},{7,15},{8,12},{9,1},{1... | collective-permute-start | bytes 638984 | tf_op jit(solution)/shard_map/ppermute | solution.py:778
  20.1 4.9 %collective-permute-start.4 = (bf16[8,104,256]{2,1,0:T(8,128)(2,1)}, bf16[8,104,256]{2,1,0:T(8,128)(2,1)S(1)}, u32[]{:S(2)}, u32[]{:S(2)}) collective-permute-start(bf16[8,104,256]{2,1,0:T(8,128)(2,1)} %constant_dynamic-update-slice_fusion.near_ref), channel_id=1, source_target_pairs={{0,1},{1,0},{2,3},{3,2},{4,5},{5,4},{6,7},{7,6},{8,9},{9,8},{10,11... | collective-permute-start | bytes 1277960 | tf_op jit(solution)/shard_map/ppermute | solution.py:748
  20.1 8.3 %collective-permute-start.3 = (bf16[8,104,256]{2,1,0:T(8,128)(2,1)}, bf16[8,104,256]{2,1,0:T(8,128)(2,1)S(1)}, u32[]{:S(2)}, u32[]{:S(2)}) collective-permute-start(bf16[8,104,256]{2,1,0:T(8,128)(2,1)} %constant_dynamic-update-slice_fusion.near_ref), channel_id=1, source_target_pairs={{0,2},{1,5},{2,0},{3,7},{4,6},{5,1},{6,4},{7,3},{8,10},{9,13},{10,... | collective-permute-start | bytes 1277960 | tf_op jit(solution)/shard_map/ppermute | solution.py:778
  42.8 3.2 %collective-permute-start.7 = (f32[8,256]{1,0:T(8,128)S(1)}, f32[8,256]{1,0:T(8,128)S(1)}, u32[]{:S(2)}, u32[]{:S(2)}) collective-permute-start(f32[8,256]{1,0:T(8,128)S(1)} %add.88), channel_id=1, source_target_pairs={{0,3},{1,2},{2,1},{3,0},{4,7},{5,6},{6,5},{7,4},{8,11},{9,10},{10,... | collective-permute-start | bytes 24584 | tf_op jit(solution)/shard_map/ppermute | solution.py:748
  46.0 3.1 %collective-permute-start.8 = (f32[8,256]{1,0:T(8,128)S(1)}, f32[8,256]{1,0:T(8,128)S(1)}, u32[]{:S(2)}, u32[]{:S(2)}) collective-permute-start(f32[8,256]{1,0:T(8,128)S(1)} %add.89), channel_id=1, source_target_pairs={{0,5},{1,4},{2,7},{3,6},{4,1},{5,0},{6,3},{7,2},{8,13},{9,12},{10,... | collective-permute-start | bytes 24584 | tf_op jit(solution)/shard_map/ppermute | solution.py:748
  49.1 3.1 %collective-permute-start.9 = (f32[8,256]{1,0:T(8,128)S(1)}, f32[8,256]{1,0:T(8,128)S(1)}, u32[]{:S(2)}, u32[]{:S(2)}) collective-permute-start(f32[8,256]{1,0:T(8,128)S(1)} %add.90), channel_id=1, source_target_pairs={{0,9},{1,8},{2,11},{3,10},{4,13},{5,12},{6,15},{7,14},{8,1},{9,0},... | collective-permute-start | bytes 24584 | tf_op jit(solution)/shard_map/ppermute | solution.py:748
  52.2 4.0 %collective-permute-start.10 = (f32[8,256]{1,0:T(8,128)S(1)}, f32[8,256]{1,0:T(8,128)S(1)}, u32[]{:S(2)}, u32[]{:S(2)}) collective-permute-start(f32[8,256]{1,0:T(8,128)S(1)} %add.91), channel_id=1, source_target_pairs={{0,17},{1,16},{2,19},{3,18},{4,21},{5,20},{6,23},{7,22},{8,25},{9,... | collective-permute-start | bytes 24584 | tf_op jit(solution)/shard_map/ppermute | solution.py:748
  61.2 3.1 %collective-permute-start.12 = (f32[8,256]{1,0:T(8,128)S(1)}, f32[8,256]{1,0:T(8,128)S(1)}, u32[]{:S(2)}, u32[]{:S(2)}) collective-permute-start(f32[8,256]{1,0:T(8,128)S(1)} %add.93), channel_id=1, source_target_pairs={{0,3},{1,2},{2,1},{3,0},{4,7},{5,6},{6,5},{7,4},{8,11},{9,10},{10,... | collective-permute-start | bytes 24584 | tf_op jit(solution)/shard_map/ppermute | solution.py:748
  64.3 3.1 %collective-permute-start.13 = (f32[8,256]{1,0:T(8,128)S(1)}, f32[8,256]{1,0:T(8,128)S(1)}, u32[]{:S(2)}, u32[]{:S(2)}) collective-permute-start(f32[8,256]{1,0:T(8,128)S(1)} %add.94), channel_id=1, source_target_pairs={{0,5},{1,4},{2,7},{3,6},{4,1},{5,0},{6,3},{7,2},{8,13},{9,12},{10,... | collective-permute-start | bytes 24584 | tf_op jit(solution)/shard_map/ppermute | solution.py:748
  67.3 3.1 %collective-permute-start.14 = (f32[8,256]{1,0:T(8,128)S(1)}, f32[8,256]{1,0:T(8,128)S(1)}, u32[]{:S(2)}, u32[]{:S(2)}) collective-permute-start(f32[8,256]{1,0:T(8,128)S(1)} %add.95), channel_id=1, source_target_pairs={{0,9},{1,8},{2,11},{3,10},{4,13},{5,12},{6,15},{7,14},{8,1},{9,0},... | collective-permute-start | bytes 24584 | tf_op jit(solution)/shard_map/ppermute | solution.py:748
  70.4 4.0 %collective-permute-start.15 = (f32[8,256]{1,0:T(8,128)S(1)}, f32[8,256]{1,0:T(8,128)S(1)}, u32[]{:S(2)}, u32[]{:S(2)}) collective-permute-start(f32[8,256]{1,0:T(8,128)S(1)} %add.96), channel_id=1, source_target_pairs={{0,17},{1,16},{2,19},{3,18},{4,21},{5,20},{6,23},{7,22},{8,25},{9,... | collective-permute-start | bytes 24584 | tf_op jit(solution)/shard_map/ppermute | solution.py:748
  78.6 3.8 %collective-permute-start.17 = (f32[8,256]{1,0:T(8,128)S(1)}, f32[8,256]{1,0:T(8,128)S(1)}, u32[]{:S(2)}, u32[]{:S(2)}) collective-permute-start(f32[8,256]{1,0:T(8,128)S(1)} %add.98), channel_id=1, source_target_pairs={{0,3},{1,2},{2,1},{3,0},{4,7},{5,6},{6,5},{7,4},{8,11},{9,10},{10,... | collective-permute-start | bytes 24584 | tf_op jit(solution)/shard_map/ppermute | solution.py:748
  82.4 3.1 %collective-permute-start.18 = (f32[8,256]{1,0:T(8,128)S(1)}, f32[8,256]{1,0:T(8,128)S(1)}, u32[]{:S(2)}, u32[]{:S(2)}) collective-permute-start(f32[8,256]{1,0:T(8,128)S(1)} %add.99), channel_id=1, source_target_pairs={{0,5},{1,4},{2,7},{3,6},{4,1},{5,0},{6,3},{7,2},{8,13},{9,12},{10,... | collective-permute-start | bytes 24584 | tf_op jit(solution)/shard_map/ppermute | solution.py:748
  85.5 3.1 %collective-permute-start.19 = (f32[8,256]{1,0:T(8,128)S(1)}, f32[8,256]{1,0:T(8,128)S(1)}, u32[]{:S(2)}, u32[]{:S(2)}) collective-permute-start(f32[8,256]{1,0:T(8,128)S(1)} %add.100), channel_id=1, source_target_pairs={{0,9},{1,8},{2,11},{3,10},{4,13},{5,12},{6,15},{7,14},{8,1},{9,0},... | collective-permute-start | bytes 24584 | tf_op jit(solution)/shard_map/ppermute | solution.py:748
  88.6 4.0 %collective-permute-start.20 = (f32[8,256]{1,0:T(8,128)S(1)}, f32[8,256]{1,0:T(8,128)S(1)}, u32[]{:S(2)}, u32[]{:S(2)}) collective-permute-start(f32[8,256]{1,0:T(8,128)S(1)} %add.101), channel_id=1, source_target_pairs={{0,17},{1,16},{2,19},{3,18},{4,21},{5,20},{6,23},{7,22},{8,25},{9,... | collective-permute-start | bytes 24584 | tf_op jit(solution)/shard_map/ppermute | solution.py:748
  109.2 8.2 %collective-permute-start.22 = (bf16[8,104,256]{2,1,0:T(8,128)(2,1)S(1)}, bf16[8,104,256]{2,1,0:T(8,128)(2,1)S(1)}, u32[]{:S(2)}, u32[]{:S(2)}) collective-permute-start(bf16[8,104,256]{2,1,0:T(8,128)(2,1)S(1)} %add_convert_fusion), channel_id=1, source_target_pairs={{0,2},{1,5},{2,0},{3,7},{4,6},{5,1},{6,4},{7,3},{8,10},{9,13},{10,... | collective-permute-start | bytes 1277960 | tf_op jit(solution)/shard_map/ppermute | solution.py:778
  117.5 5.9 %collective-permute-start.24 = (bf16[4,104,256]{2,1,0:T(8,128)(2,1)S(1)}, bf16[4,104,256]{2,1,0:T(8,128)(2,1)S(1)}, u32[]{:S(2)}, u32[]{:S(2)}) collective-permute-start(bf16[4,104,256]{2,1,0:T(8,128)(2,1)S(1)} %get-tuple-element.163), channel_id=1, source_target_pairs={{0,4},{1,9},{2,6},{3,11},{4,0},{5,13},{6,2},{7,15},{8,12},{9,1},{1... | collective-permute-start | bytes 638984 | tf_op jit(solution)/shard_map/ppermute | solution.py:778
  123.5 4.8 %collective-permute-start.25 = (bf16[2,104,256]{2,1,0:T(8,128)(2,1)S(1)}, bf16[2,104,256]{2,1,0:T(8,128)(2,1)S(1)}, u32[]{:S(2)}, u32[]{:S(2)}) collective-permute-start(bf16[2,104,256]{2,1,0:T(8,128)(2,1)S(1)} %get-tuple-element.164), channel_id=1, source_target_pairs={{0,8},{1,3},{2,10},{3,1},{4,12},{5,7},{6,14},{7,5},{8,0},{9,11},{1... | collective-permute-start | bytes 319496 | tf_op jit(solution)/shard_map/ppermute | solution.py:778
  128.9 7.0 %collective-permute-start.26 = (bf16[2,112,256]{2,1,0:T(8,128)(2,1)S(1)}, bf16[2,112,256]{2,1,0:T(8,128)(2,1)S(1)}, u32[]{:S(2)}, u32[]{:S(2)}) collective-permute-start(bf16[2,112,256]{2,1,0:T(8,128)(2,1)S(1)} %last_kernel.1.mine_ref), channel_id=1, source_target_pairs={{0,16},{1,17},{2,18},{3,19},{4,20},{5,21},{6,22},{7,23},{8,24},{9,... | collective-permute-start | bytes 344072 | tf_op jit(solution)/shard_map/ppermute | solution.py:778
  137.7 3.1 %collective-permute-start.28 = (f32[8,256]{1,0:T(8,128)S(1)}, f32[8,256]{1,0:T(8,128)S(1)}, u32[]{:S(2)}, u32[]{:S(2)}) collective-permute-start(f32[8,256]{1,0:T(8,128)S(1)} %add.109), channel_id=1, source_target_pairs={{0,3},{1,2},{2,1},{3,0},{4,7},{5,6},{6,5},{7,4},{8,11},{9,10},{10,... | collective-permute-start | bytes 24584 | tf_op jit(solution)/shard_map/ppermute | solution.py:748
  140.8 3.1 %collective-permute-start.29 = (f32[8,256]{1,0:T(8,128)S(1)}, f32[8,256]{1,0:T(8,128)S(1)}, u32[]{:S(2)}, u32[]{:S(2)}) collective-permute-start(f32[8,256]{1,0:T(8,128)S(1)} %add.110), channel_id=1, source_target_pairs={{0,5},{1,4},{2,7},{3,6},{4,1},{5,0},{6,3},{7,2},{8,13},{9,12},{10,... | collective-permute-start | bytes 24584 | tf_op jit(solution)/shard_map/ppermute | solution.py:748
  143.9 3.1 %collective-permute-start.30 = (f32[8,256]{1,0:T(8,128)S(1)}, f32[8,256]{1,0:T(8,128)S(1)}, u32[]{:S(2)}, u32[]{:S(2)}) collective-permute-start(f32[8,256]{1,0:T(8,128)S(1)} %add.111), channel_id=1, source_target_pairs={{0,9},{1,8},{2,11},{3,10},{4,13},{5,12},{6,15},{7,14},{8,1},{9,0},... | collective-permute-start | bytes 24584 | tf_op jit(solution)/shard_map/ppermute | solution.py:748
  (25 other events, 181.7 us)

commit v6 on v5

--- a/solution.py
+++ b/solution.py
@@ -528,6 +528,17 @@
     return found
 
 
+def odd_bits(number):
+    return bin(number).count("1") & 1
+
+
+def parity(chip, slots):
+    bits = chip
+    for place in range(1, slots.bit_length() - 1):
+        bits = jnp.bitwise_xor(bits, lax.shift_right_logical(chip, jnp.int32(place)))
+    return jnp.bitwise_and(bits, 1)
+
+
 def chip_orders(total):
     chips = steps_of(total)[1:]
     return (chips, chips[1:-1] + chips[:1] + chips[-1:])
@@ -539,11 +550,13 @@
     orders = chip_orders(2 * slots)
     core = info_ref[info_ref.shape[0] - 2]
     chip = info_ref[info_ref.shape[0] - 1]
+    even = parity(jnp.bitwise_and(chip, slots // 2 - 1), slots)
     for slot in range(slots):
         near = [reach(order, slot) for order in orders]
         for out_ref, owner in zip(outs[slot // half :: 2], (core, 1 - core)):
-            step = jnp.where(owner == 0, near[0], near[1])
-            row = pl.multiple_of(16 * jnp.bitwise_xor(chip, step) + 8 * owner, 8)
+            step = jnp.where(owner == even, near[0], near[1])
+            side = 1 - owner if odd_bits(slot >> 1) else owner
+            row = pl.multiple_of(16 * jnp.bitwise_xor(chip, step) + 8 * side, 8)
             for first in range(0, len(parts), 2):
                 pair = [part[pl.ds(row, 8), :] for part in parts[first : first + 2]]
                 out_ref[slot % half, first * 8 : first * 8 + 8 * len(pair), :] = low(
@@ -558,30 +571,37 @@
     core = info_ref[info_ref.shape[0] - 2]
     chip = info_ref[info_ref.shape[0] - 1]
 
-    def fill(even_refs, odd_refs):
+    held = (near_ref, far_ref)
+    others = (near_other_ref, far_other_ref)
+
+    def fill(role, own):
         for far in range(slots):
-            even, odd = [
-                [slot for slot in range(slots) if reach(order, slot) == far][0] for order in orders
+            mine, other = [
+                [slot for slot in range(slots) if reach(order, slot) == far][0]
+                for order in (orders[role], orders[1 - role])
             ]
             row = pl.multiple_of(16 * jnp.bitwise_xor(chip, far), 16)
             for first in range(0, tall, 16):
                 size = min(16, tall - first)
                 part = slice(first, first + size)
-                upper = even_refs[even // half][even % half, part, :].astype(f32)
-                lower = odd_refs[odd // half][odd % half, part, :].astype(f32)
+                pair = [
+                    held[mine // half][mine % half, part, :].astype(f32),
+                    others[other // half][other % half, part, :].astype(f32),
+                ]
+                upper, lower = pair if own == odd_bits(far) else pair[::-1]
                 for step in range(size // 8):
                     rows = slice(step * 8, step * 8 + 8)
                     out_ref[first // 8 + step, pl.ds(row, 16), :] = low(
                         jnp.concatenate([upper[rows], lower[rows]], axis=0)
                     )
 
-    @pl.when(core == 0)
-    def _():
-        fill((near_ref, far_ref), (near_other_ref, far_other_ref))
-
-    @pl.when(core != 0)
-    def _():
-        fill((near_other_ref, far_other_ref), (near_ref, far_ref))
+    even = parity(chip, slots)
+    for own in range(2):
+        for role in range(2):
+
+            @pl.when((core == own) & (jnp.bitwise_xor(even, own) == role))
+            def _(own=own, role=role):
+                fill(role, own)
 
 
 def node_grad_kernel(
@@ -773,13 +793,13 @@
     return (values, results) if results else values
 
 
-def swap_chips(values, number, total):
+def swap_chips(values, number, total, straight=0):
     orders = chip_orders(total)
-    return lax.ppermute(
-        values,
-        axis_names,
-        [(place, place ^ orders[place % 2][number]) for place in range(total)],
-    )
+    pairs = []
+    for place in range(total):
+        step = orders[odd_bits(place & ~straight)][number]
+        pairs.append((place, place ^ (step if step & straight else step | 1)))
+    return lax.ppermute(values, axis_names, pairs)
 
 
 def in_rows(total, width):
@@ -840,7 +860,7 @@
             kept, got = kept[:half], got[:half]
         sent = low(far_kept.astype(f32) + far_got.astype(f32))
         kept = kept.astype(f32) + got.astype(f32)
-        got = swap_chips(sent, number, total)
+        got = swap_chips(sent, number, total, total // 2)
         if number < len(works):
             got, done = beside(sent, got, info, works[number])
             results.append(done)
@@ -851,7 +871,7 @@
         [(array, None) for array in (kept, got, *biases)],
         [((2, kept.shape[1] + 8, kept.shape[2]), bf16, None)],
     )[0]
-    got = swap_chips(mine, rounds - 1, total)
+    got = swap_chips(mine, rounds - 1, total, total // 2)
     grad_rows, tail = call(
         pair_kernel,
         1,

time: 149 us -> 148 us (level)
  waiting for transfers between devices: 50.1 us -> 47.4 us
  starting transfers between devices: 40.4 us -> 42 us
    ppermute x23, starting transfers between devices: 24.2 us -> 25.9 us  [swap_with(): lax.ppermute(values, axis_names, [(place, place ^ step) for place in rang...]
    ppermute x8, waiting for transfers between devices: 22.8 us -> 21.3 us  [swap_chips(): return lax.ppermute(values, axis_names, pairs)]
  transfers between devices with their start and end apart: 31 -> 31, of which waited for: 28 -> 27; matrix products, arithmetic and copies ran while one was open for 2% -> 2% of each run, Pallas kernels for 11% -> 11%
where the time goes in v6:
time: 148 us
  Pallas kernels  52.2 us (35%)
  waiting for transfers between devices  47.4 us (32%)
  starting transfers between devices  42 us (28%)
  local copies, waits for them, and re-layouts  3.37 us (2%)
  other arithmetic  1.69 us (1%)
    pallas_call x16, Pallas kernels, call(): pl.pallas_call(kernel, grid_spec=pltpu.PrefetchScalarGridSpec(num_scalar_...  52.2 us
    ppermute x23, waiting for transfers between devices, swap_with(): lax.ppermute(values, axis_names, [(place, place ^ step) for place in rang...  26 us
    ppermute x23, starting transfers between devices, swap_with(): lax.ppermute(values, axis_names, [(place, place ^ step) for place in rang...  25.9 us
    ppermute x8, waiting for transfers between devices, swap_chips(): return lax.ppermute(values, axis_names, pairs)  21.3 us
    ppermute x8, starting transfers between devices, swap_chips(): return lax.ppermute(values, axis_names, pairs)  16.1 us
  transfers between devices with their start and end apart: 31, of which 27 were waited for; matrix products, arithmetic and copies ran while one was open for 2% of the time, Pallas kernels for 11%

profile of v6, /device:TPU:0, one launch (start us, length us, event | category | flops | bytes accessed | tf_op | source)
XLA Modules:
  0.0 147.7 jit_solution(10703105565261603467)
XLA Ops:
  1.8 3.5 %collective-permute-start = (bf16[1,104,256]{2,1,0:T(8,128)(2,1)S(1)}, bf16[1,104,256]{2,1,0:T(8,128)(2,1)S(1)}, u32[]{:S(2)}, u32[]{:S(2)}) collective-permute-start(bf16[1,104,256]{2,1,0:T(8,128)(2,1)S(1)} %reshape.42), channel_id=1, source_target_pairs={{0,17},{1,16},{2,19},{3,18},{4,21},{5,20},{6,23},{7,22},{8,25},{9,... | collective-permute-start | bytes 159752 | tf_op jit(solution)/shard_map/ppermute | solution.py:802
  7.6 2.4 %collective-permute-start.1 = (bf16[2,104,256]{2,1,0:T(8,128)(2,1)S(1)}, bf16[2,104,256]{2,1,0:T(8,128)(2,1)S(1)}, u32[]{:S(2)}, u32[]{:S(2)}) collective-permute-start(bf16[2,104,256]{2,1,0:T(8,128)(2,1)S(1)} %pad_maximum_fusion.1), channel_id=1, source_target_pairs={{0,9},{1,2},{2,1},{3,10},{4,7},{5,12},{6,15},{7,4},{8,11},{9,0},{1... | collective-permute-start | bytes 319496 | tf_op jit(solution)/shard_map/ppermute | solution.py:802
  10.1 2.3 %collective-permute-done.1 = bf16[2,104,256]{2,1,0:T(8,128)(2,1)S(1)} collective-permute-done((bf16[2,104,256]{2,1,0:T(8,128)(2,1)S(1)}, bf16[2,104,256]{2,1,0:T(8,128)(2,1)S(1)}, u32[]{:S(2)}, u32[]{:S(2)}) %collective-permute-start.1) | collective-permute-done | bytes 106528 | tf_op jit(solution)/shard_map/ppermute | solution.py:802
  12.4 2.4 %collective-permute-start.2 = (bf16[4,104,256]{2,1,0:T(8,128)(2,1)S(1)}, bf16[4,104,256]{2,1,0:T(8,128)(2,1)S(1)}, u32[]{:S(2)}, u32[]{:S(2)}) collective-permute-start(bf16[4,104,256]{2,1,0:T(8,128)(2,1)S(1)} %pad_maximum_fusion), channel_id=1, source_target_pairs={{0,5},{1,8},{2,11},{3,6},{4,13},{5,0},{6,3},{7,14},{8,1},{9,12},{1... | collective-permute-start | bytes 638984 | tf_op jit(solution)/shard_map/ppermute | solution.py:802
  16.0 2.3 %collective-permute-done.2 = bf16[4,104,256]{2,1,0:T(8,128)(2,1)S(1)} collective-permute-done((bf16[4,104,256]{2,1,0:T(8,128)(2,1)S(1)}, bf16[4,104,256]{2,1,0:T(8,128)(2,1)S(1)}, u32[]{:S(2)}, u32[]{:S(2)}) %collective-permute-start.2) | collective-permute-done | bytes 213024 | tf_op jit(solution)/shard_map/ppermute | solution.py:802
  20.7 3.0 %prep_kernel.1 = (bf16[4096,256]{1,0:T(8,128)(2,1)}, bf16[4096,256]{1,0:T(8,128)(2,1)}, f32[2048,128]{1,0:T(8,128)S(1)}) custom-call(s32[19]{0:T(128)S(1)} %pad_add_fusion.info_ref, s32[2,8,256]{2,1,0:T(8,128)S(1)} %reshape.43.src_ref, s32[2,8,256]{2,1,0:T(8,128)S(1)} %reshape.44.dst_ref, s32[2,8,256]{2,1,0:T(8,128)S(1)} %reshape.45.mask_ref, ...), custom_call_target="tpu_custom_call" | custom-call | flops 5000000000 | bytes 5000000 | tf_op jit(solution)/shard_map/prep_kernel/pallas_call | solution.py:747
  23.7 3.2 %collective-permute-done.3.far_ref = bf16[8,104,256]{2,1,0:T(8,128)(2,1)S(1)} collective-permute-done((bf16[8,104,256]{2,1,0:T(8,128)(2,1)}, bf16[8,104,256]{2,1,0:T(8,128)(2,1)S(1)}, u32[]{:S(2)}, u32[]{:S(2)}) %collective-permute-start.3) | collective-permute-done | bytes 426016 | tf_op jit(solution)/shard_map/ppermute | solution.py:802
  29.7 10.5 %forward_kernel.1 = (f32[2048,256]{1,0:T(8,128)S(1)}, bf16[2048,256]{1,0:T(8,128)(2,1)S(1)}, bf16[2048,256]{1,0:T(8,128)(2,1)S(1)}, bf16[2048,256]{1,0:T(8,128)(...) custom-call(s32[19]{0:T(128)S(1)} %pad_add_fusion.info_ref, ...), custom_call_target="tpu_custom_call" | custom-call | flops 5000000000 | bytes 5000000 | tf_op jit(solution)/shard_map/forward_kernel/pallas_call | solution.py:747
  50.7 2.8 %collective-permute-start.10 = (f32[8,256]{1,0:T(8,128)S(1)}, f32[8,256]{1,0:T(8,128)S(1)}, u32[]{:S(2)}, u32[]{:S(2)}) collective-permute-start(f32[8,256]{1,0:T(8,128)S(1)} %add.91), channel_id=1, source_target_pairs={{0,17},{1,16},{2,19},{3,18},{4,21},{5,20},{6,23},{7,22},{8,25},{9,... | collective-permute-start | bytes 24584 | tf_op jit(solution)/shard_map/ppermute | solution.py:768
  54.9 3.8 %mix_kernel.1 = (bf16[2048,256]{1,0:T(8,128)(2,1)S(1)}, bf16[2048,512]{1,0:T(8,128)(2,1)S(1)}, bf16[2048,512]{1,0:T(8,128)(2,1)S(1)}, f32[2048,256]{1,0:T(8,128)S(1)}, f32[8,256]{1,0:T(8,128)S(1)}) custom-call(s32[19]{0:T(128)S(1)} %pad_add_fusion.info_ref, f32[2048,256]{1,0:T(8,128)S(1)} %get-tuple-element.95.local_ref, ...), custom_call_target="tpu_custom_call" | custom-call | flops 5000000000 | bytes 5000000 | tf_op jit(solution)/shard_map/mix_kernel/pallas_call | solution.py:747
  69.2 2.7 %collective-permute-start.15 = (f32[8,256]{1,0:T(8,128)S(1)}, f32[8,256]{1,0:T(8,128)S(1)}, u32[]{:S(2)}, u32[]{:S(2)}) collective-permute-start(f32[8,256]{1,0:T(8,128)S(1)} %add.96), channel_id=1, source_target_pairs={{0,17},{1,16},{2,19},{3,18},{4,21},{5,20},{6,23},{7,22},{8,25},{9,... | collective-permute-start | bytes 24584 | tf_op jit(solution)/shard_map/ppermute | solution.py:768
  73.2 2.9 %mix_back_kernel.1 = (bf16[2048,256]{1,0:T(8,128)(2,1)S(1)}, bf16[2048,512]{1,0:T(8,128)(2,1)S(1)}, bf16[2048,256]{1,0:T(8,128)(2,1)S(1)}, f32[8,256]{1,0:T(8,128)S(1)}) custom-call(s32[19]{0:T(128)S(1)} %pad_add_fusion.info_ref, f32[2048,256]{1,0:T(8,128)S(1)} %get-tuple-element.98.mixed_ref, bf16[2048,512]{1,0:T(8,128)(2,1)S(1)} %get-tuple-element.99.slope_ref, ...), custom_call_target="tpu_custom_call" | custom-call | flops 5000000000 | bytes 5000000 | tf_op jit(solution)/shard_map/mix_back_kernel/pallas_call | solution.py:747
  78.8 2.1 %inner_grad_kernel.1 = (f32[256,512]{1,0:T(8,128)S(1)}, f32[8,512]{1,0:T(8,128)S(1)}) custom-call(s32[19]{0:T(128)S(1)} %pad_add_fusion.info_ref, bf16[2048,256]{1,0:T(8,128)(2,1)S(1)} %get-tuple-element.109.slow_ref, bf16[2048,512]{1,0:T(8,128)(2,1)S(1)} %get-tuple-element.110.dhid_ref), custom_call_target="tpu_custom_call" | custom-call | flops 5000000000 | bytes 5000000 | tf_op jit(solution)/shard_map/inner_grad_kernel/pallas_call | solution.py:747
  87.6 2.7 %collective-permute-start.20 = (f32[8,256]{1,0:T(8,128)S(1)}, f32[8,256]{1,0:T(8,128)S(1)}, u32[]{:S(2)}, u32[]{:S(2)}) collective-permute-start(f32[8,256]{1,0:T(8,128)S(1)} %add.101), channel_id=1, source_target_pairs={{0,17},{1,16},{2,19},{3,18},{4,21},{5,20},{6,23},{7,22},{8,25},{9,... | collective-permute-start | bytes 24584 | tf_op jit(solution)/shard_map/ppermute | solution.py:768
  91.6 10.9 %back_kernel.1 = (bf16[2048,1024]{1,0:T(8,128)(2,1)S(1)}, bf16[4096,256]{1,0:T(8,128)(2,1)S(1)}, f32[8,256]{1,0:T(8,128)S(1)}, bf16[2048,768]{1,0:T(8,128)(2,1)S...) custom-call(s32[19]{0:T(128)S(1)} %pad_add_fusion.info_ref, bf16[2048,256]{1,0:T(8,128)(2,1)S(1)} %get-tuple-element.121.dsum_ref, ...), custom_call_target="tpu_custom_call" | custom-call | flops 5000000000 | bytes 5000000 | tf_op jit(solution)/shard_map/back_kernel/pallas_call | solution.py:747
  102.5 3.8 %branch_grad_kernel.1 = (bf16[8,104,256]{2,1,0:T(8,128)(2,1)S(1)}, bf16[8,104,256]{2,1,0:T(8,128)(2,1)S(1)}, bf16[8,104,256]{2,1,0:T(8,128)(2,1)S(1)}, bf16[8,104,256]{2,1,0:T(8,128)(2,1)S(1)}, f32[8,512]{1,0:T(8,128)S(1)}) custom-call(s32[19]{0:T(128)S(1)} %pad_add_fusion.info_ref, bf16[2048,256]{1,0:T(8,128)(2,1)S(1)} %constant_dynamic-slice_fusion.1.x_ref, ...), custom_call_target="tpu_custom_call" | custom-call | flops 5000000000 | bytes 5000000 | tf_op jit(solution)/shard_map/branch_grad_kernel/pallas_call | solution.py:747
  109.3 4.3 %node_grad_kernel.1 = f32[2048,256]{1,0:T(8,128)} custom-call(s32[19]{0:T(128)S(1)} %pad_add_fusion.info_ref, bf16[2048,256]{1,0:T(8,128)(2,1)S(1)} %get-tuple-element.121.dsum_ref, bf16[2048,256]{1,0:T(8,128)(2,1)S(1)} %get-tuple-element.104.lhat_ref, bf16[2048,256]{1,0:T(8,128)(2,1)S(1)} %get-tuple-element.105.ghat_ref, ...), custom_call_target="tpu_custom_call" | custom-call | flops 5000000000 | bytes 5000000 | tf_op jit(solution)/shard_map/node_grad_kernel/pallas_call | solution.py:747
  113.6 2.3 %collective-permute-done.22 = bf16[8,104,256]{2,1,0:T(8,128)(2,1)S(1)} collective-permute-done((bf16[8,104,256]{2,1,0:T(8,128)(2,1)S(1)}, bf16[8,104,256]{2,1,0:T(8,128)(2,1)S(1)}, u32[]{:S(2)}, u32[]{:S(2)}) %collective-permute-start.22) | collective-permute-done | bytes 426016 | tf_op jit(solution)/shard_map/ppermute | solution.py:802
  117.3 3.0 %edge_grad_kernel.1 = f32[4096,256]{1,0:T(8,128)} custom-call(s32[19]{0:T(128)S(1)} %pad_add_fusion.info_ref, bf16[4096,256]{1,0:T(8,128)(2,1)S(1)} %get-tuple-element.134.dedge_ref, bf16[13,256,256]{2,1,0:T(8,128)(2,1)S(1)} %assemble_kernel.1.w_ref), custom_call_target="tpu_custom_call" | custom-call | flops 5000000000 | bytes 5000000 | tf_op jit(solution)/shard_map/edge_grad_kernel/pallas_call | solution.py:747
  122.6 3.0 %collective-permute-done.25.got_ref = bf16[2,104,256]{2,1,0:T(8,128)(2,1)S(1)} collective-permute-done((bf16[2,104,256]{2,1,0:T(8,128)(2,1)S(1)}, bf16[2,104,256]{2,1,0:T(8,128)(2,1)S(1)}, u32[]{:S(2)}, u32[]{:S(2)}) %collective-permute-start.25) | collective-permute-done | bytes 106528 | tf_op jit(solution)/shard_map/ppermute | solution.py:802
  126.2 2.8 %collective-permute-start.26 = (bf16[2,112,256]{2,1,0:T(8,128)(2,1)S(1)}, bf16[2,112,256]{2,1,0:T(8,128)(2,1)S(1)}, u32[]{:S(2)}, u32[]{:S(2)}) collective-permute-start(bf16[2,112,256]{2,1,0:T(8,128)(2,1)S(1)} %last_kernel.1.mine_ref), channel_id=1, source_target_pairs={{0,16},{1,17},{2,18},{3,19},{4,20},{5,21},{6,22},{7,23},{8,24},{9,... | collective-permute-start | bytes 344072 | tf_op jit(solution)/shard_map/ppermute | solution.py:802
  129.0 6.0 %collective-permute-done.26.got_ref = bf16[2,112,256]{2,1,0:T(8,128)(2,1)S(1)} collective-permute-done((bf16[2,112,256]{2,1,0:T(8,128)(2,1)S(1)}, bf16[2,112,256]{2,1,0:T(8,128)(2,1)S(1)}, u32[]{:S(2)}, u32[]{:S(2)}) %collective-permute-start.26) | collective-permute-done | bytes 114720 | tf_op jit(solution)/shard_map/ppermute | solution.py:802
  137.6 2.3 %collective-permute-done.28 = f32[8,256]{1,0:T(8,128)S(1)} collective-permute-done((f32[8,256]{1,0:T(8,128)S(1)}, f32[8,256]{1,0:T(8,128)S(1)}, u32[]{:S(2)}, u32[]{:S(2)}) %collective-permute-start.28) | collective-permute-done | bytes 8224 | tf_op jit(solution)/shard_map/ppermute | solution.py:768
  143.3 2.8 %collective-permute-done.30 = f32[8,256]{1,0:T(8,128)S(1)} collective-permute-done((f32[8,256]{1,0:T(8,128)S(1)}, f32[8,256]{1,0:T(8,128)S(1)}, u32[]{:S(2)}, u32[]{:S(2)}) %collective-permute-start.30) | collective-permute-done | bytes 8224 | tf_op jit(solution)/shard_map/ppermute | solution.py:768
  (132 shorter events, 59.0 us)
Async XLA Ops:
  1.8 5.8 %collective-permute-start = (bf16[1,104,256]{2,1,0:T(8,128)(2,1)S(1)}, bf16[1,104,256]{2,1,0:T(8,128)(2,1)S(1)}, u32[]{:S(2)}, u32[]{:S(2)}) collective-permute-start(bf16[1,104,256]{2,1,0:T(8,128)(2,1)S(1)} %reshape.42), channel_id=1, source_target_pairs={{0,17},{1,16},{2,19},{3,18},{4,21},{5,20},{6,23},{7,22},{8,25},{9,... | collective-permute-start | bytes 159752 | tf_op jit(solution)/shard_map/ppermute | solution.py:802
  7.6 4.8 %collective-permute-start.1 = (bf16[2,104,256]{2,1,0:T(8,128)(2,1)S(1)}, bf16[2,104,256]{2,1,0:T(8,128)(2,1)S(1)}, u32[]{:S(2)}, u32[]{:S(2)}) collective-permute-start(bf16[2,104,256]{2,1,0:T(8,128)(2,1)S(1)} %pad_maximum_fusion.1), channel_id=1, source_target_pairs={{0,9},{1,2},{2,1},{3,10},{4,7},{5,12},{6,15},{7,4},{8,11},{9,0},{1... | collective-permute-start | bytes 319496 | tf_op jit(solution)/shard_map/ppermute | solution.py:802
  12.4 5.9 %collective-permute-start.2 = (bf16[4,104,256]{2,1,0:T(8,128)(2,1)S(1)}, bf16[4,104,256]{2,1,0:T(8,128)(2,1)S(1)}, u32[]{:S(2)}, u32[]{:S(2)}) collective-permute-start(bf16[4,104,256]{2,1,0:T(8,128)(2,1)S(1)} %pad_maximum_fusion), channel_id=1, source_target_pairs={{0,5},{1,8},{2,11},{3,6},{4,13},{5,0},{6,3},{7,14},{8,1},{9,12},{1... | collective-permute-start | bytes 638984 | tf_op jit(solution)/shard_map/ppermute | solution.py:802
  19.0 4.7 %collective-permute-start.4 = (bf16[8,104,256]{2,1,0:T(8,128)(2,1)}, bf16[8,104,256]{2,1,0:T(8,128)(2,1)S(1)}, u32[]{:S(2)}, u32[]{:S(2)}) collective-permute-start(bf16[8,104,256]{2,1,0:T(8,128)(2,1)} %constant_dynamic-update-slice_fusion.near_ref), channel_id=1, source_target_pairs={{0,1},{1,0},{2,3},{3,2},{4,5},{5,4},{6,7},{7,6},{8,9},{9,8},{10,11... | collective-permute-start | bytes 1277960 | tf_op jit(solution)/shard_map/ppermute | solution.py:768
  19.1 7.8 %collective-permute-start.3 = (bf16[8,104,256]{2,1,0:T(8,128)(2,1)}, bf16[8,104,256]{2,1,0:T(8,128)(2,1)S(1)}, u32[]{:S(2)}, u32[]{:S(2)}) collective-permute-start(bf16[8,104,256]{2,1,0:T(8,128)(2,1)} %constant_dynamic-update-slice_fusion.near_ref), channel_id=1, source_target_pairs={{0,3},{1,4},{2,7},{3,0},{4,1},{5,6},{6,5},{7,2},{8,13},{9,10},{10,... | collective-permute-start | bytes 1277960 | tf_op jit(solution)/shard_map/ppermute | solution.py:802
  41.5 3.1 %collective-permute-start.7 = (f32[8,256]{1,0:T(8,128)S(1)}, f32[8,256]{1,0:T(8,128)S(1)}, u32[]{:S(2)}, u32[]{:S(2)}) collective-permute-start(f32[8,256]{1,0:T(8,128)S(1)} %add.88), channel_id=1, source_target_pairs={{0,3},{1,2},{2,1},{3,0},{4,7},{5,6},{6,5},{7,4},{8,11},{9,10},{10,... | collective-permute-start | bytes 24584 | tf_op jit(solution)/shard_map/ppermute | solution.py:768
  44.5 3.1 %collective-permute-start.8 = (f32[8,256]{1,0:T(8,128)S(1)}, f32[8,256]{1,0:T(8,128)S(1)}, u32[]{:S(2)}, u32[]{:S(2)}) collective-permute-start(f32[8,256]{1,0:T(8,128)S(1)} %add.89), channel_id=1, source_target_pairs={{0,5},{1,4},{2,7},{3,6},{4,1},{5,0},{6,3},{7,2},{8,13},{9,12},{10,... | collective-permute-start | bytes 24584 | tf_op jit(solution)/shard_map/ppermute | solution.py:768
  47.6 3.1 %collective-permute-start.9 = (f32[8,256]{1,0:T(8,128)S(1)}, f32[8,256]{1,0:T(8,128)S(1)}, u32[]{:S(2)}, u32[]{:S(2)}) collective-permute-start(f32[8,256]{1,0:T(8,128)S(1)} %add.90), channel_id=1, source_target_pairs={{0,9},{1,8},{2,11},{3,10},{4,13},{5,12},{6,15},{7,14},{8,1},{9,0},... | collective-permute-start | bytes 24584 | tf_op jit(solution)/shard_map/ppermute | solution.py:768
  50.7 4.2 %collective-permute-start.10 = (f32[8,256]{1,0:T(8,128)S(1)}, f32[8,256]{1,0:T(8,128)S(1)}, u32[]{:S(2)}, u32[]{:S(2)}) collective-permute-start(f32[8,256]{1,0:T(8,128)S(1)} %add.91), channel_id=1, source_target_pairs={{0,17},{1,16},{2,19},{3,18},{4,21},{5,20},{6,23},{7,22},{8,25},{9,... | collective-permute-start | bytes 24584 | tf_op jit(solution)/shard_map/ppermute | solution.py:768
  59.9 3.1 %collective-permute-start.12 = (f32[8,256]{1,0:T(8,128)S(1)}, f32[8,256]{1,0:T(8,128)S(1)}, u32[]{:S(2)}, u32[]{:S(2)}) collective-permute-start(f32[8,256]{1,0:T(8,128)S(1)} %add.93), channel_id=1, source_target_pairs={{0,3},{1,2},{2,1},{3,0},{4,7},{5,6},{6,5},{7,4},{8,11},{9,10},{10,... | collective-permute-start | bytes 24584 | tf_op jit(solution)/shard_map/ppermute | solution.py:768
  63.0 3.1 %collective-permute-start.13 = (f32[8,256]{1,0:T(8,128)S(1)}, f32[8,256]{1,0:T(8,128)S(1)}, u32[]{:S(2)}, u32[]{:S(2)}) collective-permute-start(f32[8,256]{1,0:T(8,128)S(1)} %add.94), channel_id=1, source_target_pairs={{0,5},{1,4},{2,7},{3,6},{4,1},{5,0},{6,3},{7,2},{8,13},{9,12},{10,... | collective-permute-start | bytes 24584 | tf_op jit(solution)/shard_map/ppermute | solution.py:768
  66.1 3.1 %collective-permute-start.14 = (f32[8,256]{1,0:T(8,128)S(1)}, f32[8,256]{1,0:T(8,128)S(1)}, u32[]{:S(2)}, u32[]{:S(2)}) collective-permute-start(f32[8,256]{1,0:T(8,128)S(1)} %add.95), channel_id=1, source_target_pairs={{0,9},{1,8},{2,11},{3,10},{4,13},{5,12},{6,15},{7,14},{8,1},{9,0},... | collective-permute-start | bytes 24584 | tf_op jit(solution)/shard_map/ppermute | solution.py:768
  69.2 4.0 %collective-permute-start.15 = (f32[8,256]{1,0:T(8,128)S(1)}, f32[8,256]{1,0:T(8,128)S(1)}, u32[]{:S(2)}, u32[]{:S(2)}) collective-permute-start(f32[8,256]{1,0:T(8,128)S(1)} %add.96), channel_id=1, source_target_pairs={{0,17},{1,16},{2,19},{3,18},{4,21},{5,20},{6,23},{7,22},{8,25},{9,... | collective-permute-start | bytes 24584 | tf_op jit(solution)/shard_map/ppermute | solution.py:768
  77.4 3.5 %collective-permute-start.17 = (f32[8,256]{1,0:T(8,128)S(1)}, f32[8,256]{1,0:T(8,128)S(1)}, u32[]{:S(2)}, u32[]{:S(2)}) collective-permute-start(f32[8,256]{1,0:T(8,128)S(1)} %add.98), channel_id=1, source_target_pairs={{0,3},{1,2},{2,1},{3,0},{4,7},{5,6},{6,5},{7,4},{8,11},{9,10},{10,... | collective-permute-start | bytes 24584 | tf_op jit(solution)/shard_map/ppermute | solution.py:768
  80.9 3.1 %collective-permute-start.18 = (f32[8,256]{1,0:T(8,128)S(1)}, f32[8,256]{1,0:T(8,128)S(1)}, u32[]{:S(2)}, u32[]{:S(2)}) collective-permute-start(f32[8,256]{1,0:T(8,128)S(1)} %add.99), channel_id=1, source_target_pairs={{0,5},{1,4},{2,7},{3,6},{4,1},{5,0},{6,3},{7,2},{8,13},{9,12},{10,... | collective-permute-start | bytes 24584 | tf_op jit(solution)/shard_map/ppermute | solution.py:768
  84.1 3.5 %collective-permute-start.19 = (f32[8,256]{1,0:T(8,128)S(1)}, f32[8,256]{1,0:T(8,128)S(1)}, u32[]{:S(2)}, u32[]{:S(2)}) collective-permute-start(f32[8,256]{1,0:T(8,128)S(1)} %add.100), channel_id=1, source_target_pairs={{0,9},{1,8},{2,11},{3,10},{4,13},{5,12},{6,15},{7,14},{8,1},{9,0},... | collective-permute-start | bytes 24584 | tf_op jit(solution)/shard_map/ppermute | solution.py:768
  87.6 4.0 %collective-permute-start.20 = (f32[8,256]{1,0:T(8,128)S(1)}, f32[8,256]{1,0:T(8,128)S(1)}, u32[]{:S(2)}, u32[]{:S(2)}) collective-permute-start(f32[8,256]{1,0:T(8,128)S(1)} %add.101), channel_id=1, source_target_pairs={{0,17},{1,16},{2,19},{3,18},{4,21},{5,20},{6,23},{7,22},{8,25},{9,... | collective-permute-start | bytes 24584 | tf_op jit(solution)/shard_map/ppermute | solution.py:768
  108.3 7.6 %collective-permute-start.22 = (bf16[8,104,256]{2,1,0:T(8,128)(2,1)S(1)}, bf16[8,104,256]{2,1,0:T(8,128)(2,1)S(1)}, u32[]{:S(2)}, u32[]{:S(2)}) collective-permute-start(bf16[8,104,256]{2,1,0:T(8,128)(2,1)S(1)} %add_convert_fusion), channel_id=1, source_target_pairs={{0,3},{1,4},{2,7},{3,0},{4,1},{5,6},{6,5},{7,2},{8,13},{9,10},{10,... | collective-permute-start | bytes 1277960 | tf_op jit(solution)/shard_map/ppermute | solution.py:802
  116.0 5.3 %collective-permute-start.24 = (bf16[4,104,256]{2,1,0:T(8,128)(2,1)S(1)}, bf16[4,104,256]{2,1,0:T(8,128)(2,1)S(1)}, u32[]{:S(2)}, u32[]{:S(2)}) collective-permute-start(bf16[4,104,256]{2,1,0:T(8,128)(2,1)S(1)} %get-tuple-element.163), channel_id=1, source_target_pairs={{0,5},{1,8},{2,11},{3,6},{4,13},{5,0},{6,3},{7,14},{8,1},{9,12},{1... | collective-permute-start | bytes 638984 | tf_op jit(solution)/shard_map/ppermute | solution.py:802
  121.4 4.2 %collective-permute-start.25 = (bf16[2,104,256]{2,1,0:T(8,128)(2,1)S(1)}, bf16[2,104,256]{2,1,0:T(8,128)(2,1)S(1)}, u32[]{:S(2)}, u32[]{:S(2)}) collective-permute-start(bf16[2,104,256]{2,1,0:T(8,128)(2,1)S(1)} %get-tuple-element.164), channel_id=1, source_target_pairs={{0,9},{1,2},{2,1},{3,10},{4,7},{5,12},{6,15},{7,4},{8,11},{9,0},{1... | collective-permute-start | bytes 319496 | tf_op jit(solution)/shard_map/ppermute | solution.py:802
  126.2 8.8 %collective-permute-start.26 = (bf16[2,112,256]{2,1,0:T(8,128)(2,1)S(1)}, bf16[2,112,256]{2,1,0:T(8,128)(2,1)S(1)}, u32[]{:S(2)}, u32[]{:S(2)}) collective-permute-start(bf16[2,112,256]{2,1,0:T(8,128)(2,1)S(1)} %last_kernel.1.mine_ref), channel_id=1, source_target_pairs={{0,16},{1,17},{2,18},{3,19},{4,20},{5,21},{6,22},{7,23},{8,24},{9,... | collective-permute-start | bytes 344072 | tf_op jit(solution)/shard_map/ppermute | solution.py:802
  136.9 3.1 %collective-permute-start.28 = (f32[8,256]{1,0:T(8,128)S(1)}, f32[8,256]{1,0:T(8,128)S(1)}, u32[]{:S(2)}, u32[]{:S(2)}) collective-permute-start(f32[8,256]{1,0:T(8,128)S(1)} %add.109), channel_id=1, source_target_pairs={{0,3},{1,2},{2,1},{3,0},{4,7},{5,6},{6,5},{7,4},{8,11},{9,10},{10,... | collective-permute-start | bytes 24584 | tf_op jit(solution)/shard_map/ppermute | solution.py:768
  139.9 3.1 %collective-permute-start.29 = (f32[8,256]{1,0:T(8,128)S(1)}, f32[8,256]{1,0:T(8,128)S(1)}, u32[]{:S(2)}, u32[]{:S(2)}) collective-permute-start(f32[8,256]{1,0:T(8,128)S(1)} %add.110), channel_id=1, source_target_pairs={{0,5},{1,4},{2,7},{3,6},{4,1},{5,0},{6,3},{7,2},{8,13},{9,12},{10,... | collective-permute-start | bytes 24584 | tf_op jit(solution)/shard_map/ppermute | solution.py:768
  143.0 3.1 %collective-permute-start.30 = (f32[8,256]{1,0:T(8,128)S(1)}, f32[8,256]{1,0:T(8,128)S(1)}, u32[]{:S(2)}, u32[]{:S(2)}) collective-permute-start(f32[8,256]{1,0:T(8,128)S(1)} %add.111), channel_id=1, source_target_pairs={{0,9},{1,8},{2,11},{3,10},{4,13},{5,12},{6,15},{7,14},{8,1},{9,0},... | collective-permute-start | bytes 24584 | tf_op jit(solution)/shard_map/ppermute | solution.py:768
  (25 other events, 187.0 us)

commit v7 on v6

--- a/solution.py
+++ b/solution.py
@@ -806,12 +806,29 @@
     return width * width // total == 8 * width
 
 
+def cast_kernel(info_ref, w_ref, out_ref, hold_ref):
+    mats, span = w_ref.shape
+    half = hold_ref.shape[2]
+    for piece in range(span // half):
+        hold_ref[piece % 2, pl.ds(piece // 2, mats, 8), :] = w_ref[
+            :, piece * half : (piece + 1) * half
+        ]
+    out_ref[0] = low(jnp.concatenate([hold_ref[0], hold_ref[1]], axis=1))
+
+
 def gather_matrices(shard, info, total, width, work):
     mats = shard.shape[0]
     if not in_rows(total, width):
-        gathered = lax.all_gather(shard, axis_names, axis=1, tiled=True)
+        gathered = lax.all_gather(low(shard), axis_names, axis=1, tiled=True)
         return (gathered.reshape(mats, width, width), work(info))
-    held = shard.reshape(1, mats * 8, width)
+    held = call(
+        cast_kernel,
+        1,
+        jnp.zeros((1,), jnp.int32),
+        [(shard, None)],
+        [((1, mats * 8, width), bf16, None)],
+        [pltpu.VMEM((2, mats * 8, width // 2), f32)],
+    )[0]
     for number in reversed(range(1, len(chip_orders(total)[0]))):
         held = jnp.concatenate([held, swap_chips(held, number, total)], axis=0)
     got = swap_chips(held, 0, total)
@@ -924,7 +941,6 @@
     steps = blocks // group
     tall = group * BLOCK
     tall_edges = group * EB
-    w_bf = low(weights)
     own_nodes = own_half(node_feats, branch_index)
     own_edges = own_half(edge_feats, branch_index)
     counts = jnp.sum(own_half(node_mask, branch_index).reshape(blocks, BLOCK), axis=1)
@@ -958,7 +974,7 @@
             ],
         )
 
-    matrices, (hot, turned, bias) = gather_matrices(w_bf, info, total, width, prep_work)
+    matrices, (hot, turned, bias) = gather_matrices(weights, info, total, width, prep_work)
     x_in = (own_nodes, node_spec)
     e_in = (own_edges, edge_spec)
     mats_in = (matrices, None)

time: 148 us -> 148 us (level)
  local copies, waits for them, and re-layouts: 3.37 us -> 1.71 us
  waiting for transfers between devices: 47.4 us -> 48.9 us
    ppermute x8, waiting for transfers between devices: 21.3 us -> 22.9 us  [swap_chips(): return lax.ppermute(values, axis_names, pairs)]
    pallas_call x16 -> x17, Pallas kernels: 52.2 us -> 53.3 us  [call(): pl.pallas_call(kernel, grid_spec=pltpu.PrefetchScalarGridSpec(num_scalar_...]
  transfers between devices with their start and end apart: 31 -> 31, of which waited for: 27 -> 27; matrix products, arithmetic and copies ran while one was open for 2% -> 0% of each run, Pallas kernels for 11% -> 11%
where the time goes in v7:
time: 148 us
  Pallas kernels  53.3 us (36%)
  waiting for transfers between devices  48.9 us (33%)
  starting transfers between devices  42.2 us (29%)
  local copies, waits for them, and re-layouts  1.71 us (1%)
    pallas_call x17, Pallas kernels, call(): pl.pallas_call(kernel, grid_spec=pltpu.PrefetchScalarGridSpec(num_scalar_...  53.3 us
    ppermute x23, starting transfers between devices, swap_with(): lax.ppermute(values, axis_names, [(place, place ^ step) for place in rang...  26 us
    ppermute x23, waiting for transfers between devices, swap_with(): lax.ppermute(values, axis_names, [(place, place ^ step) for place in rang...  26 us
    ppermute x8, waiting for transfers between devices, swap_chips(): return lax.ppermute(values, axis_names, pairs)  22.9 us
    ppermute x8, starting transfers between devices, swap_chips(): return lax.ppermute(values, axis_names, pairs)  16.2 us
  transfers between devices with their start and end apart: 31, of which 27 were waited for; matrix products, arithmetic and copies ran while one was open for 0% of the time, Pallas kernels for 11%

profile of v7, /device:TPU:0, one launch (start us, length us, event | category | flops | bytes accessed | tf_op | source)
XLA Modules:
  0.0 148.0 jit_solution(3512091502881257905)
XLA Ops:
  1.8 3.5 %collective-permute-start = (bf16[1,104,256]{2,1,0:T(8,128)(2,1)S(1)}, bf16[1,104,256]{2,1,0:T(8,128)(2,1)S(1)}, u32[]{:S(2)}, u32[]{:S(2)}) collective-permute-start(bf16[1,104,256]{2,1,0:T(8,128)(2,1)S(1)} %cast_kernel.1), channel_id=1, source_target_pairs={{0,17},{1,16},{2,19},{3,18},{4,21},{5,20},{6,23},{7,22},{8,25},{9,... | collective-permute-start | bytes 159752 | tf_op jit(solution)/shard_map/ppermute | solution.py:802
  7.6 2.4 %collective-permute-start.1 = (bf16[2,104,256]{2,1,0:T(8,128)(2,1)S(1)}, bf16[2,104,256]{2,1,0:T(8,128)(2,1)S(1)}, u32[]{:S(2)}, u32[]{:S(2)}) collective-permute-start(bf16[2,104,256]{2,1,0:T(8,128)(2,1)S(1)} %pad_maximum_fusion.2), channel_id=1, source_target_pairs={{0,9},{1,2},{2,1},{3,10},{4,7},{5,12},{6,15},{7,4},{8,11},{9,0},{1... | collective-permute-start | bytes 319496 | tf_op jit(solution)/shard_map/ppermute | solution.py:802
  10.0 2.3 %collective-permute-done.1 = bf16[2,104,256]{2,1,0:T(8,128)(2,1)S(1)} collective-permute-done((bf16[2,104,256]{2,1,0:T(8,128)(2,1)S(1)}, bf16[2,104,256]{2,1,0:T(8,128)(2,1)S(1)}, u32[]{:S(2)}, u32[]{:S(2)}) %collective-permute-start.1) | collective-permute-done | bytes 106528 | tf_op jit(solution)/shard_map/ppermute | solution.py:802
  12.3 2.4 %collective-permute-start.2 = (bf16[4,104,256]{2,1,0:T(8,128)(2,1)S(1)}, bf16[4,104,256]{2,1,0:T(8,128)(2,1)S(1)}, u32[]{:S(2)}, u32[]{:S(2)}) collective-permute-start(bf16[4,104,256]{2,1,0:T(8,128)(2,1)S(1)} %pad_maximum_fusion.1), channel_id=1, source_target_pairs={{0,5},{1,8},{2,11},{3,6},{4,13},{5,0},{6,3},{7,14},{8,1},{9,12},{1... | collective-permute-start | bytes 638984 | tf_op jit(solution)/shard_map/ppermute | solution.py:802
  14.8 3.5 %collective-permute-done.2 = bf16[4,104,256]{2,1,0:T(8,128)(2,1)S(1)} collective-permute-done((bf16[4,104,256]{2,1,0:T(8,128)(2,1)S(1)}, bf16[4,104,256]{2,1,0:T(8,128)(2,1)S(1)}, u32[]{:S(2)}, u32[]{:S(2)}) %collective-permute-start.2) | collective-permute-done | bytes 213024 | tf_op jit(solution)/shard_map/ppermute | solution.py:802
  20.2 3.0 %prep_kernel.1 = (bf16[4096,256]{1,0:T(8,128)(2,1)}, bf16[4096,256]{1,0:T(8,128)(2,1)}, f32[2048,128]{1,0:T(8,128)S(1)}) custom-call(s32[19]{0:T(128)S(1)} %pad_add_fusion.info_ref, s32[2,8,256]{2,1,0:T(8,128)S(1)} %reshape.39.src_ref, s32[2,8,256]{2,1,0:T(8,128)S(1)} %reshape.40.dst_ref, s32[2,8,256]{2,1,0:T(8,128)S(1)} %reshape.41.mask_ref, ...), custom_call_target="tpu_custom_call" | custom-call | flops 5000000000 | bytes 5000000 | tf_op jit(solution)/shard_map/prep_kernel/pallas_call | solution.py:747
  23.1 2.9 %collective-permute-done.3.far_ref = bf16[8,104,256]{2,1,0:T(8,128)(2,1)S(1)} collective-permute-done((bf16[8,104,256]{2,1,0:T(8,128)(2,1)S(1)}, bf16[8,104,256]{2,1,0:T(8,128)(2,1)S(1)}, u32[]{:S(2)}, u32[]{:S(2)}) %collective-permute-start.3) | collective-permute-done | bytes 426016 | tf_op jit(solution)/shard_map/ppermute | solution.py:802
  28.8 11.0 %forward_kernel.1 = (f32[2048,256]{1,0:T(8,128)S(1)}, bf16[2048,256]{1,0:T(8,128)(2,1)S(1)}, bf16[2048,256]{1,0:T(8,128)(2,1)S(1)}, bf16[2048,256]{1,0:T(8,128)(...) custom-call(s32[19]{0:T(128)S(1)} %pad_add_fusion.info_ref, ...), custom_call_target="tpu_custom_call" | custom-call | flops 5000000000 | bytes 5000000 | tf_op jit(solution)/shard_map/forward_kernel/pallas_call | solution.py:747
  50.3 2.8 %collective-permute-start.10 = (f32[8,256]{1,0:T(8,128)S(1)}, f32[8,256]{1,0:T(8,128)S(1)}, u32[]{:S(2)}, u32[]{:S(2)}) collective-permute-start(f32[8,256]{1,0:T(8,128)S(1)} %add.91), channel_id=1, source_target_pairs={{0,17},{1,16},{2,19},{3,18},{4,21},{5,20},{6,23},{7,22},{8,25},{9,... | collective-permute-start | bytes 24584 | tf_op jit(solution)/shard_map/ppermute | solution.py:768
  54.5 3.8 %mix_kernel.1 = (bf16[2048,256]{1,0:T(8,128)(2,1)S(1)}, bf16[2048,512]{1,0:T(8,128)(2,1)S(1)}, bf16[2048,512]{1,0:T(8,128)(2,1)S(1)}, f32[2048,256]{1,0:T(8,128)S(1)}, f32[8,256]{1,0:T(8,128)S(1)}) custom-call(s32[19]{0:T(128)S(1)} %pad_add_fusion.info_ref, f32[2048,256]{1,0:T(8,128)S(1)} %get-tuple-element.95.local_ref, ...), custom_call_target="tpu_custom_call" | custom-call | flops 5000000000 | bytes 5000000 | tf_op jit(solution)/shard_map/mix_kernel/pallas_call | solution.py:747
  68.7 2.7 %collective-permute-start.15 = (f32[8,256]{1,0:T(8,128)S(1)}, f32[8,256]{1,0:T(8,128)S(1)}, u32[]{:S(2)}, u32[]{:S(2)}) collective-permute-start(f32[8,256]{1,0:T(8,128)S(1)} %add.96), channel_id=1, source_target_pairs={{0,17},{1,16},{2,19},{3,18},{4,21},{5,20},{6,23},{7,22},{8,25},{9,... | collective-permute-start | bytes 24584 | tf_op jit(solution)/shard_map/ppermute | solution.py:768
  72.8 2.9 %mix_back_kernel.1 = (bf16[2048,256]{1,0:T(8,128)(2,1)S(1)}, bf16[2048,512]{1,0:T(8,128)(2,1)S(1)}, bf16[2048,256]{1,0:T(8,128)(2,1)S(1)}, f32[8,256]{1,0:T(8,128)S(1)}) custom-call(s32[19]{0:T(128)S(1)} %pad_add_fusion.info_ref, f32[2048,256]{1,0:T(8,128)S(1)} %get-tuple-element.98.mixed_ref, bf16[2048,512]{1,0:T(8,128)(2,1)S(1)} %get-tuple-element.99.slope_ref, ...), custom_call_target="tpu_custom_call" | custom-call | flops 5000000000 | bytes 5000000 | tf_op jit(solution)/shard_map/mix_back_kernel/pallas_call | solution.py:747
  78.4 2.1 %inner_grad_kernel.1 = (f32[256,512]{1,0:T(8,128)S(1)}, f32[8,512]{1,0:T(8,128)S(1)}) custom-call(s32[19]{0:T(128)S(1)} %pad_add_fusion.info_ref, bf16[2048,256]{1,0:T(8,128)(2,1)S(1)} %get-tuple-element.109.slow_ref, bf16[2048,512]{1,0:T(8,128)(2,1)S(1)} %get-tuple-element.110.dhid_ref), custom_call_target="tpu_custom_call" | custom-call | flops 5000000000 | bytes 5000000 | tf_op jit(solution)/shard_map/inner_grad_kernel/pallas_call | solution.py:747
  87.2 2.7 %collective-permute-start.20 = (f32[8,256]{1,0:T(8,128)S(1)}, f32[8,256]{1,0:T(8,128)S(1)}, u32[]{:S(2)}, u32[]{:S(2)}) collective-permute-start(f32[8,256]{1,0:T(8,128)S(1)} %add.101), channel_id=1, source_target_pairs={{0,17},{1,16},{2,19},{3,18},{4,21},{5,20},{6,23},{7,22},{8,25},{9,... | collective-permute-start | bytes 24584 | tf_op jit(solution)/shard_map/ppermute | solution.py:768
  91.2 11.4 %back_kernel.1 = (bf16[2048,1024]{1,0:T(8,128)(2,1)S(1)}, bf16[4096,256]{1,0:T(8,128)(2,1)S(1)}, f32[8,256]{1,0:T(8,128)S(1)}, bf16[2048,768]{1,0:T(8,128)(2,1)S...) custom-call(s32[19]{0:T(128)S(1)} %pad_add_fusion.info_ref, bf16[2048,256]{1,0:T(8,128)(2,1)S(1)} %get-tuple-element.121.dsum_ref, ...), custom_call_target="tpu_custom_call" | custom-call | flops 5000000000 | bytes 5000000 | tf_op jit(solution)/shard_map/back_kernel/pallas_call | solution.py:747
  102.6 3.9 %branch_grad_kernel.1 = (bf16[8,104,256]{2,1,0:T(8,128)(2,1)S(1)}, bf16[8,104,256]{2,1,0:T(8,128)(2,1)S(1)}, bf16[8,104,256]{2,1,0:T(8,128)(2,1)S(1)}, bf16[8,104,256]{2,1,0:T(8,128)(2,1)S(1)}, f32[8,512]{1,0:T(8,128)S(1)}) custom-call(s32[19]{0:T(128)S(1)} %pad_add_fusion.info_ref, bf16[2048,256]{1,0:T(8,128)(2,1)S(1)} %constant_dynamic-slice_fusion.1.x_ref, ...), custom_call_target="tpu_custom_call" | custom-call | flops 5000000000 | bytes 5000000 | tf_op jit(solution)/shard_map/branch_grad_kernel/pallas_call | solution.py:747
  109.5 4.3 %node_grad_kernel.1 = f32[2048,256]{1,0:T(8,128)} custom-call(s32[19]{0:T(128)S(1)} %pad_add_fusion.info_ref, bf16[2048,256]{1,0:T(8,128)(2,1)S(1)} %get-tuple-element.121.dsum_ref, bf16[2048,256]{1,0:T(8,128)(2,1)S(1)} %get-tuple-element.104.lhat_ref, bf16[2048,256]{1,0:T(8,128)(2,1)S(1)} %get-tuple-element.105.ghat_ref, ...), custom_call_target="tpu_custom_call" | custom-call | flops 5000000000 | bytes 5000000 | tf_op jit(solution)/shard_map/node_grad_kernel/pallas_call | solution.py:747
  113.8 2.3 %collective-permute-done.22 = bf16[8,104,256]{2,1,0:T(8,128)(2,1)S(1)} collective-permute-done((bf16[8,104,256]{2,1,0:T(8,128)(2,1)S(1)}, bf16[8,104,256]{2,1,0:T(8,128)(2,1)S(1)}, u32[]{:S(2)}, u32[]{:S(2)}) %collective-permute-start.22) | collective-permute-done | bytes 426016 | tf_op jit(solution)/shard_map/ppermute | solution.py:802
  117.5 3.0 %edge_grad_kernel.1 = f32[4096,256]{1,0:T(8,128)} custom-call(s32[19]{0:T(128)S(1)} %pad_add_fusion.info_ref, bf16[4096,256]{1,0:T(8,128)(2,1)S(1)} %get-tuple-element.134.dedge_ref, bf16[13,256,256]{2,1,0:T(8,128)(2,1)S(1)} %assemble_kernel.1.w_ref), custom_call_target="tpu_custom_call" | custom-call | flops 5000000000 | bytes 5000000 | tf_op jit(solution)/shard_map/edge_grad_kernel/pallas_call | solution.py:747
  122.8 3.0 %collective-permute-done.25.got_ref = bf16[2,104,256]{2,1,0:T(8,128)(2,1)S(1)} collective-permute-done((bf16[2,104,256]{2,1,0:T(8,128)(2,1)S(1)}, bf16[2,104,256]{2,1,0:T(8,128)(2,1)S(1)}, u32[]{:S(2)}, u32[]{:S(2)}) %collective-permute-start.25) | collective-permute-done | bytes 106528 | tf_op jit(solution)/shard_map/ppermute | solution.py:802
  126.4 2.8 %collective-permute-start.26 = (bf16[2,112,256]{2,1,0:T(8,128)(2,1)S(1)}, bf16[2,112,256]{2,1,0:T(8,128)(2,1)S(1)}, u32[]{:S(2)}, u32[]{:S(2)}) collective-permute-start(bf16[2,112,256]{2,1,0:T(8,128)(2,1)S(1)} %last_kernel.1.mine_ref), channel_id=1, source_target_pairs={{0,16},{1,17},{2,18},{3,19},{4,20},{5,21},{6,22},{7,23},{8,24},{9,... | collective-permute-start | bytes 344072 | tf_op jit(solution)/shard_map/ppermute | solution.py:802
  129.2 6.1 %collective-permute-done.26.got_ref = bf16[2,112,256]{2,1,0:T(8,128)(2,1)S(1)} collective-permute-done((bf16[2,112,256]{2,1,0:T(8,128)(2,1)S(1)}, bf16[2,112,256]{2,1,0:T(8,128)(2,1)S(1)}, u32[]{:S(2)}, u32[]{:S(2)}) %collective-permute-start.26) | collective-permute-done | bytes 114720 | tf_op jit(solution)/shard_map/ppermute | solution.py:802
  137.8 2.3 %collective-permute-done.28 = f32[8,256]{1,0:T(8,128)S(1)} collective-permute-done((f32[8,256]{1,0:T(8,128)S(1)}, f32[8,256]{1,0:T(8,128)S(1)}, u32[]{:S(2)}, u32[]{:S(2)}) %collective-permute-start.28) | collective-permute-done | bytes 8224 | tf_op jit(solution)/shard_map/ppermute | solution.py:768
  143.5 2.8 %collective-permute-done.30 = f32[8,256]{1,0:T(8,128)S(1)} collective-permute-done((f32[8,256]{1,0:T(8,128)S(1)}, f32[8,256]{1,0:T(8,128)S(1)}, u32[]{:S(2)}, u32[]{:S(2)}) %collective-permute-start.30) | collective-permute-done | bytes 8224 | tf_op jit(solution)/shard_map/ppermute | solution.py:768
  (128 shorter events, 57.4 us)
Async XLA Ops:
  1.8 5.8 %collective-permute-start = (bf16[1,104,256]{2,1,0:T(8,128)(2,1)S(1)}, bf16[1,104,256]{2,1,0:T(8,128)(2,1)S(1)}, u32[]{:S(2)}, u32[]{:S(2)}) collective-permute-start(bf16[1,104,256]{2,1,0:T(8,128)(2,1)S(1)} %cast_kernel.1), channel_id=1, source_target_pairs={{0,17},{1,16},{2,19},{3,18},{4,21},{5,20},{6,23},{7,22},{8,25},{9,... | collective-permute-start | bytes 159752 | tf_op jit(solution)/shard_map/ppermute | solution.py:802
  7.6 4.8 %collective-permute-start.1 = (bf16[2,104,256]{2,1,0:T(8,128)(2,1)S(1)}, bf16[2,104,256]{2,1,0:T(8,128)(2,1)S(1)}, u32[]{:S(2)}, u32[]{:S(2)}) collective-permute-start(bf16[2,104,256]{2,1,0:T(8,128)(2,1)S(1)} %pad_maximum_fusion.2), channel_id=1, source_target_pairs={{0,9},{1,2},{2,1},{3,10},{4,7},{5,12},{6,15},{7,4},{8,11},{9,0},{1... | collective-permute-start | bytes 319496 | tf_op jit(solution)/shard_map/ppermute | solution.py:802
  12.3 5.9 %collective-permute-start.2 = (bf16[4,104,256]{2,1,0:T(8,128)(2,1)S(1)}, bf16[4,104,256]{2,1,0:T(8,128)(2,1)S(1)}, u32[]{:S(2)}, u32[]{:S(2)}) collective-permute-start(bf16[4,104,256]{2,1,0:T(8,128)(2,1)S(1)} %pad_maximum_fusion.1), channel_id=1, source_target_pairs={{0,5},{1,8},{2,11},{3,6},{4,13},{5,0},{6,3},{7,14},{8,1},{9,12},{1... | collective-permute-start | bytes 638984 | tf_op jit(solution)/shard_map/ppermute | solution.py:802
  18.3 4.8 %collective-permute-start.4 = (bf16[8,104,256]{2,1,0:T(8,128)(2,1)S(1)}, bf16[8,104,256]{2,1,0:T(8,128)(2,1)S(1)}, u32[]{:S(2)}, u32[]{:S(2)}) collective-permute-start(bf16[8,104,256]{2,1,0:T(8,128)(2,1)S(1)} %pad_maximum_fusion.near_ref), channel_id=1, source_target_pairs={{0,1},{1,0},{2,3},{3,2},{4,5},{5,4},{6,7},{7,6},{8,9},{9,8},{10,11... | collective-permute-start | bytes 1277960 | tf_op jit(solution)/shard_map/ppermute | solution.py:768
  18.5 7.6 %collective-permute-start.3 = (bf16[8,104,256]{2,1,0:T(8,128)(2,1)S(1)}, bf16[8,104,256]{2,1,0:T(8,128)(2,1)S(1)}, u32[]{:S(2)}, u32[]{:S(2)}) collective-permute-start(bf16[8,104,256]{2,1,0:T(8,128)(2,1)S(1)} %pad_maximum_fusion.near_ref), channel_id=1, source_target_pairs={{0,3},{1,4},{2,7},{3,0},{4,1},{5,6},{6,5},{7,2},{8,13},{9,10},{10,... | collective-permute-start | bytes 1277960 | tf_op jit(solution)/shard_map/ppermute | solution.py:802
  41.0 3.1 %collective-permute-start.7 = (f32[8,256]{1,0:T(8,128)S(1)}, f32[8,256]{1,0:T(8,128)S(1)}, u32[]{:S(2)}, u32[]{:S(2)}) collective-permute-start(f32[8,256]{1,0:T(8,128)S(1)} %add.88), channel_id=1, source_target_pairs={{0,3},{1,2},{2,1},{3,0},{4,7},{5,6},{6,5},{7,4},{8,11},{9,10},{10,... | collective-permute-start | bytes 24584 | tf_op jit(solution)/shard_map/ppermute | solution.py:768
  44.1 3.1 %collective-permute-start.8 = (f32[8,256]{1,0:T(8,128)S(1)}, f32[8,256]{1,0:T(8,128)S(1)}, u32[]{:S(2)}, u32[]{:S(2)}) collective-permute-start(f32[8,256]{1,0:T(8,128)S(1)} %add.89), channel_id=1, source_target_pairs={{0,5},{1,4},{2,7},{3,6},{4,1},{5,0},{6,3},{7,2},{8,13},{9,12},{10,... | collective-permute-start | bytes 24584 | tf_op jit(solution)/shard_map/ppermute | solution.py:768
  47.2 3.1 %collective-permute-start.9 = (f32[8,256]{1,0:T(8,128)S(1)}, f32[8,256]{1,0:T(8,128)S(1)}, u32[]{:S(2)}, u32[]{:S(2)}) collective-permute-start(f32[8,256]{1,0:T(8,128)S(1)} %add.90), channel_id=1, source_target_pairs={{0,9},{1,8},{2,11},{3,10},{4,13},{5,12},{6,15},{7,14},{8,1},{9,0},... | collective-permute-start | bytes 24584 | tf_op jit(solution)/shard_map/ppermute | solution.py:768
  50.3 4.2 %collective-permute-start.10 = (f32[8,256]{1,0:T(8,128)S(1)}, f32[8,256]{1,0:T(8,128)S(1)}, u32[]{:S(2)}, u32[]{:S(2)}) collective-permute-start(f32[8,256]{1,0:T(8,128)S(1)} %add.91), channel_id=1, source_target_pairs={{0,17},{1,16},{2,19},{3,18},{4,21},{5,20},{6,23},{7,22},{8,25},{9,... | collective-permute-start | bytes 24584 | tf_op jit(solution)/shard_map/ppermute | solution.py:768
  59.5 3.1 %collective-permute-start.12 = (f32[8,256]{1,0:T(8,128)S(1)}, f32[8,256]{1,0:T(8,128)S(1)}, u32[]{:S(2)}, u32[]{:S(2)}) collective-permute-start(f32[8,256]{1,0:T(8,128)S(1)} %add.93), channel_id=1, source_target_pairs={{0,3},{1,2},{2,1},{3,0},{4,7},{5,6},{6,5},{7,4},{8,11},{9,10},{10,... | collective-permute-start | bytes 24584 | tf_op jit(solution)/shard_map/ppermute | solution.py:768
  62.6 3.1 %collective-permute-start.13 = (f32[8,256]{1,0:T(8,128)S(1)}, f32[8,256]{1,0:T(8,128)S(1)}, u32[]{:S(2)}, u32[]{:S(2)}) collective-permute-start(f32[8,256]{1,0:T(8,128)S(1)} %add.94), channel_id=1, source_target_pairs={{0,5},{1,4},{2,7},{3,6},{4,1},{5,0},{6,3},{7,2},{8,13},{9,12},{10,... | collective-permute-start | bytes 24584 | tf_op jit(solution)/shard_map/ppermute | solution.py:768
  65.7 3.1 %collective-permute-start.14 = (f32[8,256]{1,0:T(8,128)S(1)}, f32[8,256]{1,0:T(8,128)S(1)}, u32[]{:S(2)}, u32[]{:S(2)}) collective-permute-start(f32[8,256]{1,0:T(8,128)S(1)} %add.95), channel_id=1, source_target_pairs={{0,9},{1,8},{2,11},{3,10},{4,13},{5,12},{6,15},{7,14},{8,1},{9,0},... | collective-permute-start | bytes 24584 | tf_op jit(solution)/shard_map/ppermute | solution.py:768
  68.7 4.0 %collective-permute-start.15 = (f32[8,256]{1,0:T(8,128)S(1)}, f32[8,256]{1,0:T(8,128)S(1)}, u32[]{:S(2)}, u32[]{:S(2)}) collective-permute-start(f32[8,256]{1,0:T(8,128)S(1)} %add.96), channel_id=1, source_target_pairs={{0,17},{1,16},{2,19},{3,18},{4,21},{5,20},{6,23},{7,22},{8,25},{9,... | collective-permute-start | bytes 24584 | tf_op jit(solution)/shard_map/ppermute | solution.py:768
  77.0 3.5 %collective-permute-start.17 = (f32[8,256]{1,0:T(8,128)S(1)}, f32[8,256]{1,0:T(8,128)S(1)}, u32[]{:S(2)}, u32[]{:S(2)}) collective-permute-start(f32[8,256]{1,0:T(8,128)S(1)} %add.98), channel_id=1, source_target_pairs={{0,3},{1,2},{2,1},{3,0},{4,7},{5,6},{6,5},{7,4},{8,11},{9,10},{10,... | collective-permute-start | bytes 24584 | tf_op jit(solution)/shard_map/ppermute | solution.py:768
  80.5 3.1 %collective-permute-start.18 = (f32[8,256]{1,0:T(8,128)S(1)}, f32[8,256]{1,0:T(8,128)S(1)}, u32[]{:S(2)}, u32[]{:S(2)}) collective-permute-start(f32[8,256]{1,0:T(8,128)S(1)} %add.99), channel_id=1, source_target_pairs={{0,5},{1,4},{2,7},{3,6},{4,1},{5,0},{6,3},{7,2},{8,13},{9,12},{10,... | collective-permute-start | bytes 24584 | tf_op jit(solution)/shard_map/ppermute | solution.py:768
  83.7 3.5 %collective-permute-start.19 = (f32[8,256]{1,0:T(8,128)S(1)}, f32[8,256]{1,0:T(8,128)S(1)}, u32[]{:S(2)}, u32[]{:S(2)}) collective-permute-start(f32[8,256]{1,0:T(8,128)S(1)} %add.100), channel_id=1, source_target_pairs={{0,9},{1,8},{2,11},{3,10},{4,13},{5,12},{6,15},{7,14},{8,1},{9,0},... | collective-permute-start | bytes 24584 | tf_op jit(solution)/shard_map/ppermute | solution.py:768
  87.2 4.0 %collective-permute-start.20 = (f32[8,256]{1,0:T(8,128)S(1)}, f32[8,256]{1,0:T(8,128)S(1)}, u32[]{:S(2)}, u32[]{:S(2)}) collective-permute-start(f32[8,256]{1,0:T(8,128)S(1)} %add.101), channel_id=1, source_target_pairs={{0,17},{1,16},{2,19},{3,18},{4,21},{5,20},{6,23},{7,22},{8,25},{9,... | collective-permute-start | bytes 24584 | tf_op jit(solution)/shard_map/ppermute | solution.py:768
  108.4 7.6 %collective-permute-start.22 = (bf16[8,104,256]{2,1,0:T(8,128)(2,1)S(1)}, bf16[8,104,256]{2,1,0:T(8,128)(2,1)S(1)}, u32[]{:S(2)}, u32[]{:S(2)}) collective-permute-start(bf16[8,104,256]{2,1,0:T(8,128)(2,1)S(1)} %add_convert_fusion), channel_id=1, source_target_pairs={{0,3},{1,4},{2,7},{3,0},{4,1},{5,6},{6,5},{7,2},{8,13},{9,10},{10,... | collective-permute-start | bytes 1277960 | tf_op jit(solution)/shard_map/ppermute | solution.py:802
  116.2 5.3 %collective-permute-start.24 = (bf16[4,104,256]{2,1,0:T(8,128)(2,1)S(1)}, bf16[4,104,256]{2,1,0:T(8,128)(2,1)S(1)}, u32[]{:S(2)}, u32[]{:S(2)}) collective-permute-start(bf16[4,104,256]{2,1,0:T(8,128)(2,1)S(1)} %get-tuple-element.163), channel_id=1, source_target_pairs={{0,5},{1,8},{2,11},{3,6},{4,13},{5,0},{6,3},{7,14},{8,1},{9,12},{1... | collective-permute-start | bytes 638984 | tf_op jit(solution)/shard_map/ppermute | solution.py:802
  121.6 4.2 %collective-permute-start.25 = (bf16[2,104,256]{2,1,0:T(8,128)(2,1)S(1)}, bf16[2,104,256]{2,1,0:T(8,128)(2,1)S(1)}, u32[]{:S(2)}, u32[]{:S(2)}) collective-permute-start(bf16[2,104,256]{2,1,0:T(8,128)(2,1)S(1)} %get-tuple-element.164), channel_id=1, source_target_pairs={{0,9},{1,2},{2,1},{3,10},{4,7},{5,12},{6,15},{7,4},{8,11},{9,0},{1... | collective-permute-start | bytes 319496 | tf_op jit(solution)/shard_map/ppermute | solution.py:802
  126.4 8.8 %collective-permute-start.26 = (bf16[2,112,256]{2,1,0:T(8,128)(2,1)S(1)}, bf16[2,112,256]{2,1,0:T(8,128)(2,1)S(1)}, u32[]{:S(2)}, u32[]{:S(2)}) collective-permute-start(bf16[2,112,256]{2,1,0:T(8,128)(2,1)S(1)} %last_kernel.1.mine_ref), channel_id=1, source_target_pairs={{0,16},{1,17},{2,18},{3,19},{4,20},{5,21},{6,22},{7,23},{8,24},{9,... | collective-permute-start | bytes 344072 | tf_op jit(solution)/shard_map/ppermute | solution.py:802
  137.1 3.1 %collective-permute-start.28 = (f32[8,256]{1,0:T(8,128)S(1)}, f32[8,256]{1,0:T(8,128)S(1)}, u32[]{:S(2)}, u32[]{:S(2)}) collective-permute-start(f32[8,256]{1,0:T(8,128)S(1)} %add.109), channel_id=1, source_target_pairs={{0,3},{1,2},{2,1},{3,0},{4,7},{5,6},{6,5},{7,4},{8,11},{9,10},{10,... | collective-permute-start | bytes 24584 | tf_op jit(solution)/shard_map/ppermute | solution.py:768
  140.2 3.1 %collective-permute-start.29 = (f32[8,256]{1,0:T(8,128)S(1)}, f32[8,256]{1,0:T(8,128)S(1)}, u32[]{:S(2)}, u32[]{:S(2)}) collective-permute-start(f32[8,256]{1,0:T(8,128)S(1)} %add.110), channel_id=1, source_target_pairs={{0,5},{1,4},{2,7},{3,6},{4,1},{5,0},{6,3},{7,2},{8,13},{9,12},{10,... | collective-permute-start | bytes 24584 | tf_op jit(solution)/shard_map/ppermute | solution.py:768
  143.2 3.1 %collective-permute-start.30 = (f32[8,256]{1,0:T(8,128)S(1)}, f32[8,256]{1,0:T(8,128)S(1)}, u32[]{:S(2)}, u32[]{:S(2)}) collective-permute-start(f32[8,256]{1,0:T(8,128)S(1)} %add.111), channel_id=1, source_target_pairs={{0,9},{1,8},{2,11},{3,10},{4,13},{5,12},{6,15},{7,14},{8,1},{9,0},... | collective-permute-start | bytes 24584 | tf_op jit(solution)/shard_map/ppermute | solution.py:768
  (25 other events, 186.1 us)
